TPU v7x, 256 devices: a whole 4x4x8 slice. The times are simulated.
256 devices in a mesh: dp: 8 (over x, core), expert: 32 (over y, z).
Axes of the slice: x: 4, y: 4, z: 8, core: 2. Of those that a mesh axis runs over, the one named last changes fastest.
Arguments:
- tokens: bfloat16 [65536, 1280], P(('dp', 'expert')), may hold values from -6 to 6
- norm_gain: float32 [1280], replicated, may hold values from 0.5 to 1.5
- expert_ids: int32 [65536, 1], P(('dp', 'expert')), may hold values from 0 to 31
- priority: int32 [256, 256], P(('dp', 'expert')), may hold values from 0 to 255, each once within a row
- gate_prob: float32 [65536], P(('dp', 'expert')), may hold values from 0.2 to 1
- w_in: bfloat16 [32, 1280, 5120], P('expert', None, 'dp'), may hold values from -0.15625 to 0.15625
- w_out: bfloat16 [32, 5120, 1280], P('expert', 'dp'), may hold values from -0.078125 to 0.078125
- text_emb: float32 [256, 1280], P(('dp', 'expert')), may hold values from -6 to 6
- logit_scale: float32 [1], replicated, may hold values from 10 to 150
Outputs:
- moe_out: bfloat16 [65536, 1280], P(('dp', 'expert'))
- loss: float32 [1], replicated
- grad_image: float32 [256, 1280], P(('dp', 'expert'))
- grad_text: float32 [256, 1280], P(('dp', 'expert'))
Inputs may be any that keep to these rules, and one draw needn't show every extreme that they name: `priority`: each row of a group holds a distinct rank. `expert_ids`: every expert is chosen by some patch.
All inputs are finite; a program needn't handle non-finite values.
Results may differ from a plain program's by a relative error of at most 0.0055.
Values may be sent and summed in bfloat16 or wider, within the bound.
No kernel may reach another device: no remote copies, remote signals or barrier semaphores. Data moves between devices by JAX's collectives and lax.ppermute only.
A program may use at most 128 MiB of HBM per device.

v0:
```python
import jax
import jax.numpy as jnp
from jax import lax
from jax.sharding import PartitionSpec as P

PATCHES = 256


def layer_norm(block, norm_gain):
    values = block.astype(jnp.float32)
    center = values - jnp.mean(values, axis=-1, keepdims=True)
    spread = jnp.mean(center * center, axis=-1, keepdims=True)
    return (center * lax.rsqrt(spread + 1e-06) * norm_gain).astype(jnp.bfloat16)


def slot_table(group_ids, ranks, expert_count, capacity):
    same_expert = group_ids[:, None] == group_ids[None, :]
    earlier = ranks[None, :] < ranks[:, None]
    slots = jnp.sum((same_expert & earlier).astype(jnp.int32), axis=1)
    target = jnp.where(slots < capacity, group_ids * capacity + slots, -1)
    places = lax.broadcasted_iota(jnp.int32, (expert_count * capacity, group_ids.shape[0]), 0)
    return (places == target[None, :]).astype(jnp.bfloat16)


def unit_rows(values):
    radius = jnp.sqrt(jnp.sum(values * values, axis=-1, keepdims=True) + 1e-06)
    return (values / radius, radius)


def back_unit(unit_vals, radius, upstream):
    along = jnp.sum(unit_vals * upstream, axis=-1, keepdims=True)
    return (upstream - unit_vals * along) / radius


def expert_block(inputs, first, second):
    hidden = jax.nn.gelu(
        jnp.einsum("krd,kdf->krf", inputs, first, preferred_element_type=jnp.float32)
    ).astype(jnp.bfloat16)
    return jnp.einsum("krf,kfd->krd", hidden, second, preferred_element_type=jnp.float32)


def on_device(
    tokens, norm_gain, expert_ids, priority, gate_prob, w_in, w_out, text_emb, logit_scale
):
    local_tokens = tokens.shape[0]
    sources = lax.axis_size("expert")
    local_experts = w_in.shape[0]
    expert_count = sources * local_experts
    capacity = local_tokens // (2 * expert_count)
    width = tokens.shape[1]
    normed = layer_norm(tokens, norm_gain)
    table = slot_table(expert_ids[:, 0], priority[0], expert_count, capacity)
    outgoing = jnp.dot(table, normed, preferred_element_type=jnp.float32).astype(jnp.bfloat16)
    outgoing = outgoing.reshape(expert_count, capacity, width)
    incoming = lax.all_to_all(outgoing, "expert", split_axis=0, concat_axis=0, tiled=True)
    expert_inputs = incoming.reshape(sources, local_experts, capacity, width).transpose(1, 0, 2, 3)
    expert_inputs = expert_inputs.reshape(local_experts, sources * capacity, width)
    full_in, full_out = (
        lax.all_gather(w_in, "dp", axis=2, tiled=True),
        lax.all_gather(w_out, "dp", axis=1, tiled=True),
    )
    expert_sum = expert_block(expert_inputs, full_in, full_out)
    expert_result = expert_sum.astype(jnp.bfloat16).reshape(local_experts, sources, capacity, width)
    expert_result = expert_result.transpose(1, 0, 2, 3).reshape(expert_count, capacity, width)
    returned = lax.all_to_all(expert_result, "expert", split_axis=0, concat_axis=0, tiled=True)
    returned = returned.reshape(expert_count * capacity, width)
    expert_part = jnp.dot(table.T, returned, preferred_element_type=jnp.float32)
    moe_out = (tokens.astype(jnp.float32) + gate_prob[:, None] * expert_part).astype(jnp.bfloat16)
    image_count = local_tokens // PATCHES
    pooled = jnp.mean(moe_out.astype(jnp.float32).reshape(image_count, PATCHES, width), axis=1)
    image_unit, image_radius = unit_rows(pooled)
    text_unit, text_radius = unit_rows(text_emb)
    scale_value = logit_scale[0]
    first_row = lax.axis_index(("dp", "expert")) * image_count
    text_all = lax.all_gather(text_unit, ("dp", "expert"), axis=0, tiled=True)
    pair_count = text_all.shape[0]
    logits = scale_value * jnp.dot(image_unit, text_all.T, precision=lax.Precision.HIGHEST)
    row_max = jnp.max(logits, axis=1)
    row_lse = row_max + jnp.log(jnp.sum(jnp.exp(logits - row_max[:, None]), axis=1))
    col_max = lax.pmax(jnp.max(logits, axis=0), ("dp", "expert"))
    col_total = lax.psum(jnp.sum(jnp.exp(logits - col_max[None, :]), axis=0), ("dp", "expert"))
    col_lse = col_max + jnp.log(col_total)
    positions = first_row + lax.broadcasted_iota(jnp.int32, (image_count, pair_count), 0)
    columns_idx = lax.broadcasted_iota(jnp.int32, (image_count, pair_count), 1)
    diag_mask = (positions == columns_idx).astype(jnp.float32)
    diagonal = jnp.sum(logits * diag_mask, axis=1)
    row_total = lax.psum(jnp.sum(row_lse - 2.0 * diagonal), ("dp", "expert"))
    loss = (row_total + jnp.sum(col_lse)) / (2.0 * pair_count)
    grad_logits = (
        jnp.exp(logits - row_lse[:, None]) + jnp.exp(logits - col_lse[None, :]) - 2.0 * diag_mask
    ) / (2.0 * pair_count)
    d_image = scale_value * jnp.dot(grad_logits, text_all, precision=lax.Precision.HIGHEST)
    d_text = lax.psum_scatter(
        scale_value * jnp.dot(grad_logits.T, image_unit, precision=lax.Precision.HIGHEST),
        ("dp", "expert"),
        scatter_dimension=0,
        tiled=True,
    )
    grad_image = back_unit(image_unit, image_radius, d_image)
    grad_text = back_unit(text_unit, text_radius, d_text)
    return (moe_out, loss.reshape(1), grad_image, grad_text)


def solution(mesh):
    in_specs = (
        P(("dp", "expert"), None),
        P(),
        P(("dp", "expert"), None),
        P(("dp", "expert"), None),
        P(("dp", "expert")),
        P("expert", None, "dp"),
        P("expert", "dp", None),
        P(("dp", "expert"), None),
        P(),
    )
    out_specs = (
        P(("dp", "expert"), None),
        P(),
        P(("dp", "expert"), None),
        P(("dp", "expert"), None),
    )
    return jax.shard_map(
        on_device, mesh=mesh, in_specs=in_specs, out_specs=out_specs, check_vma=False
    )
```

profile of v0, /device:TPU:1, one launch (start us, length us, event | category | flops | bytes accessed | tf_op | source)
XLA Modules:
  0.0 689.3 jit_solution(15357509047168901397)
XLA Ops:
  7.2 0.7 all-gather.5.cloned.1.call-update
  8.0 0.7 all-gather.7.cloned.1.call-update
  9.9 0.8 reshape.163
  10.7 12.0 %all-to-all-start = ((bf16[32,4,1280]{2,1,0:T(4,128)(2,1)}), bf16[32,4,1280]{2,1,0:T(4,128)(2,1)S(1)}, u32[]{:S(2)}, u32[]{:S(2)}) async-start(bf16[32,4,1280]{2,1,0:T(4,128)(2,1)} %reshape.163), calls=%async_computation | async-start | bytes 655360 | tf_op jit(solution)/shard_map/all_to_all | solution.py:55
  24.7 8.2 %all-to-all-done = bf16[32,4,1280]{2,1,0:T(4,128)(2,1)S(1)} async-done(((bf16[32,4,1280]{2,1,0:T(4,128)(2,1)}), bf16[32,4,1280]{2,1,0:T(4,128)(2,1)S(1)}, u32[]{:S(2)}, u32[]{:S(2)}) %all-to-all-start) | async-done | bytes 327712 | tf_op jit(solution)/shard_map/all_to_all | solution.py:55
  33.0 53.1 %all-gather.5.cloned.1.call-done = bf16[1,1280,5120]{2,1,0:T(8,128)(2,1)} async-done(((bf16[1,1280,640]{2,1,0:T(8,128)(2,1)}), bf16[1,1280,5120]{2,1,0:T(8,128)(2,1)}) %all-gather.5.cloned.1.call-update) | async-done | bytes 13107216 | tf_op jit(solution)/shard_map/all_gather | solution.py:59
  86.1 74.4 %all-gather.7.cloned.1.call-done = bf16[1,5120,1280]{2,1,0:T(8,128)(2,1)} async-done(((bf16[1,640,1280]{2,1,0:T(8,128)(2,1)}), bf16[1,5120,1280]{2,1,0:T(8,128)(2,1)}) %all-gather.7.cloned.1.call-update) | async-done | bytes 13107216 | tf_op jit(solution)/shard_map/all_gather | solution.py:60
  160.5 12.6 %fusion.18 = bf16[128,1280]{1,0:T(8,128)(2,1)S(1)} fusion(bf16[1,5120,1280]{2,1,0:T(8,128)(2,1)} %all-gather.7.cloned.1.call-done, bf16[128,1280]{1,0:T(8,128)(2,1)S(1)} %reshape.164, bf16[1,1280,5120]{2,1,0:T(8,128)(2,1)} %all-gather.5.cloned.1.call-done), kind=kOutput, calls=%fused_computation.16 | convolution fusion | flops 3361505280 | bytes 26869760 | tf_op jit(solution)/shard_map/krf,kfd->krd/dot_general | solution.py:39
  173.2 0.8 reshape_transpose_reshape.4
  174.0 9.6 %all-to-all-start.1 = ((bf16[32,4,1280]{2,1,0:T(4,128)(2,1)}), bf16[32,4,1280]{2,1,0:T(4,128)(2,1)S(1)}, u32[]{:S(2)}, u32[]{:S(2)}) async-start(bf16[32,4,1280]{2,1,0:T(4,128)(2,1)} %reshape_transpose_reshape.4), calls=%async_computation.1 | async-start | bytes 655360 | tf_op jit(solution)/shard_map/all_to_all | solution.py:65
  184.3 10.0 %all-to-all-done.1 = bf16[32,4,1280]{2,1,0:T(4,128)(2,1)S(1)} async-done(((bf16[32,4,1280]{2,1,0:T(4,128)(2,1)}), bf16[32,4,1280]{2,1,0:T(4,128)(2,1)S(1)}, u32[]{:S(2)}, u32[]{:S(2)}) %all-to-all-start.1) | async-done | bytes 327712 | tf_op jit(solution)/shard_map/all_to_all | solution.py:65
  194.3 1.3 convert_reduce_fusion.1
  196.9 70.6 %all-gather.9.cloned.1.call-done = f32[256,1,1280]{2,1,0:T(1,128)} async-done(((f32[1,1,1280]{2,1,0:T(1,128)}), f32[256,1,1280]{2,1,0:T(1,128)}) %all-gather.9.cloned.1.call-update) | async-done | bytes 1310736 | tf_op jit(solution)/shard_map/all_gather | solution.py:75
  267.5 2.4 fusion.28
  269.9 0.6 fusion.48
  270.6 76.8 %pmax.7 = f32[256]{0:T(256)S(1)} all-reduce(f32[256]{0:T(256)S(1)} %get-tuple-element.9), channel_id=1, replica_groups=mesh['dp'=8,'expert'=32] {'dp','expert'}, use_global_device_ids=true, to_apply=%region_10.11 | all-reduce | flops 256 | bytes 2048 | tf_op jit(solution)/shard_map/pmax | solution.py:80
  347.4 1.3 select_reduce_fusion
  350.7 72.3 %all-reduce.1 = (f32[]{:T(128)}, f32[256]{0:T(256)S(1)}) all-reduce(f32[]{:T(128)S(6)} %sub.53, f32[256]{0:T(256)S(1)} %get-tuple-element.12), channel_id=1, replica_groups=mesh['dp'=8,'expert'=32] {'dp','expert'}, use_global_device_ids=true, to_apply=%region_9.10 | all-reduce | flops 257 | bytes 2056 | tf_op jit(solution)/shard_map/psum | solution.py:87
  423.7 1.3 multiply_multiply_fusion.1
  425.4 0.7 fusion.32
  426.8 0.6 subtract_divide_fusion
  429.3 248.9 %all-reduce.4.cloned.1.call-done = f32[256,1280]{1,0:T(8,128)} async-done(((f32[256,1280]{1,0:T(8,128)}), f32[256,1280]{1,0:T(8,128)}) %all-reduce.4.cloned.1.call-update) | async-done | bytes 1310736
  678.2 1.4 multiply_reduce_fusion.2
  679.6 2.0 subtract_divide_fusion.1
  (37 shorter events, 5.7 us)
Async XLA Ops:
  7.2 1.5 copy-start.3
  7.2 1.5 copy-start.4
  7.2 1.7 copy-start
  7.2 78.9 %all-gather.5.cloned.1.call-start = ((), (), s32[]{:S(2)}) async-start(), calls=%async_computation.2 | async-start | bytes 14745600 | tf_op jit(solution)/shard_map/all_gather | solution.py:59
  7.9 1.5 copy-start.6
  7.9 152.6 %all-gather.7.cloned.1.call-start = ((), (), s32[]{:S(2)}) async-start(), calls=%async_computation.3 | async-start | bytes 14745600 | tf_op jit(solution)/shard_map/all_gather | solution.py:60
  9.5 13.3 %copy-start.2 = (f32[1,1280]{1,0:T(1,128)S(1)}, f32[1,1280]{1,0:T(1,128)}, u32[]{:S(2)}) copy-start(f32[1,1280]{1,0:T(1,128)} %param.16) | copy-start | bytes 15364
  10.7 22.2 %all-to-all-start = ((bf16[32,4,1280]{2,1,0:T(4,128)(2,1)}), bf16[32,4,1280]{2,1,0:T(4,128)(2,1)S(1)}, u32[]{:S(2)}, u32[]{:S(2)}) async-start(bf16[32,4,1280]{2,1,0:T(4,128)(2,1)} %reshape.163), calls=%async_computation | async-start | bytes 655360 | tf_op jit(solution)/shard_map/all_to_all | solution.py:55
  22.8 244.8 %all-gather.9.cloned.1.call-start = ((), (), s32[]{:S(2)}) async-start(), calls=%async_computation.4 | async-start | bytes 1315840 | tf_op jit(solution)/shard_map/all_gather | solution.py:75
  173.2 21.2 %copy-start.5 = (f32[256]{0:T(256)S(1)}, f32[256]{0:T(256)}, u32[]{:S(2)}) copy-start(f32[256]{0:T(256)} %param.13) | copy-start | bytes 3076
  174.0 20.3 %all-to-all-start.1 = ((bf16[32,4,1280]{2,1,0:T(4,128)(2,1)}), bf16[32,4,1280]{2,1,0:T(4,128)(2,1)S(1)}, u32[]{:S(2)}, u32[]{:S(2)}) async-start(bf16[32,4,1280]{2,1,0:T(4,128)(2,1)} %reshape_transpose_reshape.4), calls=%async_computation.1 | async-start | bytes 655360 | tf_op jit(solution)/shard_map/all_to_all | solution.py:65
  183.6 494.6 %all-reduce.4.cloned.1.call-start = ((), (), s32[]{:S(2)}) async-start(), calls=%async_computation.5 | async-start | bytes 2621440
  423.7 1.8 copy-start.1
Sparse Core Ops, SparseCore 0:
  9.9 76.1 all-gather.4
  87.9 72.5 all-gather.6
  164.7 102.8 all-gather.8
  425.1 253.0 all-reduce.3
where the time goes:
time: 691 us; the launch traced here: 689 us
  waiting for transfers between devices  467 us (68%)
  blocking collectives  149 us (22%)
  starting transfers between devices  21.8 us (3%)
  between operations  20.5 us (3%)
  matrix products  17.4 us (3%)
  other arithmetic  11 us (2%)
    unnamed x5, waiting for transfers between devices  250 us
    pmax x1, blocking collectives, on_device(): col_max = lax.pmax(jnp.max(logits, axis=0), ('dp', 'expert'))  76.8 us
    all_gather x1, waiting for transfers between devices, on_device(): lax.all_gather(w_out, 'dp', axis=1, tiled=True)  74.4 us
    psum x1, blocking collectives, on_device(): row_total = lax.psum(jnp.sum(row_lse - 2.0 * diagonal), ('dp', 'expert'))  72.3 us
    all_gather x1, waiting for transfers between devices, on_device(): text_all = lax.all_gather(text_unit, ('dp', 'expert'), axis=0, tiled=True)  70.6 us
    all_gather x1, waiting for transfers between devices, on_device(): lax.all_gather(w_in, 'dp', axis=2, tiled=True)  53.1 us
  transfers between devices with their start and end apart: 6, of which 6 were waited for; matrix products, arithmetic and copies ran while one was open for 3% of the time, Pallas kernels for 0%

commit v1 on v0

v1 whole, which is shorter than its diff:
```python
import jax
import jax.numpy as jnp
from jax import lax
from jax.experimental import pallas as pl
from jax.experimental.pallas import tpu as pltpu
from jax.sharding import PartitionSpec as P

X, CORES, Y, Z = 4, 2, 4, 8
CAP = 4
SLOTS = Y * Z * CAP
PAIRS = X * CORES * Y * Z
VMEM = pl.BlockSpec(memory_space=pltpu.VMEM)
SMEM = pl.BlockSpec(memory_space=pltpu.SMEM)


def narrow(values):
    return values.astype(jnp.bfloat16)


def wide(values):
    return values.astype(jnp.float32)


def iota(shape, dim):
    return lax.broadcasted_iota(jnp.int32, shape, dim)


def as_column(row):
    n = row.shape[1]
    same = iota((n, n), 0) == iota((n, n), 1)
    return jnp.sum(jnp.where(same, row, 0.0), axis=1, keepdims=True)


def table_of(target):
    return narrow(wide(iota((SLOTS, target.shape[1]), 0) == target))


def dispatch_kernel(tokens_ref, gain_ref, ids_ref, ranks_ref, out_ref, target_ref):
    ids = ids_ref[...]
    base = wide(ids * 256)
    key = base + wide(ranks_ref[...])
    others = as_column(key)
    earlier = (others >= base) & (others < key)
    slots = jnp.sum(wide(earlier), axis=0, keepdims=True).astype(jnp.int32)
    target = jnp.where(slots < CAP, ids * CAP + slots, -1)
    target_ref[...] = target
    values = wide(tokens_ref[...])
    center = values - jnp.mean(values, axis=-1, keepdims=True)
    spread = jnp.mean(center * center, axis=-1, keepdims=True)
    normed = narrow(center * lax.rsqrt(spread + 1e-06) * gain_ref[...])
    out_ref[...] = narrow(
        jnp.dot(table_of(target), normed, preferred_element_type=jnp.float32)
    )


def dispatch(tokens, gain, ids, ranks):
    rows, width = tokens.shape
    return pl.pallas_call(
        dispatch_kernel,
        out_shape=(
            jax.ShapeDtypeStruct((SLOTS, width), jnp.bfloat16),
            jax.ShapeDtypeStruct((1, rows), jnp.int32),
        ),
        in_specs=[VMEM] * 4,
        out_specs=(VMEM, VMEM),
        name="dispatch",
    )(tokens, gain, ids, ranks)


def combine_kernel(returned_ref, target_ref, gate_ref, tokens_ref, out_ref, pooled_ref):
    expert_part = lax.dot_general(
        table_of(target_ref[...]),
        returned_ref[...],
        (((0,), (0,)), ((), ())),
        preferred_element_type=jnp.float32,
    )
    moe_out = narrow(wide(tokens_ref[...]) + as_column(gate_ref[...]) * expert_part)
    out_ref[...] = moe_out
    pooled = jnp.mean(wide(moe_out), axis=0, keepdims=True)
    pooled_ref[...] = jnp.broadcast_to(pooled, pooled_ref.shape)


def combine(returned, target, gate, tokens):
    rows, width = tokens.shape
    return pl.pallas_call(
        combine_kernel,
        out_shape=(
            jax.ShapeDtypeStruct((rows, width), jnp.bfloat16),
            jax.ShapeDtypeStruct((Y * Z, width), jnp.float32),
        ),
        in_specs=[VMEM] * 4,
        out_specs=(VMEM, VMEM),
        name="combine",
    )(returned, target, gate, tokens)


def contrast_kernel(
    place_ref,
    scale_ref,
    near_ref,
    other_ref,
    text_near_ref,
    text_other_ref,
    loss_ref,
    image_ref,
    dtext_ref,
    image_scr,
    text_scr,
):
    place_x, core, expert = place_ref[0], place_ref[1], place_ref[2]
    me = (place_x * CORES + core) * (Y * Z) + expert
    scale = scale_ref[0]

    def put(scratch, x, c, rows):
        square = jnp.sum(rows * rows, axis=-1, keepdims=True)
        start = pl.multiple_of((x * CORES + c) * (Y * Z), Y * Z)
        scratch[pl.ds(start, Y * Z), :] = rows / jnp.sqrt(square + 1e-06)

    for step in range(X):
        put(image_scr, step, core, near_ref[step])
        put(image_scr, step, 1 - core, other_ref[step])
        put(text_scr, (place_x - step) & (X - 1), core, text_near_ref[step])
        put(text_scr, (place_x - step) & (X - 1), 1 - core, text_other_ref[step])
    image_unit = image_scr[...]
    text_unit = text_scr[...]
    logits = scale * lax.dot_general(
        image_unit,
        text_unit,
        (((1,), (1,)), ((), ())),
        precision=lax.Precision.HIGHEST,
        preferred_element_type=jnp.float32,
    )
    row_max = jnp.max(logits, axis=1, keepdims=True)
    col_max = jnp.max(logits, axis=0, keepdims=True)
    row_lse = row_max + jnp.log(jnp.sum(jnp.exp(logits - row_max), axis=1, keepdims=True))
    col_lse = col_max + jnp.log(jnp.sum(jnp.exp(logits - col_max), axis=0, keepdims=True))
    rows_at, cols_at = iota(logits.shape, 0), iota(logits.shape, 1)
    same = rows_at == cols_at
    trace = jnp.sum(jnp.where(same, logits, 0.0), axis=(0, 1), keepdims=True)
    total = jnp.sum(row_lse, axis=0, keepdims=True) + jnp.sum(col_lse, axis=1, keepdims=True)
    loss_ref[...] = (total - 2.0 * trace) / (2.0 * PAIRS)
    grad = jnp.exp(logits - row_lse) + jnp.exp(logits - col_lse) - 2.0 * wide(same)
    grad = grad / (2.0 * PAIRS)
    own_col = jnp.sum(jnp.where(cols_at == me, grad, 0.0), axis=1, keepdims=True)
    own_row = as_column(jnp.sum(jnp.where(rows_at == me, grad, 0.0), axis=0, keepdims=True))
    d_image = scale * jnp.sum(own_row * text_unit, axis=0, keepdims=True)
    d_text = scale * jnp.sum(own_col * image_unit, axis=0, keepdims=True)

    def back(unit, radius, upstream):
        along = jnp.sum(unit * upstream, axis=-1, keepdims=True)
        return (upstream - unit * along) / radius

    def own(rows):
        radius = jnp.sqrt(jnp.sum(rows * rows, axis=-1, keepdims=True) + 1e-06)
        return rows / radius, radius

    image_ref[...] = back(*own(near_ref[place_x, pl.ds(expert, 1), :]), d_image)
    dtext_ref[...] = back(*own(text_near_ref[0, pl.ds(expert, 1), :]), d_text)


def contrast(places, scale, near, other, text_near, text_other):
    width = near.shape[-1]
    row = jax.ShapeDtypeStruct((1, width), jnp.float32)
    return pl.pallas_call(
        contrast_kernel,
        out_shape=(jax.ShapeDtypeStruct((1, 1), jnp.float32), row, row),
        in_specs=[SMEM, SMEM, VMEM, VMEM, VMEM, VMEM],
        out_specs=(VMEM, VMEM, VMEM),
        scratch_shapes=[pltpu.VMEM((PAIRS, width), jnp.float32)] * 2,
        compiler_params=pltpu.CompilerParams(vmem_limit_bytes=32 * 2**20),
        name="contrast",
    )(places, scale, near, other, text_near, text_other)


HIDDEN_STEP = 128


def expert_kernel(rows_ref, in_own, in_other, out_own, out_other, out_ref):
    first = jnp.concatenate([in_own[...], in_other[...]], axis=1)
    second = jnp.concatenate([out_own[...], out_other[...]], axis=0)
    hidden = jax.nn.gelu(jnp.dot(rows_ref[...], first, preferred_element_type=jnp.float32))
    part = jnp.dot(narrow(hidden), second, preferred_element_type=jnp.float32)

    @pl.when(pl.program_id(0) == 0)
    def _():
        out_ref[...] = part

    @pl.when(pl.program_id(0) > 0)
    def _():
        out_ref[...] += part


def expert_rows(rows, in_own, in_other, out_own, out_other):
    count, width = rows.shape
    hidden = in_own.shape[1]
    whole = pl.BlockSpec((count, width), lambda i: (0, 0))
    first = pl.BlockSpec((width, HIDDEN_STEP), lambda i: (0, i))
    second = pl.BlockSpec((HIDDEN_STEP, width), lambda i: (i, 0))
    return pl.pallas_call(
        expert_kernel,
        grid=(hidden // HIDDEN_STEP,),
        out_shape=jax.ShapeDtypeStruct((count, width), jnp.float32),
        in_specs=[whole, first, first, second, second],
        out_specs=whole,
        compiler_params=pltpu.CompilerParams(vmem_limit_bytes=32 * 2**20),
        cost_estimate=pl.CostEstimate(
            flops=8 * count * width * hidden,
            bytes_accessed=8 * width * hidden + 6 * count * width,
            transcendentals=2 * count * hidden,
        ),
        name="expert",
    )(rows, in_own, in_other, out_own, out_other)


def along_x(step):
    return "dp", [(x * 2 + c, (x + step) % X * 2 + c) for x in range(X) for c in range(CORES)]


def along_core():
    return "dp", [(i, i ^ 1) for i in range(X * CORES)]


def groups_x():
    return [[x * CORES + c for x in range(X)] for c in range(CORES)]


def to_experts(blocks):
    return lax.all_to_all(blocks, "expert", split_axis=0, concat_axis=0, tiled=True)


def on_device(
    tokens, norm_gain, expert_ids, priority, gate_prob, w_in, w_out, text_emb, logit_scale
):
    rows, width = tokens.shape
    half = SLOTS // 2
    dp_place = lax.axis_index("dp")
    places = jnp.stack([dp_place // CORES, dp_place % CORES, lax.axis_index("expert")])

    text_block = to_experts(jnp.broadcast_to(text_emb, (Y * Z, width)))
    weights = (
        w_in[0],
        lax.ppermute(w_in[0], *along_core()),
        w_out[0],
        lax.ppermute(w_out[0], *along_core()),
    )

    outgoing, target = dispatch(
        tokens, norm_gain.reshape(1, width), expert_ids.reshape(1, rows), priority
    )
    text_block, outgoing = lax.optimization_barrier((text_block, outgoing))
    text_x = [text_block] + [lax.ppermute(text_block, *along_x(d)) for d in range(1, X)]
    own_rows = to_experts(outgoing.reshape(Y * Z, CAP, width)).reshape(SLOTS, width)

    text_x, own_rows = lax.optimization_barrier((text_x, own_rows))

    left_rows = lax.ppermute(own_rows, *along_x(1))
    right_rows = lax.ppermute(own_rows, *along_x(-1))
    own_part = expert_rows(own_rows, *weights)
    left_rows, right_rows, own_part = lax.optimization_barrier((left_rows, right_rows, own_part))
    far_rows = jnp.concatenate(
        [
            lax.ppermute(left_rows[:half], *along_x(1)),
            lax.ppermute(right_rows[half:], *along_x(-1)),
        ]
    )
    side_part = expert_rows(jnp.concatenate([left_rows, right_rows]), *weights)
    far_rows, side_part = lax.optimization_barrier((far_rows, side_part))
    far_part = narrow(expert_rows(far_rows, *weights))

    from_right = lax.ppermute(far_part[:half], *along_x(-1))
    from_left = lax.ppermute(far_part[half:], *along_x(1))
    left_sum = jnp.concatenate([side_part[:half] + wide(from_right), side_part[half:SLOTS]])
    right_sum = jnp.concatenate(
        [side_part[SLOTS : SLOTS + half], side_part[SLOTS + half :] + wide(from_left)]
    )
    left_sum = lax.ppermute(narrow(left_sum), *along_x(-1))
    right_sum = lax.ppermute(narrow(right_sum), *along_x(1))
    result = narrow(own_part + wide(left_sum) + wide(right_sum))

    text_near, result = lax.optimization_barrier((jnp.stack(text_x), result))
    text_other = lax.ppermute(text_near, *along_core())
    returned = to_experts(result.reshape(Y * Z, CAP, width)).reshape(SLOTS, width)
    moe_out, pooled = combine(returned, target, gate_prob.reshape(1, rows), tokens)

    near = to_experts(pooled)
    near = lax.all_to_all(
        jnp.broadcast_to(near, (X,) + near.shape),
        "dp",
        split_axis=0,
        concat_axis=0,
        tiled=True,
        axis_index_groups=groups_x(),
    )
    other = lax.ppermute(near, *along_core())
    loss, grad_image, grad_text = contrast(
        places, logit_scale, near, other, text_near, text_other
    )
    return (moe_out, loss.reshape(1), grad_image, grad_text)


def solution(mesh):
    in_specs = (
        P(("dp", "expert"), None),
        P(),
        P(("dp", "expert"), None),
        P(("dp", "expert"), None),
        P(("dp", "expert")),
        P("expert", None, "dp"),
        P("expert", "dp", None),
        P(("dp", "expert"), None),
        P(),
    )
    out_specs = (
        P(("dp", "expert"), None),
        P(),
        P(("dp", "expert"), None),
        P(("dp", "expert"), None),
    )
    return jax.shard_map(
        on_device, mesh=mesh, in_specs=in_specs, out_specs=out_specs, check_vma=False
    )
```

time: 691 us -> 150 us (0.22)
  waiting for transfers between devices: 467 us -> 21.5 us
  blocking collectives: 149 us -> 30.1 us
  starting transfers between devices: 21.8 us -> 57.2 us
  Pallas kernels: 0 us -> 25.9 us
  between operations: 20.5 us -> 1.52 us
  matrix products: 17.4 us -> 0 us
  other arithmetic: 11 us -> 2.27 us
  local copies, waits for them, and re-layouts: 2.91 us -> 10.4 us
    unnamed x5 -> x0, waiting for transfers between devices: 250 us -> none
    all_gather x3 -> x0, waiting for transfers between devices: 198 us -> none  [the longest x1 74.4 us: on_device(): lax.all_gather(w_out, 'dp', axis=1, tiled=True)]
    pmax x1 -> x0, blocking collectives: 76.8 us -> none  [on_device(): col_max = lax.pmax(jnp.max(logits, axis=0), ('dp', 'expert'))]
    psum x1 -> x0, blocking collectives: 72.3 us -> none  [on_device(): row_total = lax.psum(jnp.sum(row_lse - 2.0 * diagonal), ('dp', 'expert'))]
    ppermute x0 -> x15, starting transfers between devices: none -> 39 us  [the longest x1 12 us: on_device(): text_other = lax.ppermute(text_near, *along_core())]
    all_to_all x0 -> x2, blocking collectives: none -> 30.1 us  [to_experts(): lax.all_to_all(blocks, 'expert', split_axis=0, concat_axis=0, tiled=True)]
    pallas_call x0 -> x6, Pallas kernels: none -> 25.9 us  [the longest x3 17.3 us: expert_rows(): pl.pallas_call(expert_kernel, grid=(hidden // HIDDEN_STEP,), out_shape=ja...]
    dot_general x5 -> x0, matrix products: 17.4 us -> none  [the longest x1 12.6 us: expert_block(): jnp.einsum('krf,kfd->krd', hidden, second, preferred_element_type=jnp.flo...]
  transfers between devices with their start and end apart: 6 -> 18, of which waited for: 6 -> 6; matrix products, arithmetic and copies ran while one was open for 3% -> 6% of each run, Pallas kernels for 0% -> 10%
where the time goes in v1:
time: 150 us; the launch traced here: 149 us
  starting transfers between devices  57.2 us (38%)
  blocking collectives  30.1 us (20%)
  Pallas kernels  25.9 us (17%)
  waiting for transfers between devices  21.5 us (14%)
  local copies, waits for them, and re-layouts  10.4 us (7%)
  other arithmetic  2.27 us (2%)
  between operations  1.52 us (1%)
    all_to_all x2, blocking collectives, to_experts(): lax.all_to_all(blocks, 'expert', split_axis=0, concat_axis=0, tiled=True)  30.1 us
    pallas_call x3, Pallas kernels, expert_rows(): pl.pallas_call(expert_kernel, grid=(hidden // HIDDEN_STEP,), out_shape=ja...  17.3 us
    all_to_all x2, starting transfers between devices, to_experts(): lax.all_to_all(blocks, 'expert', split_axis=0, concat_axis=0, tiled=True)  14.7 us
    ppermute x1, starting transfers between devices, on_device(): text_other = lax.ppermute(text_near, *along_core())  12 us
    all_to_all x2, waiting for transfers between devices, to_experts(): lax.all_to_all(blocks, 'expert', split_axis=0, concat_axis=0, tiled=True)  10.5 us
    ppermute x1, starting transfers between devices, on_device(): other = lax.ppermute(near, *along_core())  8.78 us
    ppermute x3, starting transfers between devices, on_device(): lax.ppermute(text_block, *along_x(d))  4.89 us
    ppermute x1, waiting for transfers between devices, on_device(): right_sum = lax.ppermute(narrow(right_sum), *along_x(1))  4.71 us
  transfers between devices with their start and end apart: 18, of which 6 were waited for; matrix products, arithmetic and copies ran while one was open for 6% of the time, Pallas kernels for 10%

profile of v1, /device:TPU:1, one launch (start us, length us, event | category | flops | bytes accessed | tf_op | source)
XLA Modules:
  0.0 149.0 jit_solution(17558319009581946715)
XLA Ops:
  0.6 3.3 %collective-permute-start.5 = (bf16[1280,640]{1,0:T(8,128)(2,1)}, bf16[1280,640]{1,0:T(8,128)(2,1)}, u32[]{:S(2)}, u32[]{:S(2)}) collective-permute-start(bf16[1280,640]{1,0:T(8,128)(2,1)} %bitcast.19), channel_id=1, source_target_pairs={{0,32},{32,0},{64,96},{96,64},{128,160},{160,128},{192,224},{224,1... | collective-permute-start | bytes 4915208 | tf_op jit(solution)/shard_map/ppermute | solution.py:242
  5.5 9.7 %all-to-all-start = ((f32[32,1,1280]{2,1,0:T(1,128)}), f32[32,1,1280]{2,1,0:T(1,128)}, u32[]{:S(2)}, u32[]{:S(2)}) async-start(f32[32,1,1280]{2,1,0:T(1,128)} %broadcast_in_dim.8), calls=%async_computation | async-start | bytes 327680 | tf_op jit(solution)/shard_map/all_to_all | solution.py:228
  16.5 2.5 %dispatch.1 = (bf16[128,1280]{1,0:T(8,128)(2,1)}, s32[1,256]{1,0:T(1,128)}) custom-call(bf16[256,1280]{1,0:T(8,128)(2,1)} %tokens_ref.3, f32[1,1280]{1,0:T(1,128)} %reshape.40.gain_ref, s32[1,256]{1,0:T(1,128)} %bitcast.33, s32[1,256]{1,0:T(1,128)} %ranks_ref.1), custom_call_target="tpu_custom_call" | custom-call | tf_op jit(solution)/shard_map/dispatch/pallas_call | solution.py:58
  19.0 5.5 %all-to-all-done = f32[32,1,1280]{2,1,0:T(1,128)} async-done(((f32[32,1,1280]{2,1,0:T(1,128)}), f32[32,1,1280]{2,1,0:T(1,128)}, u32[]{:S(2)}, u32[]{:S(2)}) %all-to-all-start) | async-done | bytes 163872 | tf_op jit(solution)/shard_map/all_to_all | solution.py:228
  25.4 1.8 %reshape.42 = bf16[32,4,1280]{2,1,0:T(4,128)(2,1)} reshape(bf16[128,1280]{1,0:T(8,128)(2,1)} %get-tuple-element.27) | data formatting | bytes 655360 | tf_op jit(solution)/shard_map/reshape | solution.py:252
  27.2 5.0 %all-to-all-start.1 = ((bf16[32,4,1280]{2,1,0:T(4,128)(2,1)}), bf16[32,4,1280]{2,1,0:T(4,128)(2,1)}, u32[]{:S(2)}, u32[]{:S(2)}) async-start(bf16[32,4,1280]{2,1,0:T(4,128)(2,1)} %reshape.42), calls=%async_computation.1 | async-start | bytes 655360 | tf_op jit(solution)/shard_map/all_to_all | solution.py:228
  33.5 2.5 %collective-permute-start.1 = (f32[32,1280]{1,0:T(8,128)S(1)}, f32[32,1280]{1,0:T(8,128)}, u32[]{:S(2)}, u32[]{:S(2)}) collective-permute-start(f32[32,1280]{1,0:T(8,128)S(1)} %bitcast.28), channel_id=1, source_target_pairs={{0,128},{32,160},{64,192},{96,224},{128,0},{160,32},{192,64},{224,... | collective-permute-start | bytes 491528 | tf_op jit(solution)/shard_map/ppermute | solution.py:251
  37.1 5.0 %all-to-all-done.1 = bf16[32,4,1280]{2,1,0:T(4,128)(2,1)} async-done(((bf16[32,4,1280]{2,1,0:T(4,128)(2,1)}), bf16[32,4,1280]{2,1,0:T(4,128)(2,1)}, u32[]{:S(2)}, u32[]{:S(2)}) %all-to-all-start.1) | async-done | bytes 327712 | tf_op jit(solution)/shard_map/all_to_all | solution.py:228
  42.2 1.8 %reshape.43.rows_ref = bf16[128,1280]{1,0:T(8,128)(2,1)} reshape(bf16[32,4,1280]{2,1,0:T(4,128)(2,1)} %all-to-all-done.1) | data formatting | bytes 655360 | tf_op jit(solution)/shard_map/reshape | solution.py:252
  47.7 5.4 %expert.3 = f32[128,1280]{1,0:T(8,128)S(1)} custom-call(bf16[128,1280]{1,0:T(8,128)(2,1)S(1)} %copy-done.2, bf16[1280,640]{1,0:T(8,128)(2,1)S(1)} %bitcast.20, bf16[1280,640]{1,0:T(8,128)(2,1)} %collective-permute-done.5.in_other, bf16[640,1280]{1,0:T(8,128)(2,1)S(1)} %bitcast.24, bf16[640,1280]{1,0:T(8,128)(2,1)} %collective-permute-done.6.out_other), custom_call_target="tpu_custom_call" | custom-call | flops 838860800 | bytes 7536640 | tf_op jit(solution)/shard_map/expert/pallas_call | solution.py:199
  54.8 6.5 %expert.4 = f32[256,1280]{1,0:T(8,128)S(1)} custom-call(bf16[256,1280]{1,0:T(8,128)(2,1)S(1)} %pad_maximum_fusion.1.rows_ref, bf16[1280,640]{1,0:T(8,128)(2,1)S(1)} %bitcast.21, bf16[1280,640]{1,0:T(8,128)(2,1)} %collective-permute-done.5.in_other, bf16[640,1280]{1,0:T(8,128)(2,1)S(1)} %bitcast.25, bf16[640,1280]{1,0:T(8,128)(2,1)} %collective-permute-done.6.out_other), custom_call_target="tpu_custom_call" | custom-call | flops 1677721600 | bytes 8519680 | tf_op jit(solution)/shard_map/expert/pallas_call | solution.py:199
  61.4 5.4 %expert.5 = f32[128,1280]{1,0:T(8,128)S(1)} custom-call(bf16[128,1280]{1,0:T(8,128)(2,1)S(1)} %pad_maximum_fusion.2.rows_ref, bf16[1280,640]{1,0:T(8,128)(2,1)S(1)} %bitcast.22, bf16[1280,640]{1,0:T(8,128)(2,1)} %collective-permute-done.5.in_other, bf16[640,1280]{1,0:T(8,128)(2,1)S(1)} %bitcast.26, bf16[640,1280]{1,0:T(8,128)(2,1)} %collective-permute-done.6.out_other), custom_call_target="tpu_custom_call" | custom-call | flops 838860800 | bytes 7536640 | tf_op jit(solution)/shard_map/expert/pallas_call | solution.py:199
  66.9 2.6 %collective-permute-start.9 = (bf16[64,1280]{1,0:T(8,128)(2,1)S(1)}, bf16[64,1280]{1,0:T(8,128)(2,1)S(1)}, u32[]{:S(2)}, u32[]{:S(2)}) collective-permute-start(bf16[64,1280]{1,0:T(8,128)(2,1)S(1)} %get-tuple-element.50), channel_id=1, source_target_pairs={{0,192},{32,224},{64,0},{96,32},{128,64},{160,96},{192,128},{224,1... | collective-permute-start | bytes 491528 | tf_op jit(solution)/shard_map/ppermute | solution.py:270
  69.5 2.2 %collective-permute-done.9 = bf16[64,1280]{1,0:T(8,128)(2,1)S(1)} collective-permute-done((bf16[64,1280]{1,0:T(8,128)(2,1)S(1)}, bf16[64,1280]{1,0:T(8,128)(2,1)S(1)}, u32[]{:S(2)}, u32[]{:S(2)}) %collective-permute-start.9) | collective-permute-done | bytes 163872 | tf_op jit(solution)/shard_map/ppermute | solution.py:270
  71.7 3.1 %collective-permute-done.11 = bf16[64,1280]{1,0:T(8,128)(2,1)S(1)} collective-permute-done((bf16[64,1280]{1,0:T(8,128)(2,1)S(1)}, bf16[64,1280]{1,0:T(8,128)(2,1)S(1)}, u32[]{:S(2)}, u32[]{:S(2)}) %collective-permute-start.11) | collective-permute-done | bytes 163872 | tf_op jit(solution)/shard_map/ppermute | solution.py:271
  75.2 2.7 %collective-permute-start.10 = (bf16[128,1280]{1,0:T(8,128)(2,1)S(1)}, bf16[128,1280]{1,0:T(8,128)(2,1)S(1)}, u32[]{:S(2)}, u32[]{:S(2)}) collective-permute-start(bf16[128,1280]{1,0:T(8,128)(2,1)S(1)} %pad_maximum_fusion.3), channel_id=1, source_target_pairs={{0,192},{32,224},{64,0},{96,32},{128,64},{160,96},{192,128},{224,1... | collective-permute-start | bytes 983048 | tf_op jit(solution)/shard_map/ppermute | solution.py:276
  79.1 4.7 %collective-permute-done.12 = bf16[128,1280]{1,0:T(8,128)(2,1)S(1)} collective-permute-done((bf16[128,1280]{1,0:T(8,128)(2,1)S(1)}, bf16[128,1280]{1,0:T(8,128)(2,1)S(1)}, u32[]{:S(2)}, u32[]{:S(2)}) %collective-permute-start.12) | collective-permute-done | bytes 327712 | tf_op jit(solution)/shard_map/ppermute | solution.py:277
  84.0 16.2 %all_to_all.36 = bf16[32,4,1280]{2,1,0:T(4,128)(2,1)S(1)} all-to-all(bf16[32,4,1280]{2,1,0:T(4,128)(2,1)S(1)} %reshape.44), channel_id=1, replica_groups=mesh['dp'=8,'expert'=32] {'expert'}, dimensions={0} | all-to-all | bytes 655360 | tf_op jit(solution)/shard_map/all_to_all | solution.py:228
  101.0 2.6 %combine.1 = (bf16[256,1280]{1,0:T(8,128)(2,1)}, f32[32,1280]{1,0:T(8,128)}) custom-call(bf16[128,1280]{1,0:T(8,128)(2,1)} %reshape.45.returned_ref, s32[1,256]{1,0:T(1,128)} %get-tuple-element.39.target_ref, f32[1,256]{1,0:T(1,128)} %bitcast.34, bf16[256,1280]{1,0:T(8,128)(2,1)} %tokens_ref.3), custom_call_target="tpu_custom_call" | custom-call | tf_op jit(solution)/shard_map/combine/pallas_call | solution.py:85
  104.7 13.9 %all_to_all.37 = f32[32,1,1280]{2,1,0:T(1,128)S(1)} all-to-all(f32[32,1,1280]{2,1,0:T(1,128)S(1)} %copy.13), channel_id=1, replica_groups=mesh['dp'=8,'expert'=32] {'expert'}, dimensions={0} | all-to-all | bytes 327680 | tf_op jit(solution)/shard_map/all_to_all | solution.py:228
  119.4 3.5 %all-to-all-start.4 = ((f32[4,32,1280]{2,1,0:T(8,128)}), f32[4,32,1280]{2,1,0:T(8,128)S(1)}, u32[]{:S(2)}, u32[]{:S(2)}) async-start(f32[4,32,1280]{2,1,0:T(8,128)} %broadcast_in_dim.9), calls=%async_computation.4 | async-start | bytes 1310720 | tf_op jit(solution)/shard_map/all_to_all | solution.py:286
  122.9 12.0 %collective-permute-start.14 = (f32[4,32,1280]{2,1,0:T(8,128)S(1)}, f32[4,32,1280]{2,1,0:T(8,128)S(1)}, u32[]{:S(2)}, u32[]{:S(2)}) collective-permute-start(f32[4,32,1280]{2,1,0:T(8,128)S(1)} %pad_maximum_fusion.text_near_ref), channel_id=1, source_target_pairs={{0,32},{32,0},{64,96},{96,64},{128,160},{160,128},{192,224},{224,1... | collective-permute-start | bytes 1966088 | tf_op jit(solution)/shard_map/ppermute | solution.py:281
  134.9 8.8 %collective-permute-start.13 = (f32[4,32,1280]{2,1,0:T(8,128)S(1)}, f32[4,32,1280]{2,1,0:T(8,128)S(1)}, u32[]{:S(2)}, u32[]{:S(2)}) collective-permute-start(f32[4,32,1280]{2,1,0:T(8,128)S(1)} %all-to-all-done.4.near_ref), channel_id=1, source_target_pairs={{0,32},{32,0},{64,96},{96,64},{128,160},{160,128},{192,224},{224,1... | collective-permute-start | bytes 1966088 | tf_op jit(solution)/shard_map/ppermute | solution.py:294
  145.4 3.6 %contrast.1 = (f32[1,1]{1,0:T(1,128)}, f32[1,1280]{1,0:T(1,128)}, f32[1,1280]{1,0:T(1,128)}) custom-call(s32[3]{0:T(128)S(1)} %pad_add_fusion.place_ref, f32[1]{0:T(128)S(6)} %copy.20.scale_ref, f32[4,32,1280]{2,1,0:T(8,128)S(1)} %all-to-all-done.4.near_ref, f32[4,32,1280]{2,1,0:T(8,128)S(1)} %collective-permute-done.13.other_ref, ...), custom_call_target="tpu_custom_call" | custom-call | tf_op jit(solution)/shard_map/contrast/pallas_call | solution.py:164
  (51 shorter events, 17.4 us)
Async XLA Ops:
  0.6 46.1 %collective-permute-start.5 = (bf16[1280,640]{1,0:T(8,128)(2,1)}, bf16[1280,640]{1,0:T(8,128)(2,1)}, u32[]{:S(2)}, u32[]{:S(2)}) collective-permute-start(bf16[1280,640]{1,0:T(8,128)(2,1)} %bitcast.19), channel_id=1, source_target_pairs={{0,32},{32,0},{64,96},{96,64},{128,160},{160,128},{192,224},{224,1... | collective-permute-start | bytes 4915208 | tf_op jit(solution)/shard_map/ppermute | solution.py:242
  4.0 42.8 %collective-permute-start.6 = (bf16[640,1280]{1,0:T(8,128)(2,1)}, bf16[640,1280]{1,0:T(8,128)(2,1)}, u32[]{:S(2)}, u32[]{:S(2)}) collective-permute-start(bf16[640,1280]{1,0:T(8,128)(2,1)} %bitcast.23), channel_id=1, source_target_pairs={{0,32},{32,0},{64,96},{96,64},{128,160},{160,128},{192,224},{224,1... | collective-permute-start | bytes 4915208 | tf_op jit(solution)/shard_map/ppermute | solution.py:244
  5.5 41.2 %copy-start.1 = (bf16[1,640,1280]{2,1,0:T(8,128)(2,1)S(1)}, bf16[1,640,1280]{2,1,0:T(8,128)(2,1)}, u32[]{:S(2)}) copy-start(bf16[1,640,1280]{2,1,0:T(8,128)(2,1)} %param.15) | copy-start | bytes 4915204
  5.5 19.0 %all-to-all-start = ((f32[32,1,1280]{2,1,0:T(1,128)}), f32[32,1,1280]{2,1,0:T(1,128)}, u32[]{:S(2)}, u32[]{:S(2)}) async-start(f32[32,1,1280]{2,1,0:T(1,128)} %broadcast_in_dim.8), calls=%async_computation | async-start | bytes 327680 | tf_op jit(solution)/shard_map/all_to_all | solution.py:228
  19.0 27.7 %copy-start = (bf16[1,1280,640]{2,1,0:T(8,128)(2,1)S(1)}, bf16[1,1280,640]{2,1,0:T(8,128)(2,1)}, u32[]{:S(2)}) copy-start(bf16[1,1280,640]{2,1,0:T(8,128)(2,1)} %param.14) | copy-start | bytes 4915204
  27.2 15.0 %all-to-all-start.1 = ((bf16[32,4,1280]{2,1,0:T(4,128)(2,1)}), bf16[32,4,1280]{2,1,0:T(4,128)(2,1)}, u32[]{:S(2)}, u32[]{:S(2)}) async-start(bf16[32,4,1280]{2,1,0:T(4,128)(2,1)} %reshape.42), calls=%async_computation.1 | async-start | bytes 655360 | tf_op jit(solution)/shard_map/all_to_all | solution.py:228
  32.2 11.7 %collective-permute-start = (f32[32,1280]{1,0:T(8,128)S(1)}, f32[32,1280]{1,0:T(8,128)}, u32[]{:S(2)}, u32[]{:S(2)}) collective-permute-start(f32[32,1280]{1,0:T(8,128)S(1)} %bitcast.27), channel_id=1, source_target_pairs={{0,64},{32,96},{64,128},{96,160},{128,192},{160,224},{192,0},{224,... | collective-permute-start | bytes 491528 | tf_op jit(solution)/shard_map/ppermute | solution.py:251
  33.5 10.4 %collective-permute-start.1 = (f32[32,1280]{1,0:T(8,128)S(1)}, f32[32,1280]{1,0:T(8,128)}, u32[]{:S(2)}, u32[]{:S(2)}) collective-permute-start(f32[32,1280]{1,0:T(8,128)S(1)} %bitcast.28), channel_id=1, source_target_pairs={{0,128},{32,160},{64,192},{96,224},{128,0},{160,32},{192,64},{224,... | collective-permute-start | bytes 491528 | tf_op jit(solution)/shard_map/ppermute | solution.py:251
  36.0 8.0 %collective-permute-start.2 = (f32[32,1280]{1,0:T(8,128)S(1)}, f32[32,1280]{1,0:T(8,128)}, u32[]{:S(2)}, u32[]{:S(2)}) collective-permute-start(f32[32,1280]{1,0:T(8,128)S(1)} %bitcast.29), channel_id=1, source_target_pairs={{0,192},{32,224},{64,0},{96,32},{128,64},{160,96},{192,128},{224,1... | collective-permute-start | bytes 491528 | tf_op jit(solution)/shard_map/ppermute | solution.py:251
  44.0 9.1 %collective-permute-start.3 = (bf16[128,1280]{1,0:T(8,128)(2,1)}, bf16[128,1280]{1,0:T(8,128)(2,1)S(1)}, u32[]{:S(2)}, u32[]{:S(2)}) collective-permute-start(bf16[128,1280]{1,0:T(8,128)(2,1)} %reshape.43.rows_ref), channel_id=1, source_target_pairs={{0,64},{32,96},{64,128},{96,160},{128,192},{160,224},{192,0},{224,... | collective-permute-start | bytes 983048 | tf_op jit(solution)/shard_map/ppermute | solution.py:256
  45.3 7.9 %collective-permute-start.4 = (bf16[128,1280]{1,0:T(8,128)(2,1)}, bf16[128,1280]{1,0:T(8,128)(2,1)S(1)}, u32[]{:S(2)}, u32[]{:S(2)}) collective-permute-start(bf16[128,1280]{1,0:T(8,128)(2,1)} %reshape.43.rows_ref), channel_id=1, source_target_pairs={{0,192},{32,224},{64,0},{96,32},{128,64},{160,96},{192,128},{224,1... | collective-permute-start | bytes 983048 | tf_op jit(solution)/shard_map/ppermute | solution.py:257
  46.8 1.0 copy-start.2
  53.2 8.2 %collective-permute-start.8 = (bf16[64,1280]{1,0:T(8,128)(2,1)S(1)}, bf16[64,1280]{1,0:T(8,128)(2,1)S(1)}, u32[]{:S(2)}, u32[]{:S(2)}) collective-permute-start(bf16[64,1280]{1,0:T(8,128)(2,1)S(1)} %slice.27), channel_id=1, source_target_pairs={{0,192},{32,224},{64,0},{96,32},{128,64},{160,96},{192,128},{224,1... | collective-permute-start | bytes 491528 | tf_op jit(solution)/shard_map/ppermute | solution.py:263
  54.5 6.8 %collective-permute-start.7 = (bf16[64,1280]{1,0:T(8,128)(2,1)S(1)}, bf16[64,1280]{1,0:T(8,128)(2,1)S(1)}, u32[]{:S(2)}, u32[]{:S(2)}) collective-permute-start(bf16[64,1280]{1,0:T(8,128)(2,1)S(1)} %slice.26), channel_id=1, source_target_pairs={{0,64},{32,96},{64,128},{96,160},{128,192},{160,224},{192,0},{224,... | collective-permute-start | bytes 491528 | tf_op jit(solution)/shard_map/ppermute | solution.py:262
  66.9 4.8 %collective-permute-start.9 = (bf16[64,1280]{1,0:T(8,128)(2,1)S(1)}, bf16[64,1280]{1,0:T(8,128)(2,1)S(1)}, u32[]{:S(2)}, u32[]{:S(2)}) collective-permute-start(bf16[64,1280]{1,0:T(8,128)(2,1)S(1)} %get-tuple-element.50), channel_id=1, source_target_pairs={{0,192},{32,224},{64,0},{96,32},{128,64},{160,96},{192,128},{224,1... | collective-permute-start | bytes 491528 | tf_op jit(solution)/shard_map/ppermute | solution.py:270
  69.4 5.4 %collective-permute-start.11 = (bf16[64,1280]{1,0:T(8,128)(2,1)S(1)}, bf16[64,1280]{1,0:T(8,128)(2,1)S(1)}, u32[]{:S(2)}, u32[]{:S(2)}) collective-permute-start(bf16[64,1280]{1,0:T(8,128)(2,1)S(1)} %get-tuple-element.51), channel_id=1, source_target_pairs={{0,64},{32,96},{64,128},{96,160},{128,192},{160,224},{192,0},{224,... | collective-permute-start | bytes 491528 | tf_op jit(solution)/shard_map/ppermute | solution.py:271
  74.9 8.9 %collective-permute-start.12 = (bf16[128,1280]{1,0:T(8,128)(2,1)S(1)}, bf16[128,1280]{1,0:T(8,128)(2,1)S(1)}, u32[]{:S(2)}, u32[]{:S(2)}) collective-permute-start(bf16[128,1280]{1,0:T(8,128)(2,1)S(1)} %pad_maximum_fusion.4), channel_id=1, source_target_pairs={{0,64},{32,96},{64,128},{96,160},{128,192},{160,224},{192,0},{224,... | collective-permute-start | bytes 983048 | tf_op jit(solution)/shard_map/ppermute | solution.py:277
  75.2 8.6 %collective-permute-start.10 = (bf16[128,1280]{1,0:T(8,128)(2,1)S(1)}, bf16[128,1280]{1,0:T(8,128)(2,1)S(1)}, u32[]{:S(2)}, u32[]{:S(2)}) collective-permute-start(bf16[128,1280]{1,0:T(8,128)(2,1)S(1)} %pad_maximum_fusion.3), channel_id=1, source_target_pairs={{0,192},{32,224},{64,0},{96,32},{128,64},{160,96},{192,128},{224,1... | collective-permute-start | bytes 983048 | tf_op jit(solution)/shard_map/ppermute | solution.py:276
  119.4 15.5 %all-to-all-start.4 = ((f32[4,32,1280]{2,1,0:T(8,128)}), f32[4,32,1280]{2,1,0:T(8,128)S(1)}, u32[]{:S(2)}, u32[]{:S(2)}) async-start(f32[4,32,1280]{2,1,0:T(8,128)} %broadcast_in_dim.9), calls=%async_computation.4 | async-start | bytes 1310720 | tf_op jit(solution)/shard_map/all_to_all | solution.py:286
  122.9 21.5 %collective-permute-start.14 = (f32[4,32,1280]{2,1,0:T(8,128)S(1)}, f32[4,32,1280]{2,1,0:T(8,128)S(1)}, u32[]{:S(2)}, u32[]{:S(2)}) collective-permute-start(f32[4,32,1280]{2,1,0:T(8,128)S(1)} %pad_maximum_fusion.text_near_ref), channel_id=1, source_target_pairs={{0,32},{32,0},{64,96},{96,64},{128,160},{160,128},{192,224},{224,1... | collective-permute-start | bytes 1966088 | tf_op jit(solution)/shard_map/ppermute | solution.py:281
  134.9 10.5 %collective-permute-start.13 = (f32[4,32,1280]{2,1,0:T(8,128)S(1)}, f32[4,32,1280]{2,1,0:T(8,128)S(1)}, u32[]{:S(2)}, u32[]{:S(2)}) collective-permute-start(f32[4,32,1280]{2,1,0:T(8,128)S(1)} %all-to-all-done.4.near_ref), channel_id=1, source_target_pairs={{0,32},{32,0},{64,96},{96,64},{128,160},{160,128},{192,224},{224,1... | collective-permute-start | bytes 1966088 | tf_op jit(solution)/shard_map/ppermute | solution.py:294

commit v2 on v1

--- a/solution.py
+++ b/solution.py
@@ -7,6 +7,8 @@
 
 X, CORES, Y, Z = 4, 2, 4, 8
 CAP = 4
+ROWS, PARTS = 8, 3
+LANES, WIDTH = 128, 1280
 SLOTS = Y * Z * CAP
 PAIRS = X * CORES * Y * Z
 VMEM = pl.BlockSpec(memory_space=pltpu.VMEM)
@@ -35,36 +37,70 @@
     return narrow(wide(iota((SLOTS, target.shape[1]), 0) == target))
 
 
-def dispatch_kernel(tokens_ref, gain_ref, ids_ref, ranks_ref, out_ref, target_ref):
+def dispatch_kernel(tokens_ref, gain_ref, ids_ref, ranks_ref, text_ref, out_ref, target_ref):
     ids = ids_ref[...]
     base = wide(ids * 256)
     key = base + wide(ranks_ref[...])
     others = as_column(key)
     earlier = (others >= base) & (others < key)
     slots = jnp.sum(wide(earlier), axis=0, keepdims=True).astype(jnp.int32)
-    target = jnp.where(slots < CAP, ids * CAP + slots, -1)
-    target_ref[...] = target
+    kept = slots < CAP
+    target_ref[...] = jnp.where(kept, ids * CAP + slots, -1)
     values = wide(tokens_ref[...])
     center = values - jnp.mean(values, axis=-1, keepdims=True)
     spread = jnp.mean(center * center, axis=-1, keepdims=True)
-    normed = narrow(center * lax.rsqrt(spread + 1e-06) * gain_ref[...])
-    out_ref[...] = narrow(
-        jnp.dot(table_of(target), normed, preferred_element_type=jnp.float32)
-    )
-
-
-def dispatch(tokens, gain, ids, ranks):
+    gain = jnp.concatenate([gain_ref[i : i + 1, :] for i in range(gain_ref.shape[0])], axis=1)
+    normed = narrow(center * lax.rsqrt(spread + 1e-06) * gain)
+    table = narrow(wide(iota((Y * Z * ROWS, ids.shape[1]), 0) == jnp.where(kept, ids * ROWS + slots, -1)))
+    picked = jnp.dot(table, normed, preferred_element_type=jnp.float32)
+    part = iota(picked.shape, 0) & (ROWS - 1)
+    rest = text_ref[...]
+    for index in range(PARTS):
+        piece = wide(narrow(rest))
+        rest = rest - piece
+        picked = jnp.where(part == CAP + index, piece, picked)
+    out_ref[...] = narrow(picked)
+
+
+def dispatch(tokens, gain, ids, ranks, text):
     rows, width = tokens.shape
     return pl.pallas_call(
         dispatch_kernel,
         out_shape=(
-            jax.ShapeDtypeStruct((SLOTS, width), jnp.bfloat16),
+            jax.ShapeDtypeStruct((Y * Z * ROWS, width), jnp.bfloat16),
             jax.ShapeDtypeStruct((1, rows), jnp.int32),
         ),
-        in_specs=[VMEM] * 4,
+        in_specs=[VMEM] * 5,
         out_specs=(VMEM, VMEM),
+        compiler_params=pltpu.CompilerParams(vmem_limit_bytes=32 * 2**20),
         name="dispatch",
-    )(tokens, gain, ids, ranks)
+    )(tokens, gain, ids, ranks, text)
+
+
+def unpack_kernel(blocks_ref, rows_ref, text_ref):
+    blocks = blocks_ref[...]
+    count = blocks.shape[0]
+    row, col = iota((SLOTS, count), 0), iota((SLOTS, count), 1)
+    pick = narrow(wide(col == (row >> 2) * ROWS + (row & (CAP - 1))))
+    rows_ref[...] = narrow(jnp.dot(pick, blocks, preferred_element_type=jnp.float32))
+    row, col = iota((Y * Z, count), 0), iota((Y * Z, count), 1)
+    part = col - row * ROWS
+    pick = narrow(wide((part >= CAP) & (part < CAP + PARTS)))
+    text_ref[...] = jnp.dot(pick, blocks, preferred_element_type=jnp.float32)
+
+
+def unpack(blocks):
+    width = blocks.shape[1]
+    return pl.pallas_call(
+        unpack_kernel,
+        out_shape=(
+            jax.ShapeDtypeStruct((SLOTS, width), jnp.bfloat16),
+            jax.ShapeDtypeStruct((Y * Z, width), jnp.float32),
+        ),
+        in_specs=[VMEM],
+        out_specs=(VMEM, VMEM),
+        name="unpack",
+    )(blocks)
 
 
 def combine_kernel(returned_ref, target_ref, gate_ref, tokens_ref, out_ref, pooled_ref):
@@ -77,7 +113,10 @@
     moe_out = narrow(wide(tokens_ref[...]) + as_column(gate_ref[...]) * expert_part)
     out_ref[...] = moe_out
     pooled = jnp.mean(wide(moe_out), axis=0, keepdims=True)
-    pooled_ref[...] = jnp.broadcast_to(pooled, pooled_ref.shape)
+    pieces = pooled.shape[1] // LANES
+    for index in range(pieces):
+        piece = pooled[:, index * LANES : (index + 1) * LANES]
+        pooled_ref[pl.ds(index, Y * Z, stride=pieces), :] = jnp.broadcast_to(piece, (Y * Z, LANES))
 
 
 def combine(returned, target, gate, tokens):
@@ -86,7 +125,7 @@
         combine_kernel,
         out_shape=(
             jax.ShapeDtypeStruct((rows, width), jnp.bfloat16),
-            jax.ShapeDtypeStruct((Y * Z, width), jnp.float32),
+            jax.ShapeDtypeStruct((Y * Z * width // LANES, LANES), jnp.float32),
         ),
         in_specs=[VMEM] * 4,
         out_specs=(VMEM, VMEM),
@@ -94,33 +133,33 @@
     )(returned, target, gate, tokens)
 
 
-def contrast_kernel(
-    place_ref,
-    scale_ref,
-    near_ref,
-    other_ref,
-    text_near_ref,
-    text_other_ref,
-    loss_ref,
-    image_ref,
-    dtext_ref,
-    image_scr,
-    text_scr,
-):
+def full_rows(ref):
+    pieces = WIDTH // LANES
+    count = ref.shape[0] // pieces
+    return jnp.concatenate(
+        [ref[pl.ds(i, count, stride=pieces), :] for i in range(pieces)], axis=1
+    )
+
+
+def contrast_kernel(place_ref, scale_ref, *refs):
+    images, texts = (refs[:5], refs[5:10]), (refs[10:14], refs[14:18])
+    loss_ref, image_ref, dtext_ref, image_scr, text_scr = refs[18:]
     place_x, core, expert = place_ref[0], place_ref[1], place_ref[2]
     me = (place_x * CORES + core) * (Y * Z) + expert
     scale = scale_ref[0]
 
-    def put(scratch, x, c, rows):
+    def put(scratch, x, c, first, rows):
         square = jnp.sum(rows * rows, axis=-1, keepdims=True)
-        start = pl.multiple_of((x * CORES + c) * (Y * Z), Y * Z)
-        scratch[pl.ds(start, Y * Z), :] = rows / jnp.sqrt(square + 1e-06)
-
-    for step in range(X):
-        put(image_scr, step, core, near_ref[step])
-        put(image_scr, step, 1 - core, other_ref[step])
-        put(text_scr, (place_x - step) & (X - 1), core, text_near_ref[step])
-        put(text_scr, (place_x - step) & (X - 1), 1 - core, text_other_ref[step])
+        start = pl.multiple_of((x & (X - 1)) * (CORES * Y * Z) + c * (Y * Z) + first, 8)
+        scratch[pl.ds(start, rows.shape[0]), :] = rows / jnp.sqrt(square + 1e-06)
+
+    half = Y * Z // 2
+    for side in range(CORES):
+        c = core + side - 2 * core * side
+        for ref, step, first in zip(images[side], (0, 3, 1, 2, 2), (0, 0, 0, 0, half)):
+            put(image_scr, place_x + step, c, first, full_rows(ref))
+        for ref, step in zip(texts[side], (0, 3, 2, 1)):
+            put(text_scr, place_x + step, c, 0, ref[...])
     image_unit = image_scr[...]
     text_unit = text_scr[...]
     logits = scale * lax.dot_general(
@@ -154,54 +193,60 @@
         radius = jnp.sqrt(jnp.sum(rows * rows, axis=-1, keepdims=True) + 1e-06)
         return rows / radius, radius
 
-    image_ref[...] = back(*own(near_ref[place_x, pl.ds(expert, 1), :]), d_image)
-    dtext_ref[...] = back(*own(text_near_ref[0, pl.ds(expert, 1), :]), d_text)
-
-
-def contrast(places, scale, near, other, text_near, text_other):
-    width = near.shape[-1]
-    row = jax.ShapeDtypeStruct((1, width), jnp.float32)
+    pieces = WIDTH // LANES
+    own_image = jnp.concatenate(
+        [images[0][0][pl.ds(expert * pieces + i, 1), :] for i in range(pieces)], axis=1
+    )
+    image_ref[...] = back(*own(own_image), d_image)
+    dtext_ref[...] = back(*own(texts[0][0][pl.ds(expert, 1), :]), d_text)
+
+
+def contrast(places, scale, images, other_images, texts, other_texts):
+    row = jax.ShapeDtypeStruct((1, WIDTH), jnp.float32)
     return pl.pallas_call(
         contrast_kernel,
         out_shape=(jax.ShapeDtypeStruct((1, 1), jnp.float32), row, row),
-        in_specs=[SMEM, SMEM, VMEM, VMEM, VMEM, VMEM],
+        in_specs=[SMEM, SMEM] + [VMEM] * 18,
         out_specs=(VMEM, VMEM, VMEM),
-        scratch_shapes=[pltpu.VMEM((PAIRS, width), jnp.float32)] * 2,
+        scratch_shapes=[pltpu.VMEM((PAIRS, WIDTH), jnp.float32)] * 2,
         compiler_params=pltpu.CompilerParams(vmem_limit_bytes=32 * 2**20),
         name="contrast",
-    )(places, scale, near, other, text_near, text_other)
-
-
-HIDDEN_STEP = 128
-
-
-def expert_kernel(rows_ref, in_own, in_other, out_own, out_other, out_ref):
-    first = jnp.concatenate([in_own[...], in_other[...]], axis=1)
-    second = jnp.concatenate([out_own[...], out_other[...]], axis=0)
-    hidden = jax.nn.gelu(jnp.dot(rows_ref[...], first, preferred_element_type=jnp.float32))
-    part = jnp.dot(narrow(hidden), second, preferred_element_type=jnp.float32)
-
-    @pl.when(pl.program_id(0) == 0)
-    def _():
-        out_ref[...] = part
-
-    @pl.when(pl.program_id(0) > 0)
-    def _():
-        out_ref[...] += part
+    )(places, scale, *images, *other_images, *texts, *other_texts)
+
+
+def expert_kernel(rows_ref, in_own, in_other, out_own, out_other, out_ref, hidden_scr):
+    rows = rows_ref[...]
+    share = in_own.shape[1]
+    tile = 2 * LANES
+    whole = share // tile * tile
+    cuts = [slice(i, i + tile) for i in range(0, whole, tile)]
+
+    def hidden_of(first):
+        hidden = jax.nn.gelu(jnp.dot(rows, first, preferred_element_type=jnp.float32))
+        return narrow(hidden)
+
+    for cut in cuts:
+        hidden_scr[:, cut] = hidden_of(in_own[:, cut])
+        hidden_scr[:, share + cut.start : share + cut.stop] = hidden_of(in_other[:, cut])
+    last = hidden_of(jnp.concatenate([in_own[:, whole:], in_other[:, whole:]], axis=1))
+    hidden_scr[:, whole:share] = last[:, : share - whole]
+    hidden_scr[:, share + whole :] = last[:, share - whole :]
+    hidden = hidden_scr[...]
+    for i in range(0, out_ref.shape[1], tile):
+        cut = slice(i, i + tile)
+        second = jnp.concatenate([out_own[:, cut], out_other[:, cut]], axis=0)
+        out_ref[:, cut] = jnp.dot(hidden, second, preferred_element_type=jnp.float32)
 
 
 def expert_rows(rows, in_own, in_other, out_own, out_other):
     count, width = rows.shape
     hidden = in_own.shape[1]
-    whole = pl.BlockSpec((count, width), lambda i: (0, 0))
-    first = pl.BlockSpec((width, HIDDEN_STEP), lambda i: (0, i))
-    second = pl.BlockSpec((HIDDEN_STEP, width), lambda i: (i, 0))
     return pl.pallas_call(
         expert_kernel,
-        grid=(hidden // HIDDEN_STEP,),
         out_shape=jax.ShapeDtypeStruct((count, width), jnp.float32),
-        in_specs=[whole, first, first, second, second],
-        out_specs=whole,
+        in_specs=[VMEM] * 5,
+        out_specs=VMEM,
+        scratch_shapes=[pltpu.VMEM((count, 2 * hidden), jnp.bfloat16)],
         compiler_params=pltpu.CompilerParams(vmem_limit_bytes=32 * 2**20),
         cost_estimate=pl.CostEstimate(
             flops=8 * count * width * hidden,
@@ -220,10 +265,6 @@
     return "dp", [(i, i ^ 1) for i in range(X * CORES)]
 
 
-def groups_x():
-    return [[x * CORES + c for x in range(X)] for c in range(CORES)]
-
-
 def to_experts(blocks):
     return lax.all_to_all(blocks, "expert", split_axis=0, concat_axis=0, tiled=True)
 
@@ -236,7 +277,6 @@
     dp_place = lax.axis_index("dp")
     places = jnp.stack([dp_place // CORES, dp_place % CORES, lax.axis_index("expert")])
 
-    text_block = to_experts(jnp.broadcast_to(text_emb, (Y * Z, width)))
     weights = (
         w_in[0],
         lax.ppermute(w_in[0], *along_core()),
@@ -245,13 +285,14 @@
     )
 
     outgoing, target = dispatch(
-        tokens, norm_gain.reshape(1, width), expert_ids.reshape(1, rows), priority
-    )
-    text_block, outgoing = lax.optimization_barrier((text_block, outgoing))
-    text_x = [text_block] + [lax.ppermute(text_block, *along_x(d)) for d in range(1, X)]
-    own_rows = to_experts(outgoing.reshape(Y * Z, CAP, width)).reshape(SLOTS, width)
-
-    text_x, own_rows = lax.optimization_barrier((text_x, own_rows))
+        tokens,
+        norm_gain.reshape(width // LANES, LANES),
+        expert_ids.reshape(1, rows),
+        priority,
+        text_emb,
+    )
+    incoming = to_experts(outgoing.reshape(Y * Z, ROWS, width))
+    own_rows, text_block = unpack(incoming.reshape(Y * Z * ROWS, width))
 
     left_rows = lax.ppermute(own_rows, *along_x(1))
     right_rows = lax.ppermute(own_rows, *along_x(-1))
@@ -277,23 +318,25 @@
     right_sum = lax.ppermute(narrow(right_sum), *along_x(1))
     result = narrow(own_part + wide(left_sum) + wide(right_sum))
 
-    text_near, result = lax.optimization_barrier((jnp.stack(text_x), result))
-    text_other = lax.ppermute(text_near, *along_core())
+    text_block, result = lax.optimization_barrier((text_block, result))
+    texts = [text_block] + [lax.ppermute(text_block, *along_x(d)) for d in range(1, X)]
     returned = to_experts(result.reshape(Y * Z, CAP, width)).reshape(SLOTS, width)
+    texts, returned = lax.optimization_barrier((texts, returned))
     moe_out, pooled = combine(returned, target, gate_prob.reshape(1, rows), tokens)
 
-    near = to_experts(pooled)
-    near = lax.all_to_all(
-        jnp.broadcast_to(near, (X,) + near.shape),
-        "dp",
-        split_axis=0,
-        concat_axis=0,
-        tiled=True,
-        axis_index_groups=groups_x(),
-    )
-    other = lax.ppermute(near, *along_core())
+    near = to_experts(pooled.reshape(Y * Z, 1, width)).reshape(pooled.shape)
+    half = near.shape[0] // 2
+    left = lax.ppermute(near, *along_x(1))
+    right = lax.ppermute(near, *along_x(-1))
+    far = [lax.ppermute(left[:half], *along_x(1)), lax.ppermute(right[half:], *along_x(-1))]
+    images = [near, left, right] + far
     loss, grad_image, grad_text = contrast(
-        places, logit_scale, near, other, text_near, text_other
+        places,
+        logit_scale,
+        images,
+        [lax.ppermute(block, *along_core()) for block in images],
+        texts,
+        [lax.ppermute(block, *along_core()) for block in texts],
     )
     return (moe_out, loss.reshape(1), grad_image, grad_text)
 

time: 150 us -> 137 us (0.913)
  blocking collectives: 30.1 us -> 42.8 us
  starting transfers between devices: 57.2 us -> 45.5 us
  Pallas kernels: 25.9 us -> 18.3 us
  local copies, waits for them, and re-layouts: 10.4 us -> 7.94 us
  other arithmetic: 2.27 us -> 0.45 us
    all_to_all x2, blocking collectives: 30.1 us -> 42.8 us  [to_experts(): lax.all_to_all(blocks, 'expert', split_axis=0, concat_axis=0, tiled=True)]
    pallas_call x4 -> x5, Pallas kernels: 19.8 us -> 12.1 us  [the longest x3 9.1 us: expert_rows(): pl.pallas_call(expert_kernel, out_shape=jax.ShapeDtypeStruct((count, widt...]
    all_to_all x2 -> x1, starting transfers between devices: 14.7 us -> 9.04 us  [to_experts(): lax.all_to_all(blocks, 'expert', split_axis=0, concat_axis=0, tiled=True)]
    reshape x3 -> x0, local copies, waits for them, and re-layouts: 4.84 us -> none  [the longest x1 1.77 us: on_device(): to_experts(outgoing.reshape(Y * Z, CAP, width)).reshape(SLOTS, width)]
    all_to_all x2 -> x1, waiting for transfers between devices: 10.5 us -> 5.86 us  [to_experts(): lax.all_to_all(blocks, 'expert', split_axis=0, concat_axis=0, tiled=True)]
    unnamed x8 -> x22, local copies, waits for them, and re-layouts: 1.92 us -> 6.25 us
    all_to_all x1 -> x0, starting transfers between devices: 3.48 us -> none  [on_device(): lax.all_to_all(jnp.broadcast_to(near, (X,) + near.shape), 'dp', split_axi...]
    broadcast_in_dim x2 -> x0, local copies, waits for them, and re-layouts: 1.64 us -> none  [the longest x1 0.89 us: on_device(): jnp.broadcast_to(near, (X,) + near.shape)]
  transfers between devices with their start and end apart: 18 -> 27, of which waited for: 6 -> 9; matrix products, arithmetic and copies ran while one was open for 6% -> 1% of each run, Pallas kernels for 10% -> 7%
where the time goes in v2:
time: 137 us
  starting transfers between devices  45.5 us (33%)
  blocking collectives  42.8 us (31%)
  waiting for transfers between devices  20.2 us (15%)
  Pallas kernels  18.3 us (13%)
  local copies, waits for them, and re-layouts  7.94 us (6%)
  between operations  1.56 us (1%)
    all_to_all x2, blocking collectives, to_experts(): lax.all_to_all(blocks, 'expert', split_axis=0, concat_axis=0, tiled=True)  42.8 us
    ppermute x9, starting transfers between devices, on_device(): lax.ppermute(block, *along_core())  14 us
    pallas_call x3, Pallas kernels, expert_rows(): pl.pallas_call(expert_kernel, out_shape=jax.ShapeDtypeStruct((count, widt...  9.1 us
    all_to_all x1, starting transfers between devices, to_experts(): lax.all_to_all(blocks, 'expert', split_axis=0, concat_axis=0, tiled=True)  9.04 us
    unnamed x22, local copies, waits for them, and re-layouts  6.25 us
    ppermute x1, waiting for transfers between devices, on_device(): right_sum = lax.ppermute(narrow(right_sum), *along_x(1))  5.87 us
    all_to_all x1, waiting for transfers between devices, to_experts(): lax.all_to_all(blocks, 'expert', split_axis=0, concat_axis=0, tiled=True)  5.86 us
    ppermute x3, starting transfers between devices, on_device(): lax.ppermute(text_block, *along_x(d))  4.04 us
  transfers between devices with their start and end apart: 27, of which 9 were waited for; matrix products, arithmetic and copies ran while one was open for 1% of the time, Pallas kernels for 7%

profile of v2, /device:TPU:1, one launch (start us, length us, event | category | flops | bytes accessed | tf_op | source)
XLA Modules:
  0.0 136.8 jit_solution(14790206537882974055)
XLA Ops:
  0.6 3.3 %collective-permute-start.2 = (bf16[1280,640]{1,0:T(8,128)(2,1)}, bf16[1280,640]{1,0:T(8,128)(2,1)S(1)}, u32[]{:S(2)}, u32[]{:S(2)}) collective-permute-start(bf16[1280,640]{1,0:T(8,128)(2,1)} %bitcast.13), channel_id=1, source_target_pairs={{0,32},{32,0},{64,96},{96,64},{128,160},{160,128},{192,224},{224,1... | collective-permute-start | bytes 4915208 | tf_op jit(solution)/shard_map/ppermute | solution.py:282
  8.8 26.3 %all_to_all.15 = bf16[32,8,1280]{2,1,0:T(8,128)(2,1)} all-to-all(bf16[32,8,1280]{2,1,0:T(8,128)(2,1)S(1)} %bitcast.25), channel_id=1, replica_groups=mesh['dp'=8,'expert'=32] {'expert'}, dimensions={0} | all-to-all | bytes 1310720 | tf_op jit(solution)/shard_map/all_to_all | solution.py:269
  35.0 2.1 %unpack.1 = (bf16[128,1280]{1,0:T(8,128)(2,1)}, f32[32,1280]{1,0:T(8,128)}) custom-call(bf16[256,1280]{1,0:T(8,128)(2,1)} %bitcast.28), custom_call_target="tpu_custom_call" | custom-call | tf_op jit(solution)/shard_map/unpack/pallas_call | solution.py:94
  38.4 1.5 %collective-permute-start.1 = (bf16[128,1280]{1,0:T(8,128)(2,1)}, bf16[128,1280]{1,0:T(8,128)(2,1)S(1)}, u32[]{:S(2)}, u32[]{:S(2)}) collective-permute-start(bf16[128,1280]{1,0:T(8,128)(2,1)} %get-tuple-element.27.rows_ref), channel_id=1, source_target_pairs={{0,192},{32,224},{64,0},{96,32},{128,64},{160,96},{192,128},{224,1... | collective-permute-start | bytes 983048 | tf_op jit(solution)/shard_map/ppermute | solution.py:298
  39.9 1.4 %copy-done.1 = bf16[1,640,1280]{2,1,0:T(8,128)(2,1)S(1)} copy-done((bf16[1,640,1280]{2,1,0:T(8,128)(2,1)S(1)}, bf16[1,640,1280]{2,1,0:T(8,128)(2,1)}, u32[]{:S(2)}) %copy-start.1) | copy-done | bytes 1638424
  42.3 2.7 %expert.3 = f32[128,1280]{1,0:T(8,128)S(1)} custom-call(bf16[128,1280]{1,0:T(8,128)(2,1)S(1)} %copy-done.4, bf16[1280,640]{1,0:T(8,128)(2,1)S(1)} %bitcast.14, bf16[1280,640]{1,0:T(8,128)(2,1)S(1)} %collective-permute-done.2.in_other, bf16[640,1280]{1,0:T(8,128)(2,1)S(1)} %bitcast.18, bf16[640,1280]{1,0:T(8,128)(2,1)} %collective-permute-done.3.out_other), custom_call_target="tpu_custom_call" | custom-call | flops 838860800 | bytes 7536640 | tf_op jit(solution)/shard_map/expert/pallas_call | solution.py:244
  45.1 2.2 %collective-permute-start.5 = (bf16[64,1280]{1,0:T(8,128)(2,1)S(1)}, bf16[64,1280]{1,0:T(8,128)(2,1)S(1)}, u32[]{:S(2)}, u32[]{:S(2)}) collective-permute-start(bf16[64,1280]{1,0:T(8,128)(2,1)S(1)} %slice.33), channel_id=1, source_target_pairs={{0,192},{32,224},{64,0},{96,32},{128,64},{160,96},{192,128},{224,1... | collective-permute-start | bytes 491528 | tf_op jit(solution)/shard_map/ppermute | solution.py:304
  47.5 3.7 %expert.4 = f32[256,1280]{1,0:T(8,128)S(1)} custom-call(bf16[256,1280]{1,0:T(8,128)(2,1)S(1)} %pad_maximum_fusion.rows_ref, bf16[1280,640]{1,0:T(8,128)(2,1)S(1)} %bitcast.15, bf16[1280,640]{1,0:T(8,128)(2,1)S(1)} %collective-permute-done.2.in_other, bf16[640,1280]{1,0:T(8,128)(2,1)S(1)} %bitcast.19, bf16[640,1280]{1,0:T(8,128)(2,1)} %collective-permute-done.3.out_other), custom_call_target="tpu_custom_call" | custom-call | flops 1677721600 | bytes 8519680 | tf_op jit(solution)/shard_map/expert/pallas_call | solution.py:244
  51.4 1.4 collective-permute-done.4
  52.8 2.7 %expert.5 = f32[128,1280]{1,0:T(8,128)S(1)} custom-call(bf16[128,1280]{1,0:T(8,128)(2,1)S(1)} %pad_maximum_fusion.1.rows_ref, bf16[1280,640]{1,0:T(8,128)(2,1)S(1)} %bitcast.16, bf16[1280,640]{1,0:T(8,128)(2,1)S(1)} %collective-permute-done.2.in_other, bf16[640,1280]{1,0:T(8,128)(2,1)S(1)} %bitcast.20, bf16[640,1280]{1,0:T(8,128)(2,1)} %collective-permute-done.3.out_other), custom_call_target="tpu_custom_call" | custom-call | flops 838860800 | bytes 7536640 | tf_op jit(solution)/shard_map/expert/pallas_call | solution.py:244
  57.2 2.9 %collective-permute-done.6 = bf16[64,1280]{1,0:T(8,128)(2,1)S(1)} collective-permute-done((bf16[64,1280]{1,0:T(8,128)(2,1)S(1)}, bf16[64,1280]{1,0:T(8,128)(2,1)S(1)}, u32[]{:S(2)}, u32[]{:S(2)}) %collective-permute-start.6) | collective-permute-done | bytes 163872 | tf_op jit(solution)/shard_map/ppermute | solution.py:311
  60.1 2.0 %collective-permute-done.8 = bf16[64,1280]{1,0:T(8,128)(2,1)S(1)} collective-permute-done((bf16[64,1280]{1,0:T(8,128)(2,1)S(1)}, bf16[64,1280]{1,0:T(8,128)(2,1)S(1)}, u32[]{:S(2)}, u32[]{:S(2)}) %collective-permute-start.8) | collective-permute-done | bytes 163872 | tf_op jit(solution)/shard_map/ppermute | solution.py:312
  62.5 2.7 %collective-permute-start.7 = (bf16[128,1280]{1,0:T(8,128)(2,1)S(1)}, bf16[128,1280]{1,0:T(8,128)(2,1)S(1)}, u32[]{:S(2)}, u32[]{:S(2)}) collective-permute-start(bf16[128,1280]{1,0:T(8,128)(2,1)S(1)} %pad_maximum_fusion.2), channel_id=1, source_target_pairs={{0,192},{32,224},{64,0},{96,32},{128,64},{160,96},{192,128},{224,1... | collective-permute-start | bytes 983048 | tf_op jit(solution)/shard_map/ppermute | solution.py:317
  65.3 5.9 %collective-permute-done.9 = bf16[128,1280]{1,0:T(8,128)(2,1)S(1)} collective-permute-done((bf16[128,1280]{1,0:T(8,128)(2,1)S(1)}, bf16[128,1280]{1,0:T(8,128)(2,1)S(1)}, u32[]{:S(2)}, u32[]{:S(2)}) %collective-permute-start.9) | collective-permute-done | bytes 327712 | tf_op jit(solution)/shard_map/ppermute | solution.py:318
  72.1 9.0 %all-to-all-start.1 = ((bf16[32,4,1280]{2,1,0:T(4,128)(2,1)}), bf16[32,4,1280]{2,1,0:T(4,128)(2,1)S(1)}, u32[]{:S(2)}, u32[]{:S(2)}) async-start(bf16[32,4,1280]{2,1,0:T(4,128)(2,1)} %reshape.42), calls=%async_computation.1 | async-start | bytes 655360 | tf_op jit(solution)/shard_map/all_to_all | solution.py:269
  81.2 4.0 %collective-permute-start.11 = (f32[32,1280]{1,0:T(8,128)S(1)}, f32[32,1280]{1,0:T(8,128)S(1)}, u32[]{:S(2)}, u32[]{:S(2)}) collective-permute-start(f32[32,1280]{1,0:T(8,128)S(1)} %copy-done.5), channel_id=1, source_target_pairs={{0,128},{32,160},{64,192},{96,224},{128,0},{160,32},{192,64},{224,... | collective-permute-start | bytes 491528 | tf_op jit(solution)/shard_map/ppermute | solution.py:322
  85.2 5.9 %all-to-all-done.1 = bf16[32,4,1280]{2,1,0:T(4,128)(2,1)S(1)} async-done(((bf16[32,4,1280]{2,1,0:T(4,128)(2,1)}), bf16[32,4,1280]{2,1,0:T(4,128)(2,1)S(1)}, u32[]{:S(2)}, u32[]{:S(2)}) %all-to-all-start.1) | async-done | bytes 327712 | tf_op jit(solution)/shard_map/all_to_all | solution.py:269
  91.8 2.6 %combine.1 = (bf16[256,1280]{1,0:T(8,128)(2,1)}, f32[320,128]{1,0:T(8,128)}) custom-call(bf16[128,1280]{1,0:T(8,128)(2,1)} %reshape.43.returned_ref, s32[1,256]{1,0:T(1,128)} %copy-done.10, f32[1,256]{1,0:T(1,128)} %bitcast.30, bf16[256,1280]{1,0:T(8,128)(2,1)} %tokens_ref.3), custom_call_target="tpu_custom_call" | custom-call | tf_op jit(solution)/shard_map/combine/pallas_call | solution.py:124
  94.4 16.6 %all_to_all.16 = f32[32,1,1280]{2,1,0:T(1,128)S(1)} all-to-all(f32[32,1,1280]{2,1,0:T(1,128)} %bitcast.29), channel_id=1, replica_groups=mesh['dp'=8,'expert'=32] {'expert'}, dimensions={0} | all-to-all | bytes 327680 | tf_op jit(solution)/shard_map/all_to_all | solution.py:269
  111.2 2.4 %collective-permute-start.14 = (f32[320,128]{1,0:T(8,128)S(1)}, f32[320,128]{1,0:T(8,128)S(1)}, u32[]{:S(2)}, u32[]{:S(2)}) collective-permute-start(f32[320,128]{1,0:T(8,128)S(1)} %bitcast.22), channel_id=1, source_target_pairs={{0,192},{32,224},{64,0},{96,32},{128,64},{160,96},{192,128},{224,1... | collective-permute-start | bytes 491528 | tf_op jit(solution)/shard_map/ppermute | solution.py:330
  113.6 8.8 %collective-permute-start.22 = (f32[32,1280]{1,0:T(8,128)S(1)}, f32[32,1280]{1,0:T(8,128)S(1)}, u32[]{:S(2)}, u32[]{:S(2)}) collective-permute-start(f32[32,1280]{1,0:T(8,128)S(1)} %copy-done.5), channel_id=1, source_target_pairs={{0,32},{32,0},{64,96},{96,64},{128,160},{160,128},{192,224},{224,1... | collective-permute-start | bytes 491528 | tf_op jit(solution)/shard_map/ppermute | solution.py:339
  123.0 2.8 %collective-permute-start.25 = (f32[32,1280]{1,0:T(8,128)S(1)}, f32[32,1280]{1,0:T(8,128)S(1)}, u32[]{:S(2)}, u32[]{:S(2)}) collective-permute-start(f32[32,1280]{1,0:T(8,128)S(1)} %collective-permute-done.12.refs_13_), channel_id=1, source_target_pairs={{0,32},{32,0},{64,96},{96,64},{128,160},{160,128},{192,224},{224,1... | collective-permute-start | bytes 491528 | tf_op jit(solution)/shard_map/ppermute | solution.py:339
  125.9 2.7 %collective-permute-start.16 = (f32[160,128]{1,0:T(8,128)S(1)}, f32[160,128]{1,0:T(8,128)S(1)}, u32[]{:S(2)}, u32[]{:S(2)}) collective-permute-start(f32[160,128]{1,0:T(8,128)S(1)} %slice.47), channel_id=1, source_target_pairs={{0,192},{32,224},{64,0},{96,32},{128,64},{160,96},{192,128},{224,1... | collective-permute-start | bytes 245768 | tf_op jit(solution)/shard_map/ppermute | solution.py:331
  133.2 3.6 %contrast.1 = (f32[1,1]{1,0:T(1,128)}, f32[1,1280]{1,0:T(1,128)}, f32[1,1280]{1,0:T(1,128)}) custom-call(s32[3]{0:T(128)S(1)} %pad_add_fusion.place_ref, f32[1]{0:T(128)S(6)} %copy.14.scale_ref, f32[320,128]{1,0:T(8,128)S(1)} %bitcast.24, f32[320,128]{1,0:T(8,128)S(1)} %collective-permute-done.13.refs_1_, f32[320,128]{1,0:T(8,128)S(1)} %collective-permute-done.14.refs_2_, ...), custom_call_target="tpu_custom_call" | custom-call | tf_op jit(solution)/shard_map/contrast/pallas_call | solution.py:206
  (78 shorter events, 16.1 us)
Async XLA Ops:
  0.6 39.2 %collective-permute-start.2 = (bf16[1280,640]{1,0:T(8,128)(2,1)}, bf16[1280,640]{1,0:T(8,128)(2,1)S(1)}, u32[]{:S(2)}, u32[]{:S(2)}) collective-permute-start(bf16[1280,640]{1,0:T(8,128)(2,1)} %bitcast.13), channel_id=1, source_target_pairs={{0,32},{32,0},{64,96},{96,64},{128,160},{160,128},{192,224},{224,1... | collective-permute-start | bytes 4915208 | tf_op jit(solution)/shard_map/ppermute | solution.py:282
  4.0 35.9 %collective-permute-start.3 = (bf16[640,1280]{1,0:T(8,128)(2,1)}, bf16[640,1280]{1,0:T(8,128)(2,1)}, u32[]{:S(2)}, u32[]{:S(2)}) collective-permute-start(bf16[640,1280]{1,0:T(8,128)(2,1)} %bitcast.17), channel_id=1, source_target_pairs={{0,32},{32,0},{64,96},{96,64},{128,160},{160,128},{192,224},{224,1... | collective-permute-start | bytes 4915208 | tf_op jit(solution)/shard_map/ppermute | solution.py:284
  37.2 7.8 %collective-permute-start = (bf16[128,1280]{1,0:T(8,128)(2,1)}, bf16[128,1280]{1,0:T(8,128)(2,1)S(1)}, u32[]{:S(2)}, u32[]{:S(2)}) collective-permute-start(bf16[128,1280]{1,0:T(8,128)(2,1)} %get-tuple-element.27.rows_ref), channel_id=1, source_target_pairs={{0,64},{32,96},{64,128},{96,160},{128,192},{160,224},{192,0},{224,... | collective-permute-start | bytes 983048 | tf_op jit(solution)/shard_map/ppermute | solution.py:297
  38.4 6.6 %collective-permute-start.1 = (bf16[128,1280]{1,0:T(8,128)(2,1)}, bf16[128,1280]{1,0:T(8,128)(2,1)S(1)}, u32[]{:S(2)}, u32[]{:S(2)}) collective-permute-start(bf16[128,1280]{1,0:T(8,128)(2,1)} %get-tuple-element.27.rows_ref), channel_id=1, source_target_pairs={{0,192},{32,224},{64,0},{96,32},{128,64},{160,96},{192,128},{224,1... | collective-permute-start | bytes 983048 | tf_op jit(solution)/shard_map/ppermute | solution.py:298
  45.1 6.4 %collective-permute-start.5 = (bf16[64,1280]{1,0:T(8,128)(2,1)S(1)}, bf16[64,1280]{1,0:T(8,128)(2,1)S(1)}, u32[]{:S(2)}, u32[]{:S(2)}) collective-permute-start(bf16[64,1280]{1,0:T(8,128)(2,1)S(1)} %slice.33), channel_id=1, source_target_pairs={{0,192},{32,224},{64,0},{96,32},{128,64},{160,96},{192,128},{224,1... | collective-permute-start | bytes 491528 | tf_op jit(solution)/shard_map/ppermute | solution.py:304
  47.3 5.5 %collective-permute-start.4 = (bf16[64,1280]{1,0:T(8,128)(2,1)S(1)}, bf16[64,1280]{1,0:T(8,128)(2,1)S(1)}, u32[]{:S(2)}, u32[]{:S(2)}) collective-permute-start(bf16[64,1280]{1,0:T(8,128)(2,1)S(1)} %slice.32), channel_id=1, source_target_pairs={{0,64},{32,96},{64,128},{96,160},{128,192},{160,224},{192,0},{224,... | collective-permute-start | bytes 491528 | tf_op jit(solution)/shard_map/ppermute | solution.py:303
  55.6 4.5 %collective-permute-start.6 = (bf16[64,1280]{1,0:T(8,128)(2,1)S(1)}, bf16[64,1280]{1,0:T(8,128)(2,1)S(1)}, u32[]{:S(2)}, u32[]{:S(2)}) collective-permute-start(bf16[64,1280]{1,0:T(8,128)(2,1)S(1)} %get-tuple-element.50), channel_id=1, source_target_pairs={{0,192},{32,224},{64,0},{96,32},{128,64},{160,96},{192,128},{224,1... | collective-permute-start | bytes 491528 | tf_op jit(solution)/shard_map/ppermute | solution.py:311
  56.7 5.4 %collective-permute-start.8 = (bf16[64,1280]{1,0:T(8,128)(2,1)S(1)}, bf16[64,1280]{1,0:T(8,128)(2,1)S(1)}, u32[]{:S(2)}, u32[]{:S(2)}) collective-permute-start(bf16[64,1280]{1,0:T(8,128)(2,1)S(1)} %get-tuple-element.51), channel_id=1, source_target_pairs={{0,64},{32,96},{64,128},{96,160},{128,192},{160,224},{192,0},{224,... | collective-permute-start | bytes 491528 | tf_op jit(solution)/shard_map/ppermute | solution.py:312
  62.2 8.9 %collective-permute-start.9 = (bf16[128,1280]{1,0:T(8,128)(2,1)S(1)}, bf16[128,1280]{1,0:T(8,128)(2,1)S(1)}, u32[]{:S(2)}, u32[]{:S(2)}) collective-permute-start(bf16[128,1280]{1,0:T(8,128)(2,1)S(1)} %pad_maximum_fusion.3), channel_id=1, source_target_pairs={{0,64},{32,96},{64,128},{96,160},{128,192},{160,224},{192,0},{224,... | collective-permute-start | bytes 983048 | tf_op jit(solution)/shard_map/ppermute | solution.py:318
  62.5 8.6 %collective-permute-start.7 = (bf16[128,1280]{1,0:T(8,128)(2,1)S(1)}, bf16[128,1280]{1,0:T(8,128)(2,1)S(1)}, u32[]{:S(2)}, u32[]{:S(2)}) collective-permute-start(bf16[128,1280]{1,0:T(8,128)(2,1)S(1)} %pad_maximum_fusion.2), channel_id=1, source_target_pairs={{0,192},{32,224},{64,0},{96,32},{128,64},{160,96},{192,128},{224,1... | collective-permute-start | bytes 983048 | tf_op jit(solution)/shard_map/ppermute | solution.py:317
  72.1 19.0 %all-to-all-start.1 = ((bf16[32,4,1280]{2,1,0:T(4,128)(2,1)}), bf16[32,4,1280]{2,1,0:T(4,128)(2,1)S(1)}, u32[]{:S(2)}, u32[]{:S(2)}) async-start(bf16[32,4,1280]{2,1,0:T(4,128)(2,1)} %reshape.42), calls=%async_computation.1 | async-start | bytes 655360 | tf_op jit(solution)/shard_map/all_to_all | solution.py:269
  81.1 10.7 %collective-permute-start.10 = (f32[32,1280]{1,0:T(8,128)S(1)}, f32[32,1280]{1,0:T(8,128)S(1)}, u32[]{:S(2)}, u32[]{:S(2)}) collective-permute-start(f32[32,1280]{1,0:T(8,128)S(1)} %copy-done.5), channel_id=1, source_target_pairs={{0,64},{32,96},{64,128},{96,160},{128,192},{160,224},{192,0},{224,... | collective-permute-start | bytes 491528 | tf_op jit(solution)/shard_map/ppermute | solution.py:322
  81.2 10.6 %collective-permute-start.11 = (f32[32,1280]{1,0:T(8,128)S(1)}, f32[32,1280]{1,0:T(8,128)S(1)}, u32[]{:S(2)}, u32[]{:S(2)}) collective-permute-start(f32[32,1280]{1,0:T(8,128)S(1)} %copy-done.5), channel_id=1, source_target_pairs={{0,128},{32,160},{64,192},{96,224},{128,0},{160,32},{192,64},{224,... | collective-permute-start | bytes 491528 | tf_op jit(solution)/shard_map/ppermute | solution.py:322
  85.2 6.7 %collective-permute-start.12 = (f32[32,1280]{1,0:T(8,128)S(1)}, f32[32,1280]{1,0:T(8,128)S(1)}, u32[]{:S(2)}, u32[]{:S(2)}) collective-permute-start(f32[32,1280]{1,0:T(8,128)S(1)} %copy-done.5), channel_id=1, source_target_pairs={{0,192},{32,224},{64,0},{96,32},{128,64},{160,96},{192,128},{224,1... | collective-permute-start | bytes 491528 | tf_op jit(solution)/shard_map/ppermute | solution.py:322
  111.0 12.0 %collective-permute-start.13 = (f32[320,128]{1,0:T(8,128)S(1)}, f32[320,128]{1,0:T(8,128)S(1)}, u32[]{:S(2)}, u32[]{:S(2)}) collective-permute-start(f32[320,128]{1,0:T(8,128)S(1)} %bitcast.21), channel_id=1, source_target_pairs={{0,64},{32,96},{64,128},{96,160},{128,192},{160,224},{192,0},{224,... | collective-permute-start | bytes 491528 | tf_op jit(solution)/shard_map/ppermute | solution.py:329
  111.2 14.5 %collective-permute-start.14 = (f32[320,128]{1,0:T(8,128)S(1)}, f32[320,128]{1,0:T(8,128)S(1)}, u32[]{:S(2)}, u32[]{:S(2)}) collective-permute-start(f32[320,128]{1,0:T(8,128)S(1)} %bitcast.22), channel_id=1, source_target_pairs={{0,192},{32,224},{64,0},{96,32},{128,64},{160,96},{192,128},{224,1... | collective-permute-start | bytes 491528 | tf_op jit(solution)/shard_map/ppermute | solution.py:330
  113.6 12.2 %collective-permute-start.22 = (f32[32,1280]{1,0:T(8,128)S(1)}, f32[32,1280]{1,0:T(8,128)S(1)}, u32[]{:S(2)}, u32[]{:S(2)}) collective-permute-start(f32[32,1280]{1,0:T(8,128)S(1)} %copy-done.5), channel_id=1, source_target_pairs={{0,32},{32,0},{64,96},{96,64},{128,160},{160,128},{192,224},{224,1... | collective-permute-start | bytes 491528 | tf_op jit(solution)/shard_map/ppermute | solution.py:339
  122.4 6.2 %collective-permute-start.23 = (f32[32,1280]{1,0:T(8,128)S(1)}, f32[32,1280]{1,0:T(8,128)S(1)}, u32[]{:S(2)}, u32[]{:S(2)}) collective-permute-start(f32[32,1280]{1,0:T(8,128)S(1)} %collective-permute-done.10.refs_11_), channel_id=1, source_target_pairs={{0,32},{32,0},{64,96},{96,64},{128,160},{160,128},{192,224},{224,1... | collective-permute-start | bytes 491528 | tf_op jit(solution)/shard_map/ppermute | solution.py:339
  122.4 6.7 %collective-permute-start.24 = (f32[32,1280]{1,0:T(8,128)S(1)}, f32[32,1280]{1,0:T(8,128)S(1)}, u32[]{:S(2)}, u32[]{:S(2)}) collective-permute-start(f32[32,1280]{1,0:T(8,128)S(1)} %collective-permute-done.11.refs_12_), channel_id=1, source_target_pairs={{0,32},{32,0},{64,96},{96,64},{128,160},{160,128},{192,224},{224,1... | collective-permute-start | bytes 491528 | tf_op jit(solution)/shard_map/ppermute | solution.py:339
  123.0 6.3 %collective-permute-start.25 = (f32[32,1280]{1,0:T(8,128)S(1)}, f32[32,1280]{1,0:T(8,128)S(1)}, u32[]{:S(2)}, u32[]{:S(2)}) collective-permute-start(f32[32,1280]{1,0:T(8,128)S(1)} %collective-permute-done.12.refs_13_), channel_id=1, source_target_pairs={{0,32},{32,0},{64,96},{96,64},{128,160},{160,128},{192,224},{224,1... | collective-permute-start | bytes 491528 | tf_op jit(solution)/shard_map/ppermute | solution.py:339
  125.8 5.4 %collective-permute-start.15 = (f32[160,128]{1,0:T(8,128)S(1)}, f32[160,128]{1,0:T(8,128)S(1)}, u32[]{:S(2)}, u32[]{:S(2)}) collective-permute-start(f32[160,128]{1,0:T(8,128)S(1)} %slice.46), channel_id=1, source_target_pairs={{0,64},{32,96},{64,128},{96,160},{128,192},{160,224},{192,0},{224,... | collective-permute-start | bytes 245768 | tf_op jit(solution)/shard_map/ppermute | solution.py:331
  125.9 6.0 %collective-permute-start.16 = (f32[160,128]{1,0:T(8,128)S(1)}, f32[160,128]{1,0:T(8,128)S(1)}, u32[]{:S(2)}, u32[]{:S(2)}) collective-permute-start(f32[160,128]{1,0:T(8,128)S(1)} %slice.47), channel_id=1, source_target_pairs={{0,192},{32,224},{64,0},{96,32},{128,64},{160,96},{192,128},{224,1... | collective-permute-start | bytes 245768 | tf_op jit(solution)/shard_map/ppermute | solution.py:331
  129.2 4.0 %collective-permute-start.18 = (f32[320,128]{1,0:T(8,128)S(1)}, f32[320,128]{1,0:T(8,128)S(1)}, u32[]{:S(2)}, u32[]{:S(2)}) collective-permute-start(f32[320,128]{1,0:T(8,128)S(1)} %collective-permute-done.13.refs_1_), channel_id=1, source_target_pairs={{0,32},{32,0},{64,96},{96,64},{128,160},{160,128},{192,224},{224,1... | collective-permute-start | bytes 491528 | tf_op jit(solution)/shard_map/ppermute | solution.py:337
  129.3 3.9 %collective-permute-start.19 = (f32[320,128]{1,0:T(8,128)S(1)}, f32[320,128]{1,0:T(8,128)S(1)}, u32[]{:S(2)}, u32[]{:S(2)}) collective-permute-start(f32[320,128]{1,0:T(8,128)S(1)} %collective-permute-done.14.refs_2_), channel_id=1, source_target_pairs={{0,32},{32,0},{64,96},{96,64},{128,160},{160,128},{192,224},{224,1... | collective-permute-start | bytes 491528 | tf_op jit(solution)/shard_map/ppermute | solution.py:337
  (14 other events, 91.9 us)

commit v3 on v2

--- a/solution.py
+++ b/solution.py
@@ -7,11 +7,11 @@
 
 X, CORES, Y, Z = 4, 2, 4, 8
 CAP = 4
-ROWS, PARTS = 8, 3
 LANES, WIDTH = 128, 1280
 SLOTS = Y * Z * CAP
 PAIRS = X * CORES * Y * Z
 VMEM = pl.BlockSpec(memory_space=pltpu.VMEM)
+HBM = pl.BlockSpec(memory_space=pltpu.HBM)
 SMEM = pl.BlockSpec(memory_space=pltpu.SMEM)
 
 
@@ -37,70 +37,54 @@
     return narrow(wide(iota((SLOTS, target.shape[1]), 0) == target))
 
 
-def dispatch_kernel(tokens_ref, gain_ref, ids_ref, ranks_ref, text_ref, out_ref, target_ref):
+def fetch(pairs, sems):
+    copies = [
+        pltpu.make_async_copy(source, target, sems.at[i]) for i, (source, target) in enumerate(pairs)
+    ]
+    for copy in copies:
+        copy.start()
+    for copy in copies:
+        copy.wait()
+
+
+def dispatch_kernel(tokens_hbm, gain_hbm, ids_hbm, ranks_hbm, out_ref, target_ref, *scratch):
+    tokens_ref, gain_ref, ids_ref, ranks_ref, sems = scratch
+    sources = (tokens_hbm, gain_hbm, ids_hbm, ranks_hbm)
+    fetch(list(zip(sources, (tokens_ref, gain_ref, ids_ref, ranks_ref))), sems)
     ids = ids_ref[...]
     base = wide(ids * 256)
     key = base + wide(ranks_ref[...])
     others = as_column(key)
     earlier = (others >= base) & (others < key)
     slots = jnp.sum(wide(earlier), axis=0, keepdims=True).astype(jnp.int32)
-    kept = slots < CAP
-    target_ref[...] = jnp.where(kept, ids * CAP + slots, -1)
+    target = jnp.where(slots < CAP, ids * CAP + slots, -1)
+    target_ref[...] = target
     values = wide(tokens_ref[...])
     center = values - jnp.mean(values, axis=-1, keepdims=True)
     spread = jnp.mean(center * center, axis=-1, keepdims=True)
     gain = jnp.concatenate([gain_ref[i : i + 1, :] for i in range(gain_ref.shape[0])], axis=1)
     normed = narrow(center * lax.rsqrt(spread + 1e-06) * gain)
-    table = narrow(wide(iota((Y * Z * ROWS, ids.shape[1]), 0) == jnp.where(kept, ids * ROWS + slots, -1)))
-    picked = jnp.dot(table, normed, preferred_element_type=jnp.float32)
-    part = iota(picked.shape, 0) & (ROWS - 1)
-    rest = text_ref[...]
-    for index in range(PARTS):
-        piece = wide(narrow(rest))
-        rest = rest - piece
-        picked = jnp.where(part == CAP + index, piece, picked)
-    out_ref[...] = narrow(picked)
-
-
-def dispatch(tokens, gain, ids, ranks, text):
+    out_ref[...] = narrow(
+        jnp.dot(table_of(target), normed, preferred_element_type=jnp.float32)
+    )
+
+
+def dispatch(tokens, gain, ids, ranks):
     rows, width = tokens.shape
+    inputs = (tokens, gain, ids, ranks)
     return pl.pallas_call(
         dispatch_kernel,
         out_shape=(
-            jax.ShapeDtypeStruct((Y * Z * ROWS, width), jnp.bfloat16),
+            jax.ShapeDtypeStruct((SLOTS, width), jnp.bfloat16),
             jax.ShapeDtypeStruct((1, rows), jnp.int32),
         ),
-        in_specs=[VMEM] * 5,
+        in_specs=[HBM] * 4,
         out_specs=(VMEM, VMEM),
-        compiler_params=pltpu.CompilerParams(vmem_limit_bytes=32 * 2**20),
+        scratch_shapes=[pltpu.VMEM(x.shape, x.dtype) for x in inputs]
+        + [pltpu.SemaphoreType.DMA((len(inputs),))],
+        compiler_params=pltpu.CompilerParams(vmem_limit_bytes=64 * 2**20),
         name="dispatch",
-    )(tokens, gain, ids, ranks, text)
-
-
-def unpack_kernel(blocks_ref, rows_ref, text_ref):
-    blocks = blocks_ref[...]
-    count = blocks.shape[0]
-    row, col = iota((SLOTS, count), 0), iota((SLOTS, count), 1)
-    pick = narrow(wide(col == (row >> 2) * ROWS + (row & (CAP - 1))))
-    rows_ref[...] = narrow(jnp.dot(pick, blocks, preferred_element_type=jnp.float32))
-    row, col = iota((Y * Z, count), 0), iota((Y * Z, count), 1)
-    part = col - row * ROWS
-    pick = narrow(wide((part >= CAP) & (part < CAP + PARTS)))
-    text_ref[...] = jnp.dot(pick, blocks, preferred_element_type=jnp.float32)
-
-
-def unpack(blocks):
-    width = blocks.shape[1]
-    return pl.pallas_call(
-        unpack_kernel,
-        out_shape=(
-            jax.ShapeDtypeStruct((SLOTS, width), jnp.bfloat16),
-            jax.ShapeDtypeStruct((Y * Z, width), jnp.float32),
-        ),
-        in_specs=[VMEM],
-        out_specs=(VMEM, VMEM),
-        name="unpack",
-    )(blocks)
+    )(*inputs)
 
 
 def combine_kernel(returned_ref, target_ref, gate_ref, tokens_ref, out_ref, pooled_ref):
@@ -159,7 +143,7 @@
         for ref, step, first in zip(images[side], (0, 3, 1, 2, 2), (0, 0, 0, 0, half)):
             put(image_scr, place_x + step, c, first, full_rows(ref))
         for ref, step in zip(texts[side], (0, 3, 2, 1)):
-            put(text_scr, place_x + step, c, 0, ref[...])
+            put(text_scr, place_x + step, c, 0, full_rows(ref))
     image_unit = image_scr[...]
     text_unit = text_scr[...]
     logits = scale * lax.dot_general(
@@ -193,12 +177,14 @@
         radius = jnp.sqrt(jnp.sum(rows * rows, axis=-1, keepdims=True) + 1e-06)
         return rows / radius, radius
 
-    pieces = WIDTH // LANES
-    own_image = jnp.concatenate(
-        [images[0][0][pl.ds(expert * pieces + i, 1), :] for i in range(pieces)], axis=1
-    )
-    image_ref[...] = back(*own(own_image), d_image)
-    dtext_ref[...] = back(*own(texts[0][0][pl.ds(expert, 1), :]), d_text)
+    def own_row(ref):
+        pieces = WIDTH // LANES
+        return jnp.concatenate(
+            [ref[pl.ds(expert * pieces + i, 1), :] for i in range(pieces)], axis=1
+        )
+
+    image_ref[...] = back(*own(own_row(images[0][0])), d_image)
+    dtext_ref[...] = back(*own(own_row(texts[0][0])), d_text)
 
 
 def contrast(places, scale, images, other_images, texts, other_texts):
@@ -265,6 +251,26 @@
     return "dp", [(i, i ^ 1) for i in range(X * CORES)]
 
 
+def along_y(step):
+    return "expert", [(y * Z + z, (y + step) % Y * Z + z) for y in range(Y) for z in range(Z)]
+
+
+def flip_z(bit):
+    return "expert", [(e, e ^ bit) for e in range(Y * Z)]
+
+
+def in_order(block, other, place, bit):
+    first = (place & bit) == 0
+    return jnp.concatenate([jnp.where(first, block, other), jnp.where(first, other, block)])
+
+
+def in_order_y(got, place):
+    order = [got[-k % Y] for k in range(Y)]
+    rows = got[0].shape[0]
+    start = (Y - place) % Y * rows
+    return lax.dynamic_slice_in_dim(jnp.concatenate(order + order), start, Y * rows)
+
+
 def to_experts(blocks):
     return lax.all_to_all(blocks, "expert", split_axis=0, concat_axis=0, tiled=True)
 
@@ -277,6 +283,17 @@
     dp_place = lax.axis_index("dp")
     places = jnp.stack([dp_place // CORES, dp_place % CORES, lax.axis_index("expert")])
 
+    expert_place = lax.axis_index("expert")
+    place_y, place_z = expert_place // Z, expert_place % Z
+
+    text = text_emb.reshape(1, 1, width)
+    other = lax.ppermute(text, *flip_z(1))
+
+    outgoing, target = dispatch(
+        tokens, norm_gain.reshape(width // LANES, LANES), expert_ids.reshape(1, rows), priority
+    )
+    outgoing, w_in, w_out = lax.optimization_barrier((outgoing, w_in, w_out))
+
     weights = (
         w_in[0],
         lax.ppermute(w_in[0], *along_core()),
@@ -284,28 +301,27 @@
         lax.ppermute(w_out[0], *along_core()),
     )
 
-    outgoing, target = dispatch(
-        tokens,
-        norm_gain.reshape(width // LANES, LANES),
-        expert_ids.reshape(1, rows),
-        priority,
-        text_emb,
-    )
-    incoming = to_experts(outgoing.reshape(Y * Z, ROWS, width))
-    own_rows, text_block = unpack(incoming.reshape(Y * Z * ROWS, width))
+    own_rows = to_experts(outgoing.reshape(Y * Z, CAP, width)).reshape(SLOTS, width)
+    other, own_rows = lax.optimization_barrier((other, own_rows))
+    text = in_order(text, other, place_z, 1)
 
     left_rows = lax.ppermute(own_rows, *along_x(1))
     right_rows = lax.ppermute(own_rows, *along_x(-1))
     own_part = expert_rows(own_rows, *weights)
-    left_rows, right_rows, own_part = lax.optimization_barrier((left_rows, right_rows, own_part))
+    other = lax.ppermute(text, *flip_z(2))
+    left_rows, right_rows, own_part, other = lax.optimization_barrier(
+        (left_rows, right_rows, own_part, other)
+    )
     far_rows = jnp.concatenate(
         [
             lax.ppermute(left_rows[:half], *along_x(1)),
             lax.ppermute(right_rows[half:], *along_x(-1)),
         ]
     )
+    text = in_order(text, other, place_z, 2)
+    other = lax.ppermute(text, *flip_z(4))
     side_part = expert_rows(jnp.concatenate([left_rows, right_rows]), *weights)
-    far_rows, side_part = lax.optimization_barrier((far_rows, side_part))
+    far_rows, side_part, other = lax.optimization_barrier((far_rows, side_part, other))
     far_part = narrow(expert_rows(far_rows, *weights))
 
     from_right = lax.ppermute(far_part[:half], *along_x(-1))
@@ -314,17 +330,24 @@
     right_sum = jnp.concatenate(
         [side_part[SLOTS : SLOTS + half], side_part[SLOTS + half :] + wide(from_left)]
     )
-    left_sum = lax.ppermute(narrow(left_sum), *along_x(-1))
-    right_sum = lax.ppermute(narrow(right_sum), *along_x(1))
+    left_sum, right_sum, other = lax.optimization_barrier(
+        (narrow(left_sum), narrow(right_sum), other)
+    )
+    left_sum = lax.ppermute(left_sum, *along_x(-1))
+    right_sum = lax.ppermute(right_sum, *along_x(1))
+    text = in_order(text, other, place_z, 4)
+    others = [lax.ppermute(text, *along_y(d)) for d in range(1, Y)]
+    left_sum, right_sum, *others = lax.optimization_barrier([left_sum, right_sum] + others)
     result = narrow(own_part + wide(left_sum) + wide(right_sum))
-
-    text_block, result = lax.optimization_barrier((text_block, result))
-    texts = [text_block] + [lax.ppermute(text_block, *along_x(d)) for d in range(1, X)]
+    text = in_order_y([text] + others, place_y)
+
     returned = to_experts(result.reshape(Y * Z, CAP, width)).reshape(SLOTS, width)
-    texts, returned = lax.optimization_barrier((texts, returned))
     moe_out, pooled = combine(returned, target, gate_prob.reshape(1, rows), tokens)
 
+    text, pooled = lax.optimization_barrier((text.reshape(pooled.shape), pooled))
+    texts = [text] + [lax.ppermute(text, *along_x(d)) for d in range(1, X)]
     near = to_experts(pooled.reshape(Y * Z, 1, width)).reshape(pooled.shape)
+    texts, near = lax.optimization_barrier((texts, near))
     half = near.shape[0] // 2
     left = lax.ppermute(near, *along_x(1))
     right = lax.ppermute(near, *along_x(-1))

time: 137 us -> 135 us (0.985)
  blocking collectives: 42.8 us -> 0 us
  starting transfers between devices: 45.5 us -> 71.8 us
  waiting for transfers between devices: 20.2 us -> 34.9 us
    all_to_all x2 -> x0, blocking collectives: 42.8 us -> none  [to_experts(): lax.all_to_all(blocks, 'expert', split_axis=0, concat_axis=0, tiled=True)]
    all_to_all x1 -> x3, waiting for transfers between devices: 5.86 us -> 19.8 us  [to_experts(): lax.all_to_all(blocks, 'expert', split_axis=0, concat_axis=0, tiled=True)]
    all_to_all x1 -> x3, starting transfers between devices: 9.04 us -> 20.9 us  [to_experts(): lax.all_to_all(blocks, 'expert', split_axis=0, concat_axis=0, tiled=True)]
    ppermute x5 -> x11, starting transfers between devices: 7.04 us -> 15.5 us  [the longest x1 4.07 us: on_device(): other = lax.ppermute(text, *flip_z(2))]
    ppermute x5 -> x11, waiting for transfers between devices: 5.89 us -> 11.2 us  [the longest x3 6.65 us: on_device(): texts = [text] + [lax.ppermute(text, *along_x(d)) for d in range(1, X)]]
    ppermute x9, starting transfers between devices: 14 us -> 19.2 us  [on_device(): lax.ppermute(block, *along_core())]
    unnamed x22 -> x8, local copies, waits for them, and re-layouts: 6.25 us -> 2.41 us
    reshape x0 -> x3, local copies, waits for them, and re-layouts: none -> 3.57 us  [the longest x1 1.79 us: on_device(): outgoing.reshape(Y * Z, CAP, width)]
  transfers between devices with their start and end apart: 27 -> 35, of which waited for: 9 -> 13; matrix products, arithmetic and copies ran while one was open for 1% -> 3% of each run, Pallas kernels for 7% -> 5%
where the time goes in v3:
time: 135 us; the launch traced here: 134 us
  starting transfers between devices  71.8 us (53%)
  waiting for transfers between devices  34.9 us (26%)
  Pallas kernels  17.7 us (13%)
  local copies, waits for them, and re-layouts  7.76 us (6%)
  between operations  1.64 us (1%)
    all_to_all x3, starting transfers between devices, to_experts(): lax.all_to_all(blocks, 'expert', split_axis=0, concat_axis=0, tiled=True)  20.9 us
    all_to_all x3, waiting for transfers between devices, to_experts(): lax.all_to_all(blocks, 'expert', split_axis=0, concat_axis=0, tiled=True)  19.8 us
    ppermute x9, starting transfers between devices, on_device(): lax.ppermute(block, *along_core())  19.2 us
    pallas_call x3, Pallas kernels, expert_rows(): pl.pallas_call(expert_kernel, out_shape=jax.ShapeDtypeStruct((count, widt...  9.1 us
    ppermute x3, waiting for transfers between devices, on_device(): texts = [text] + [lax.ppermute(text, *along_x(d)) for d in range(1, X)]  6.65 us
    ppermute x1, starting transfers between devices, on_device(): other = lax.ppermute(text, *flip_z(2))  4.07 us
    pallas_call x1, Pallas kernels, contrast(): pl.pallas_call(contrast_kernel, out_shape=(jax.ShapeDtypeStruct((1, 1), j...  3.6 us
    ppermute x3, waiting for transfers between devices, on_device(): others = [lax.ppermute(text, *along_y(d)) for d in range(1, Y)]  3.33 us
  transfers between devices with their start and end apart: 35, of which 13 were waited for; matrix products, arithmetic and copies ran while one was open for 3% of the time, Pallas kernels for 5%

profile of v3, /device:TPU:1, one launch (start us, length us, event | category | flops | bytes accessed | tf_op | source)
XLA Modules:
  0.0 134.3 jit_solution(15707684366685256555)
XLA Ops:
  0.6 2.5 %dispatch.1 = (bf16[128,1280]{1,0:T(8,128)(2,1)}, s32[1,256]{1,0:T(1,128)}) custom-call(bf16[256,1280]{1,0:T(8,128)(2,1)} %tokens_ref.1, f32[10,128]{1,0:T(8,128)} %bitcast.29, s32[1,256]{1,0:T(1,128)} %bitcast.31, s32[1,256]{1,0:T(1,128)} %ranks_hbm.1), custom_call_target="tpu_custom_call" | custom-call | tf_op jit(solution)/shard_map/dispatch/pallas_call | solution.py:75
  3.1 3.3 %collective-permute-start.3 = (bf16[1280,640]{1,0:T(8,128)(2,1)}, bf16[1280,640]{1,0:T(8,128)(2,1)S(1)}, u32[]{:S(2)}, u32[]{:S(2)}) collective-permute-start(bf16[1280,640]{1,0:T(8,128)(2,1)} %bitcast.16), channel_id=1, source_target_pairs={{0,32},{32,0},{64,96},{96,64},{128,160},{160,128},{192,224},{224,1... | collective-permute-start | bytes 4915208 | tf_op jit(solution)/shard_map/ppermute | solution.py:299
  8.4 9.6 %all-to-all-start = ((bf16[32,4,1280]{2,1,0:T(4,128)(2,1)}), bf16[32,4,1280]{2,1,0:T(4,128)(2,1)}, u32[]{:S(2)}, u32[]{:S(2)}) async-start(bf16[32,4,1280]{2,1,0:T(4,128)(2,1)} %reshape.47), calls=%async_computation | async-start | bytes 655360 | tf_op jit(solution)/shard_map/all_to_all | solution.py:275
  19.2 9.2 %all-to-all-done = bf16[32,4,1280]{2,1,0:T(4,128)(2,1)} async-done(((bf16[32,4,1280]{2,1,0:T(4,128)(2,1)}), bf16[32,4,1280]{2,1,0:T(4,128)(2,1)}, u32[]{:S(2)}, u32[]{:S(2)}) %all-to-all-start) | async-done | bytes 327712 | tf_op jit(solution)/shard_map/all_to_all | solution.py:275
  30.1 2.5 %collective-permute-start.2 = (bf16[128,1280]{1,0:T(8,128)(2,1)}, bf16[128,1280]{1,0:T(8,128)(2,1)S(1)}, u32[]{:S(2)}, u32[]{:S(2)}) collective-permute-start(bf16[128,1280]{1,0:T(8,128)(2,1)} %reshape.48.rows_ref), channel_id=1, source_target_pairs={{0,192},{32,224},{64,0},{96,32},{128,64},{160,96},{192,128},{224,1... | collective-permute-start | bytes 983048 | tf_op jit(solution)/shard_map/ppermute | solution.py:309
  32.7 4.1 %collective-permute-start.5 = (f32[2,1,1280]{2,0,1:T(2,128)S(1)}, f32[2,1,1280]{2,0,1:T(2,128)S(1)}, u32[]{:S(2)}, u32[]{:S(2)}) collective-permute-start(f32[2,1,1280]{2,0,1:T(2,128)S(1)} %pad_maximum_fusion.6), channel_id=1, source_target_pairs={{0,2},{1,3},{2,0},{3,1},{4,6},{5,7},{6,4},{7,5},{8,10},{9,11},{10,... | collective-permute-start | bytes 30728 | tf_op jit(solution)/shard_map/ppermute | solution.py:311
  39.2 2.7 %expert.3 = f32[128,1280]{1,0:T(8,128)S(1)} custom-call(bf16[128,1280]{1,0:T(8,128)(2,1)S(1)} %copy-done.2, bf16[1280,640]{1,0:T(8,128)(2,1)S(1)} %bitcast.17, bf16[1280,640]{1,0:T(8,128)(2,1)S(1)} %collective-permute-done.3.in_other, bf16[640,1280]{1,0:T(8,128)(2,1)S(1)} %bitcast.21, bf16[640,1280]{1,0:T(8,128)(2,1)} %collective-permute-done.4.out_other), custom_call_target="tpu_custom_call" | custom-call | flops 838860800 | bytes 7536640 | tf_op jit(solution)/shard_map/expert/pallas_call | solution.py:230
  42.0 2.8 %collective-permute-start.7 = (bf16[64,1280]{1,0:T(8,128)(2,1)S(1)}, bf16[64,1280]{1,0:T(8,128)(2,1)S(1)}, u32[]{:S(2)}, u32[]{:S(2)}) collective-permute-start(bf16[64,1280]{1,0:T(8,128)(2,1)S(1)} %slice.33), channel_id=1, source_target_pairs={{0,192},{32,224},{64,0},{96,32},{128,64},{160,96},{192,128},{224,1... | collective-permute-start | bytes 491528 | tf_op jit(solution)/shard_map/ppermute | solution.py:318
  44.8 2.5 %collective-permute-start.8 = (f32[4,1,1280]{2,0,1:T(4,128)S(1)}, f32[4,1,1280]{2,0,1:T(4,128)S(1)}, u32[]{:S(2)}, u32[]{:S(2)}) collective-permute-start(f32[4,1,1280]{2,0,1:T(4,128)S(1)} %pad_maximum_fusion.5), channel_id=1, source_target_pairs={{0,4},{1,5},{2,6},{3,7},{4,0},{5,1},{6,2},{7,3},{8,12},{9,13},{10,... | collective-permute-start | bytes 61448 | tf_op jit(solution)/shard_map/ppermute | solution.py:322
  47.3 3.7 %expert.4 = f32[256,1280]{1,0:T(8,128)S(1)} custom-call(bf16[256,1280]{1,0:T(8,128)(2,1)S(1)} %pad_maximum_fusion.rows_ref, bf16[1280,640]{1,0:T(8,128)(2,1)S(1)} %bitcast.18, bf16[1280,640]{1,0:T(8,128)(2,1)S(1)} %collective-permute-done.3.in_other, bf16[640,1280]{1,0:T(8,128)(2,1)S(1)} %bitcast.22, bf16[640,1280]{1,0:T(8,128)(2,1)} %collective-permute-done.4.out_other), custom_call_target="tpu_custom_call" | custom-call | flops 1677721600 | bytes 8519680 | tf_op jit(solution)/shard_map/expert/pallas_call | solution.py:230
  51.4 2.7 %expert.5 = f32[128,1280]{1,0:T(8,128)S(1)} custom-call(bf16[128,1280]{1,0:T(8,128)(2,1)S(1)} %pad_maximum_fusion.1.rows_ref, bf16[1280,640]{1,0:T(8,128)(2,1)S(1)} %bitcast.19, bf16[1280,640]{1,0:T(8,128)(2,1)S(1)} %collective-permute-done.3.in_other, bf16[640,1280]{1,0:T(8,128)(2,1)S(1)} %bitcast.23, bf16[640,1280]{1,0:T(8,128)(2,1)} %collective-permute-done.4.out_other), custom_call_target="tpu_custom_call" | custom-call | flops 838860800 | bytes 7536640 | tf_op jit(solution)/shard_map/expert/pallas_call | solution.py:230
  54.3 2.9 %collective-permute-start.9 = (bf16[64,1280]{1,0:T(8,128)(2,1)S(1)}, bf16[64,1280]{1,0:T(8,128)(2,1)S(1)}, u32[]{:S(2)}, u32[]{:S(2)}) collective-permute-start(bf16[64,1280]{1,0:T(8,128)(2,1)S(1)} %get-tuple-element.77), channel_id=1, source_target_pairs={{0,192},{32,224},{64,0},{96,32},{128,64},{160,96},{192,128},{224,1... | collective-permute-start | bytes 491528 | tf_op jit(solution)/shard_map/ppermute | solution.py:327
  59.8 3.0 %collective-permute-start.11 = (bf16[128,1280]{1,0:T(8,128)(2,1)S(1)}, bf16[128,1280]{1,0:T(8,128)(2,1)S(1)}, u32[]{:S(2)}, u32[]{:S(2)}) collective-permute-start(bf16[128,1280]{1,0:T(8,128)(2,1)S(1)} %get-tuple-element.51), channel_id=1, source_target_pairs={{0,192},{32,224},{64,0},{96,32},{128,64},{160,96},{192,128},{224,1... | collective-permute-start | bytes 983048 | tf_op jit(solution)/shard_map/ppermute | solution.py:336
  65.8 2.4 %collective-permute-done.14 = f32[8,1,1280]{2,0,1:T(8,128)S(1)} collective-permute-done((f32[8,1,1280]{2,0,1:T(8,128)S(1)}, f32[8,1,1280]{2,0,1:T(8,128)S(1)}, u32[]{:S(2)}, u32[]{:S(2)}) %collective-permute-start.14) | collective-permute-done | bytes 40992 | tf_op jit(solution)/shard_map/ppermute | solution.py:339
  70.8 6.5 %all-to-all-start.1 = ((bf16[32,4,1280]{2,1,0:T(4,128)(2,1)}), bf16[32,4,1280]{2,1,0:T(4,128)(2,1)S(1)}, u32[]{:S(2)}, u32[]{:S(2)}) async-start(bf16[32,4,1280]{2,1,0:T(4,128)(2,1)} %reshape.49), calls=%async_computation.1 | async-start | bytes 655360 | tf_op jit(solution)/shard_map/all_to_all | solution.py:275
  77.5 9.8 %all-to-all-done.1 = bf16[32,4,1280]{2,1,0:T(4,128)(2,1)S(1)} async-done(((bf16[32,4,1280]{2,1,0:T(4,128)(2,1)}), bf16[32,4,1280]{2,1,0:T(4,128)(2,1)S(1)}, u32[]{:S(2)}, u32[]{:S(2)}) %all-to-all-start.1) | async-done | bytes 327712 | tf_op jit(solution)/shard_map/all_to_all | solution.py:275
  88.0 2.6 %combine.1 = (bf16[256,1280]{1,0:T(8,128)(2,1)}, f32[320,128]{1,0:T(8,128)}) custom-call(bf16[128,1280]{1,0:T(8,128)(2,1)} %reshape.50.returned_ref, s32[1,256]{1,0:T(1,128)} %get-tuple-element.56.target_ref, f32[1,256]{1,0:T(1,128)} %bitcast.32, bf16[256,1280]{1,0:T(8,128)(2,1)} %tokens_ref.1), custom_call_target="tpu_custom_call" | custom-call | tf_op jit(solution)/shard_map/combine/pallas_call | solution.py:108
  90.6 4.8 %all-to-all-start.2 = ((f32[32,1,1280]{2,1,0:T(1,128)}), f32[32,1,1280]{2,1,0:T(1,128)S(1)}, u32[]{:S(2)}, u32[]{:S(2)}) async-start(f32[32,1,1280]{2,1,0:T(1,128)} %bitcast.28), calls=%async_computation.2 | async-start | bytes 327680 | tf_op jit(solution)/shard_map/all_to_all | solution.py:275
  97.2 2.5 %collective-permute-done.18.refs_13_ = f32[320,128]{1,0:T(8,128)S(1)} collective-permute-done((f32[320,128]{1,0:T(8,128)S(1)}, f32[320,128]{1,0:T(8,128)S(1)}, u32[]{:S(2)}, u32[]{:S(2)}) %collective-permute-start.18) | collective-permute-done | bytes 163872 | tf_op jit(solution)/shard_map/ppermute | solution.py:348
  99.7 2.6 %collective-permute-done.17.refs_12_ = f32[320,128]{1,0:T(8,128)S(1)} collective-permute-done((f32[320,128]{1,0:T(8,128)S(1)}, f32[320,128]{1,0:T(8,128)S(1)}, u32[]{:S(2)}, u32[]{:S(2)}) %collective-permute-start.17) | collective-permute-done | bytes 163872 | tf_op jit(solution)/shard_map/ppermute | solution.py:348
  106.1 11.1 %collective-permute-start.28 = (f32[320,128]{1,0:T(8,128)S(1)}, f32[320,128]{1,0:T(8,128)S(1)}, u32[]{:S(2)}, u32[]{:S(2)}) collective-permute-start(f32[320,128]{1,0:T(8,128)S(1)} %reshape.52.refs_10_), channel_id=1, source_target_pairs={{0,32},{32,0},{64,96},{96,64},{128,160},{160,128},{192,224},{224,1... | collective-permute-start | bytes 491528 | tf_op jit(solution)/shard_map/ppermute | solution.py:362
  117.8 2.8 %collective-permute-start.31 = (f32[320,128]{1,0:T(8,128)S(1)}, f32[320,128]{1,0:T(8,128)S(1)}, u32[]{:S(2)}, u32[]{:S(2)}) collective-permute-start(f32[320,128]{1,0:T(8,128)S(1)} %collective-permute-done.18.refs_13_), channel_id=1, source_target_pairs={{0,32},{32,0},{64,96},{96,64},{128,160},{160,128},{192,224},{224,1... | collective-permute-start | bytes 491528 | tf_op jit(solution)/shard_map/ppermute | solution.py:362
  120.6 3.1 %collective-permute-start.22 = (f32[160,128]{1,0:T(8,128)S(1)}, f32[160,128]{1,0:T(8,128)S(1)}, u32[]{:S(2)}, u32[]{:S(2)}) collective-permute-start(f32[160,128]{1,0:T(8,128)S(1)} %slice.47), channel_id=1, source_target_pairs={{0,192},{32,224},{64,0},{96,32},{128,64},{160,96},{192,128},{224,1... | collective-permute-start | bytes 245768 | tf_op jit(solution)/shard_map/ppermute | solution.py:354
  130.7 3.6 %contrast.1 = (f32[1,1]{1,0:T(1,128)}, f32[1,1280]{1,0:T(1,128)}, f32[1,1280]{1,0:T(1,128)}) custom-call(s32[3]{0:T(128)S(1)} %pad_add_fusion.place_ref, f32[1]{0:T(128)S(6)} %copy.14.scale_ref, f32[320,128]{1,0:T(8,128)S(1)} %bitcast.27, f32[320,128]{1,0:T(8,128)S(1)} %collective-permute-done.19.refs_1_, f32[320,128]{1,0:T(8,128)S(1)} %collective-permute-done.20.refs_2_, ...), custom_call_target="tpu_custom_call" | custom-call | tf_op jit(solution)/shard_map/contrast/pallas_call | solution.py:192
  (87 shorter events, 29.7 us)
Async XLA Ops:
  3.1 33.6 %collective-permute-start.3 = (bf16[1280,640]{1,0:T(8,128)(2,1)}, bf16[1280,640]{1,0:T(8,128)(2,1)S(1)}, u32[]{:S(2)}, u32[]{:S(2)}) collective-permute-start(bf16[1280,640]{1,0:T(8,128)(2,1)} %bitcast.16), channel_id=1, source_target_pairs={{0,32},{32,0},{64,96},{96,64},{128,160},{160,128},{192,224},{224,1... | collective-permute-start | bytes 4915208 | tf_op jit(solution)/shard_map/ppermute | solution.py:299
  6.5 30.3 %collective-permute-start.4 = (bf16[640,1280]{1,0:T(8,128)(2,1)}, bf16[640,1280]{1,0:T(8,128)(2,1)}, u32[]{:S(2)}, u32[]{:S(2)}) collective-permute-start(bf16[640,1280]{1,0:T(8,128)(2,1)} %bitcast.20), channel_id=1, source_target_pairs={{0,32},{32,0},{64,96},{96,64},{128,160},{160,128},{192,224},{224,1... | collective-permute-start | bytes 4915208 | tf_op jit(solution)/shard_map/ppermute | solution.py:301
  8.4 20.0 %all-to-all-start = ((bf16[32,4,1280]{2,1,0:T(4,128)(2,1)}), bf16[32,4,1280]{2,1,0:T(4,128)(2,1)}, u32[]{:S(2)}, u32[]{:S(2)}) async-start(bf16[32,4,1280]{2,1,0:T(4,128)(2,1)} %reshape.47), calls=%async_computation | async-start | bytes 655360 | tf_op jit(solution)/shard_map/all_to_all | solution.py:275
  18.0 12.2 %collective-permute-start = (f32[1,1,1280]{2,0,1:T(1,128)}, f32[1,1,1280]{2,0,1:T(1,128)S(1)}, u32[]{:S(2)}, u32[]{:S(2)}) collective-permute-start(f32[1,1,1280]{2,0,1:T(1,128)} %bitcast.30), channel_id=1, source_target_pairs={{0,1},{1,0},{2,3},{3,2},{4,5},{5,4},{6,7},{7,6},{8,9},{9,8},{10,11... | collective-permute-start | bytes 15368 | tf_op jit(solution)/shard_map/ppermute | solution.py:290
  30.1 11.7 %collective-permute-start.2 = (bf16[128,1280]{1,0:T(8,128)(2,1)}, bf16[128,1280]{1,0:T(8,128)(2,1)S(1)}, u32[]{:S(2)}, u32[]{:S(2)}) collective-permute-start(bf16[128,1280]{1,0:T(8,128)(2,1)} %reshape.48.rows_ref), channel_id=1, source_target_pairs={{0,192},{32,224},{64,0},{96,32},{128,64},{160,96},{192,128},{224,1... | collective-permute-start | bytes 983048 | tf_op jit(solution)/shard_map/ppermute | solution.py:309
  32.6 9.3 %collective-permute-start.1 = (bf16[128,1280]{1,0:T(8,128)(2,1)}, bf16[128,1280]{1,0:T(8,128)(2,1)S(1)}, u32[]{:S(2)}, u32[]{:S(2)}) collective-permute-start(bf16[128,1280]{1,0:T(8,128)(2,1)} %reshape.48.rows_ref), channel_id=1, source_target_pairs={{0,64},{32,96},{64,128},{96,160},{128,192},{160,224},{192,0},{224,... | collective-permute-start | bytes 983048 | tf_op jit(solution)/shard_map/ppermute | solution.py:308
  32.7 9.2 %collective-permute-start.5 = (f32[2,1,1280]{2,0,1:T(2,128)S(1)}, f32[2,1,1280]{2,0,1:T(2,128)S(1)}, u32[]{:S(2)}, u32[]{:S(2)}) collective-permute-start(f32[2,1,1280]{2,0,1:T(2,128)S(1)} %pad_maximum_fusion.6), channel_id=1, source_target_pairs={{0,2},{1,3},{2,0},{3,1},{4,6},{5,7},{6,4},{7,5},{8,10},{9,11},{10,... | collective-permute-start | bytes 30728 | tf_op jit(solution)/shard_map/ppermute | solution.py:311
  42.0 9.0 %collective-permute-start.7 = (bf16[64,1280]{1,0:T(8,128)(2,1)S(1)}, bf16[64,1280]{1,0:T(8,128)(2,1)S(1)}, u32[]{:S(2)}, u32[]{:S(2)}) collective-permute-start(bf16[64,1280]{1,0:T(8,128)(2,1)S(1)} %slice.33), channel_id=1, source_target_pairs={{0,192},{32,224},{64,0},{96,32},{128,64},{160,96},{192,128},{224,1... | collective-permute-start | bytes 491528 | tf_op jit(solution)/shard_map/ppermute | solution.py:318
  44.7 6.2 %collective-permute-start.6 = (bf16[64,1280]{1,0:T(8,128)(2,1)S(1)}, bf16[64,1280]{1,0:T(8,128)(2,1)S(1)}, u32[]{:S(2)}, u32[]{:S(2)}) collective-permute-start(bf16[64,1280]{1,0:T(8,128)(2,1)S(1)} %slice.32), channel_id=1, source_target_pairs={{0,64},{32,96},{64,128},{96,160},{128,192},{160,224},{192,0},{224,... | collective-permute-start | bytes 491528 | tf_op jit(solution)/shard_map/ppermute | solution.py:317
  44.8 6.6 %collective-permute-start.8 = (f32[4,1,1280]{2,0,1:T(4,128)S(1)}, f32[4,1,1280]{2,0,1:T(4,128)S(1)}, u32[]{:S(2)}, u32[]{:S(2)}) collective-permute-start(f32[4,1,1280]{2,0,1:T(4,128)S(1)} %pad_maximum_fusion.5), channel_id=1, source_target_pairs={{0,4},{1,5},{2,6},{3,7},{4,0},{5,1},{6,2},{7,3},{8,12},{9,13},{10,... | collective-permute-start | bytes 61448 | tf_op jit(solution)/shard_map/ppermute | solution.py:322
  59.8 9.3 %collective-permute-start.11 = (bf16[128,1280]{1,0:T(8,128)(2,1)S(1)}, bf16[128,1280]{1,0:T(8,128)(2,1)S(1)}, u32[]{:S(2)}, u32[]{:S(2)}) collective-permute-start(bf16[128,1280]{1,0:T(8,128)(2,1)S(1)} %get-tuple-element.51), channel_id=1, source_target_pairs={{0,192},{32,224},{64,0},{96,32},{128,64},{160,96},{192,128},{224,1... | collective-permute-start | bytes 983048 | tf_op jit(solution)/shard_map/ppermute | solution.py:336
  62.8 7.1 %collective-permute-start.12 = (bf16[128,1280]{1,0:T(8,128)(2,1)S(1)}, bf16[128,1280]{1,0:T(8,128)(2,1)S(1)}, u32[]{:S(2)}, u32[]{:S(2)}) collective-permute-start(bf16[128,1280]{1,0:T(8,128)(2,1)S(1)} %get-tuple-element.52), channel_id=1, source_target_pairs={{0,64},{32,96},{64,128},{96,160},{128,192},{160,224},{192,0},{224,... | collective-permute-start | bytes 983048 | tf_op jit(solution)/shard_map/ppermute | solution.py:337
  70.8 16.4 %all-to-all-start.1 = ((bf16[32,4,1280]{2,1,0:T(4,128)(2,1)}), bf16[32,4,1280]{2,1,0:T(4,128)(2,1)S(1)}, u32[]{:S(2)}, u32[]{:S(2)}) async-start(bf16[32,4,1280]{2,1,0:T(4,128)(2,1)} %reshape.49), calls=%async_computation.1 | async-start | bytes 655360 | tf_op jit(solution)/shard_map/all_to_all | solution.py:275
  90.6 14.1 %all-to-all-start.2 = ((f32[32,1,1280]{2,1,0:T(1,128)}), f32[32,1,1280]{2,1,0:T(1,128)S(1)}, u32[]{:S(2)}, u32[]{:S(2)}) async-start(f32[32,1,1280]{2,1,0:T(1,128)} %bitcast.28), calls=%async_computation.2 | async-start | bytes 327680 | tf_op jit(solution)/shard_map/all_to_all | solution.py:275
  96.5 5.8 %collective-permute-start.17 = (f32[320,128]{1,0:T(8,128)S(1)}, f32[320,128]{1,0:T(8,128)S(1)}, u32[]{:S(2)}, u32[]{:S(2)}) collective-permute-start(f32[320,128]{1,0:T(8,128)S(1)} %reshape.52.refs_10_), channel_id=1, source_target_pairs={{0,128},{32,160},{64,192},{96,224},{128,0},{160,32},{192,64},{224,... | collective-permute-start | bytes 491528 | tf_op jit(solution)/shard_map/ppermute | solution.py:348
  96.5 7.3 %collective-permute-start.16 = (f32[320,128]{1,0:T(8,128)S(1)}, f32[320,128]{1,0:T(8,128)S(1)}, u32[]{:S(2)}, u32[]{:S(2)}) collective-permute-start(f32[320,128]{1,0:T(8,128)S(1)} %reshape.52.refs_10_), channel_id=1, source_target_pairs={{0,64},{32,96},{64,128},{96,160},{128,192},{160,224},{192,0},{224,... | collective-permute-start | bytes 491528 | tf_op jit(solution)/shard_map/ppermute | solution.py:348
  104.7 13.1 %collective-permute-start.20 = (f32[320,128]{1,0:T(8,128)S(1)}, f32[320,128]{1,0:T(8,128)S(1)}, u32[]{:S(2)}, u32[]{:S(2)}) collective-permute-start(f32[320,128]{1,0:T(8,128)S(1)} %bitcast.24), channel_id=1, source_target_pairs={{0,192},{32,224},{64,0},{96,32},{128,64},{160,96},{192,128},{224,1... | collective-permute-start | bytes 491528 | tf_op jit(solution)/shard_map/ppermute | solution.py:353
  105.7 14.9 %collective-permute-start.19 = (f32[320,128]{1,0:T(8,128)S(1)}, f32[320,128]{1,0:T(8,128)S(1)}, u32[]{:S(2)}, u32[]{:S(2)}) collective-permute-start(f32[320,128]{1,0:T(8,128)S(1)} %bitcast.25), channel_id=1, source_target_pairs={{0,64},{32,96},{64,128},{96,160},{128,192},{160,224},{192,0},{224,... | collective-permute-start | bytes 491528 | tf_op jit(solution)/shard_map/ppermute | solution.py:352
  106.1 17.5 %collective-permute-start.28 = (f32[320,128]{1,0:T(8,128)S(1)}, f32[320,128]{1,0:T(8,128)S(1)}, u32[]{:S(2)}, u32[]{:S(2)}) collective-permute-start(f32[320,128]{1,0:T(8,128)S(1)} %reshape.52.refs_10_), channel_id=1, source_target_pairs={{0,32},{32,0},{64,96},{96,64},{128,160},{160,128},{192,224},{224,1... | collective-permute-start | bytes 491528 | tf_op jit(solution)/shard_map/ppermute | solution.py:362
  117.3 6.5 %collective-permute-start.29 = (f32[320,128]{1,0:T(8,128)S(1)}, f32[320,128]{1,0:T(8,128)S(1)}, u32[]{:S(2)}, u32[]{:S(2)}) collective-permute-start(f32[320,128]{1,0:T(8,128)S(1)} %collective-permute-done.16.refs_11_), channel_id=1, source_target_pairs={{0,32},{32,0},{64,96},{96,64},{128,160},{160,128},{192,224},{224,1... | collective-permute-start | bytes 491528 | tf_op jit(solution)/shard_map/ppermute | solution.py:362
  117.3 8.5 %collective-permute-start.30 = (f32[320,128]{1,0:T(8,128)S(1)}, f32[320,128]{1,0:T(8,128)S(1)}, u32[]{:S(2)}, u32[]{:S(2)}) collective-permute-start(f32[320,128]{1,0:T(8,128)S(1)} %collective-permute-done.17.refs_12_), channel_id=1, source_target_pairs={{0,32},{32,0},{64,96},{96,64},{128,160},{160,128},{192,224},{224,1... | collective-permute-start | bytes 491528 | tf_op jit(solution)/shard_map/ppermute | solution.py:362
  117.8 8.0 %collective-permute-start.31 = (f32[320,128]{1,0:T(8,128)S(1)}, f32[320,128]{1,0:T(8,128)S(1)}, u32[]{:S(2)}, u32[]{:S(2)}) collective-permute-start(f32[320,128]{1,0:T(8,128)S(1)} %collective-permute-done.18.refs_13_), channel_id=1, source_target_pairs={{0,32},{32,0},{64,96},{96,64},{128,160},{160,128},{192,224},{224,1... | collective-permute-start | bytes 491528 | tf_op jit(solution)/shard_map/ppermute | solution.py:362
  120.6 6.3 %collective-permute-start.22 = (f32[160,128]{1,0:T(8,128)S(1)}, f32[160,128]{1,0:T(8,128)S(1)}, u32[]{:S(2)}, u32[]{:S(2)}) collective-permute-start(f32[160,128]{1,0:T(8,128)S(1)} %slice.47), channel_id=1, source_target_pairs={{0,192},{32,224},{64,0},{96,32},{128,64},{160,96},{192,128},{224,1... | collective-permute-start | bytes 245768 | tf_op jit(solution)/shard_map/ppermute | solution.py:354
  123.8 6.1 %collective-permute-start.23 = (f32[320,128]{1,0:T(8,128)S(1)}, f32[320,128]{1,0:T(8,128)S(1)}, u32[]{:S(2)}, u32[]{:S(2)}) collective-permute-start(f32[320,128]{1,0:T(8,128)S(1)} %bitcast.26), channel_id=1, source_target_pairs={{0,32},{32,0},{64,96},{96,64},{128,160},{160,128},{192,224},{224,1... | collective-permute-start | bytes 491528 | tf_op jit(solution)/shard_map/ppermute | solution.py:360
  (15 other events, 111.9 us)

commit v4 on v3

--- a/solution.py
+++ b/solution.py
@@ -117,33 +117,37 @@
     )(returned, target, gate, tokens)
 
 
-def full_rows(ref):
+def full_rows(ref, first=0, every=1):
     pieces = WIDTH // LANES
-    count = ref.shape[0] // pieces
+    step = pieces * every
+    count = ref.shape[0] // step
     return jnp.concatenate(
-        [ref[pl.ds(i, count, stride=pieces), :] for i in range(pieces)], axis=1
-    )
-
-
-def contrast_kernel(place_ref, scale_ref, *refs):
+        [ref[pl.ds(first * pieces + i, count, stride=step), :] for i in range(pieces)], axis=1
+    )
+
+
+def contrast_kernel(place_ref, scale_ref, text_ref, *refs):
     images, texts = (refs[:5], refs[5:10]), (refs[10:14], refs[14:18])
     loss_ref, image_ref, dtext_ref, image_scr, text_scr = refs[18:]
     place_x, core, expert = place_ref[0], place_ref[1], place_ref[2]
     me = (place_x * CORES + core) * (Y * Z) + expert
     scale = scale_ref[0]
 
-    def put(scratch, x, c, first, rows):
+    def put(scratch, step, c, first, rows):
         square = jnp.sum(rows * rows, axis=-1, keepdims=True)
-        start = pl.multiple_of((x & (X - 1)) * (CORES * Y * Z) + c * (Y * Z) + first, 8)
+        x = (place_x + step) & (X - 1)
+        start = pl.multiple_of((x * CORES + c) * (Y * Z) + first, 8)
         scratch[pl.ds(start, rows.shape[0]), :] = rows / jnp.sqrt(square + 1e-06)
 
     half = Y * Z // 2
     for side in range(CORES):
         c = core + side - 2 * core * side
         for ref, step, first in zip(images[side], (0, 3, 1, 2, 2), (0, 0, 0, 0, half)):
-            put(image_scr, place_x + step, c, first, full_rows(ref))
-        for ref, step in zip(texts[side], (0, 3, 2, 1)):
-            put(text_scr, place_x + step, c, 0, full_rows(ref))
+            put(image_scr, step, c, first, full_rows(ref))
+    for own_ref, other_ref, step in zip(*texts, (0, 3, 2, 1)):
+        for c in range(CORES):
+            own_rows, other_rows = full_rows(own_ref, c, CORES), full_rows(other_ref, c, CORES)
+            put(text_scr, step, c, 0, jnp.where(core == 1, own_rows, other_rows))
     image_unit = image_scr[...]
     text_unit = text_scr[...]
     logits = scale * lax.dot_general(
@@ -184,20 +188,20 @@
         )
 
     image_ref[...] = back(*own(own_row(images[0][0])), d_image)
-    dtext_ref[...] = back(*own(own_row(texts[0][0])), d_text)
-
-
-def contrast(places, scale, images, other_images, texts, other_texts):
+    dtext_ref[...] = back(*own(text_ref[...]), d_text)
+
+
+def contrast(places, scale, text, images, other_images, texts, other_texts):
     row = jax.ShapeDtypeStruct((1, WIDTH), jnp.float32)
     return pl.pallas_call(
         contrast_kernel,
         out_shape=(jax.ShapeDtypeStruct((1, 1), jnp.float32), row, row),
-        in_specs=[SMEM, SMEM] + [VMEM] * 18,
+        in_specs=[SMEM, SMEM] + [VMEM] * 19,
         out_specs=(VMEM, VMEM, VMEM),
         scratch_shapes=[pltpu.VMEM((PAIRS, WIDTH), jnp.float32)] * 2,
         compiler_params=pltpu.CompilerParams(vmem_limit_bytes=32 * 2**20),
         name="contrast",
-    )(places, scale, *images, *other_images, *texts, *other_texts)
+    )(places, scale, text, *images, *other_images, *texts, *other_texts)
 
 
 def expert_kernel(rows_ref, in_own, in_other, out_own, out_other, out_ref, hidden_scr):
@@ -251,12 +255,31 @@
     return "dp", [(i, i ^ 1) for i in range(X * CORES)]
 
 
-def along_y(step):
-    return "expert", [(y * Z + z, (y + step) % Y * Z + z) for y in range(Y) for z in range(Z)]
-
-
-def flip_z(bit):
-    return "expert", [(e, e ^ bit) for e in range(Y * Z)]
+def text_pairs(move):
+    pairs = []
+    for x in range(X):
+        for y in range(Y):
+            for z in range(Z):
+                to_x, to_y, to_z = move(x, y, z)
+                source = (x * CORES + 1) * Y * Z + y * Z + z
+                pairs.append((source, (to_x * CORES + 1) * Y * Z + to_y * Z + to_z))
+    return ("dp", "expert"), pairs
+
+
+def text_z(bit):
+    return text_pairs(lambda x, y, z: (x, y, z ^ bit))
+
+
+def text_y(step):
+    return text_pairs(lambda x, y, z: (x, (y + step) % Y, z))
+
+
+def text_x(step):
+    return text_pairs(lambda x, y, z: ((x + step) % X, y, z))
+
+
+def to_core(core):
+    return "dp", [(x * CORES + 1 - core, x * CORES + core) for x in range(X)]
 
 
 def in_order(block, other, place, bit):
@@ -287,12 +310,12 @@
     place_y, place_z = expert_place // Z, expert_place % Z
 
     text = text_emb.reshape(1, 1, width)
-    other = lax.ppermute(text, *flip_z(1))
+    text = jnp.concatenate([lax.ppermute(text, *to_core(1)), text])
 
     outgoing, target = dispatch(
         tokens, norm_gain.reshape(width // LANES, LANES), expert_ids.reshape(1, rows), priority
     )
-    outgoing, w_in, w_out = lax.optimization_barrier((outgoing, w_in, w_out))
+    text, outgoing, w_in, w_out = lax.optimization_barrier((text, outgoing, w_in, w_out))
 
     weights = (
         w_in[0],
@@ -302,13 +325,12 @@
     )
 
     own_rows = to_experts(outgoing.reshape(Y * Z, CAP, width)).reshape(SLOTS, width)
-    other, own_rows = lax.optimization_barrier((other, own_rows))
-    text = in_order(text, other, place_z, 1)
+    text, own_rows = lax.optimization_barrier((text, own_rows))
 
     left_rows = lax.ppermute(own_rows, *along_x(1))
     right_rows = lax.ppermute(own_rows, *along_x(-1))
     own_part = expert_rows(own_rows, *weights)
-    other = lax.ppermute(text, *flip_z(2))
+    other = lax.ppermute(text, *text_z(1))
     left_rows, right_rows, own_part, other = lax.optimization_barrier(
         (left_rows, right_rows, own_part, other)
     )
@@ -318,14 +340,17 @@
             lax.ppermute(right_rows[half:], *along_x(-1)),
         ]
     )
-    text = in_order(text, other, place_z, 2)
-    other = lax.ppermute(text, *flip_z(4))
+    text = in_order(text, other, place_z, 1)
+    other = lax.ppermute(text, *text_z(2))
     side_part = expert_rows(jnp.concatenate([left_rows, right_rows]), *weights)
     far_rows, side_part, other = lax.optimization_barrier((far_rows, side_part, other))
     far_part = narrow(expert_rows(far_rows, *weights))
 
     from_right = lax.ppermute(far_part[:half], *along_x(-1))
     from_left = lax.ppermute(far_part[half:], *along_x(1))
+    text = in_order(text, other, place_z, 2)
+    other = lax.ppermute(text, *text_z(4))
+    from_left, from_right, other = lax.optimization_barrier((from_left, from_right, other))
     left_sum = jnp.concatenate([side_part[:half] + wide(from_right), side_part[half:SLOTS]])
     right_sum = jnp.concatenate(
         [side_part[SLOTS : SLOTS + half], side_part[SLOTS + half :] + wide(from_left)]
@@ -336,7 +361,7 @@
     left_sum = lax.ppermute(left_sum, *along_x(-1))
     right_sum = lax.ppermute(right_sum, *along_x(1))
     text = in_order(text, other, place_z, 4)
-    others = [lax.ppermute(text, *along_y(d)) for d in range(1, Y)]
+    others = [lax.ppermute(text, *text_y(d)) for d in range(1, Y)]
     left_sum, right_sum, *others = lax.optimization_barrier([left_sum, right_sum] + others)
     result = narrow(own_part + wide(left_sum) + wide(right_sum))
     text = in_order_y([text] + others, place_y)
@@ -344,8 +369,8 @@
     returned = to_experts(result.reshape(Y * Z, CAP, width)).reshape(SLOTS, width)
     moe_out, pooled = combine(returned, target, gate_prob.reshape(1, rows), tokens)
 
-    text, pooled = lax.optimization_barrier((text.reshape(pooled.shape), pooled))
-    texts = [text] + [lax.ppermute(text, *along_x(d)) for d in range(1, X)]
+    text, pooled = lax.optimization_barrier((text.reshape(-1, LANES), pooled))
+    texts = [text] + [lax.ppermute(text, *text_x(d)) for d in range(1, X)]
     near = to_experts(pooled.reshape(Y * Z, 1, width)).reshape(pooled.shape)
     texts, near = lax.optimization_barrier((texts, near))
     half = near.shape[0] // 2
@@ -356,10 +381,11 @@
     loss, grad_image, grad_text = contrast(
         places,
         logit_scale,
+        text_emb,
         images,
         [lax.ppermute(block, *along_core()) for block in images],
         texts,
-        [lax.ppermute(block, *along_core()) for block in texts],
+        [lax.ppermute(block, *to_core(0)) for block in texts],
     )
     return (moe_out, loss.reshape(1), grad_image, grad_text)
 

time: 135 us -> 162 us (1.20)
  blocking collectives: 0 us -> 34.5 us
  starting transfers between devices: 71.8 us -> 59.4 us
  local copies, waits for them, and re-layouts: 7.76 us -> 14.3 us
  waiting for transfers between devices: 34.9 us -> 29.8 us
  other arithmetic: 0.53 us -> 2.35 us
    all_to_all x0 -> x2, blocking collectives: none -> 34.5 us  [to_experts(): lax.all_to_all(blocks, 'expert', split_axis=0, concat_axis=0, tiled=True)]
    ppermute x9 -> x14, starting transfers between devices: 12.5 us -> 35.3 us  [the longest x3 8.67 us: on_device(): others = [lax.ppermute(text, *text_y(d)) for d in range(1, Y)]]
    ppermute x9 -> x5, starting transfers between devices: 19.2 us -> 0.19 us  [on_device(): lax.ppermute(block, *along_core())]
    all_to_all x3 -> x1, starting transfers between devices: 20.9 us -> 6.51 us  [to_experts(): lax.all_to_all(blocks, 'expert', split_axis=0, concat_axis=0, tiled=True)]
    all_to_all x3 -> x1, waiting for transfers between devices: 19.8 us -> 9.81 us  [to_experts(): lax.all_to_all(blocks, 'expert', split_axis=0, concat_axis=0, tiled=True)]
    unnamed x8 -> x31, local copies, waits for them, and re-layouts: 2.41 us -> 6.99 us
    ppermute x1, starting transfers between devices: 3.02 us -> 0.3 us  [on_device(): left_sum = lax.ppermute(left_sum, *along_x(-1))]
    ppermute x1, waiting for transfers between devices: 0.01 us -> 2.52 us  [on_device(): right = lax.ppermute(near, *along_x(-1))]
  transfers between devices with their start and end apart: 35 -> 34, of which waited for: 13 -> 11; matrix products, arithmetic and copies ran while one was open for 3% -> 2% of each run, Pallas kernels for 5% -> 6%
where the time goes in v4:
time: 162 us; the launch traced here: 160 us
  starting transfers between devices  59.4 us (37%)
  blocking collectives  34.5 us (21%)
  waiting for transfers between devices  29.8 us (18%)
  Pallas kernels  18.1 us (11%)
  local copies, waits for them, and re-layouts  14.3 us (9%)
  other arithmetic  2.35 us (1%)
  between operations  1.93 us (1%)
    all_to_all x2, blocking collectives, to_experts(): lax.all_to_all(blocks, 'expert', split_axis=0, concat_axis=0, tiled=True)  34.5 us
    all_to_all x1, waiting for transfers between devices, to_experts(): lax.all_to_all(blocks, 'expert', split_axis=0, concat_axis=0, tiled=True)  9.81 us
    pallas_call x3, Pallas kernels, expert_rows(): pl.pallas_call(expert_kernel, out_shape=jax.ShapeDtypeStruct((count, widt...  9.11 us
    ppermute x3, starting transfers between devices, on_device(): others = [lax.ppermute(text, *text_y(d)) for d in range(1, Y)]  8.67 us
    ppermute x3, starting transfers between devices, on_device(): texts = [text] + [lax.ppermute(text, *text_x(d)) for d in range(1, X)]  7.93 us
    ppermute x4, starting transfers between devices, on_device(): lax.ppermute(block, *to_core(0))  7.43 us
    unnamed x31, local copies, waits for them, and re-layouts  6.99 us
    all_to_all x1, starting transfers between devices, to_experts(): lax.all_to_all(blocks, 'expert', split_axis=0, concat_axis=0, tiled=True)  6.51 us
  transfers between devices with their start and end apart: 34, of which 11 were waited for; matrix products, arithmetic and copies ran while one was open for 2% of the time, Pallas kernels for 6%

profile of v4, /device:TPU:1, one launch (start us, length us, event | category | flops | bytes accessed | tf_op | source)
XLA Modules:
  0.0 160.4 jit_solution(2265905170085638976)
XLA Ops:
  1.9 2.5 %dispatch.1 = (bf16[128,1280]{1,0:T(8,128)(2,1)}, s32[1,256]{1,0:T(1,128)}) custom-call(bf16[256,1280]{1,0:T(8,128)(2,1)} %tokens_ref.1, f32[10,128]{1,0:T(8,128)} %bitcast.29, s32[1,256]{1,0:T(1,128)} %bitcast.30, s32[1,256]{1,0:T(1,128)} %ranks_hbm.1), custom_call_target="tpu_custom_call" | custom-call | tf_op jit(solution)/shard_map/dispatch/pallas_call | solution.py:75
  11.1 20.5 %all_to_all.15 = bf16[32,4,1280]{2,1,0:T(4,128)(2,1)} all-to-all(bf16[32,4,1280]{2,1,0:T(4,128)(2,1)} %reshape.47), channel_id=1, replica_groups=mesh['dp'=8,'expert'=32] {'expert'}, dimensions={0} | all-to-all | bytes 655360 | tf_op jit(solution)/shard_map/all_to_all | solution.py:298
  33.3 2.5 %collective-permute-start.2 = (bf16[128,1280]{1,0:T(8,128)(2,1)}, bf16[128,1280]{1,0:T(8,128)(2,1)}, u32[]{:S(2)}, u32[]{:S(2)}) collective-permute-start(bf16[128,1280]{1,0:T(8,128)(2,1)} %reshape.48.rows_ref), channel_id=1, source_target_pairs={{0,192},{32,224},{64,0},{96,32},{128,64},{160,96},{192,128},{224,1... | collective-permute-start | bytes 983048 | tf_op jit(solution)/shard_map/ppermute | solution.py:331
  35.8 5.4 %collective-permute-start.5 = (f32[2,1,1280]{2,0,1:T(2,128)S(1)}, f32[2,1,1280]{2,0,1:T(2,128)S(1)}, u32[]{:S(2)}, u32[]{:S(2)}) collective-permute-start(f32[2,1,1280]{2,0,1:T(2,128)S(1)} %pad_maximum_fusion.7), channel_id=1, source_target_pairs={{32,33},{33,32},{34,35},{35,34},{36,37},{37,36},{38,39},{39,38},{4... | collective-permute-start | bytes 30728 | tf_op jit(solution)/shard_map/ppermute | solution.py:333
  43.7 2.7 %expert.3 = f32[128,1280]{1,0:T(8,128)S(1)} custom-call(bf16[128,1280]{1,0:T(8,128)(2,1)S(1)} %copy-done.4, bf16[1280,640]{1,0:T(8,128)(2,1)S(1)} %bitcast.15, bf16[1280,640]{1,0:T(8,128)(2,1)S(1)} %collective-permute-done.3.in_other, bf16[640,1280]{1,0:T(8,128)(2,1)S(1)} %bitcast.19, bf16[640,1280]{1,0:T(8,128)(2,1)} %collective-permute-done.4.out_other), custom_call_target="tpu_custom_call" | custom-call | flops 838860800 | bytes 7536640 | tf_op jit(solution)/shard_map/expert/pallas_call | solution.py:234
  49.6 2.8 %collective-permute-start.7 = (bf16[64,1280]{1,0:T(8,128)(2,1)S(1)}, bf16[64,1280]{1,0:T(8,128)(2,1)S(1)}, u32[]{:S(2)}, u32[]{:S(2)}) collective-permute-start(bf16[64,1280]{1,0:T(8,128)(2,1)S(1)} %slice.33), channel_id=1, source_target_pairs={{0,192},{32,224},{64,0},{96,32},{128,64},{160,96},{192,128},{224,1... | collective-permute-start | bytes 491528 | tf_op jit(solution)/shard_map/ppermute | solution.py:340
  54.7 3.7 %expert.4 = f32[256,1280]{1,0:T(8,128)S(1)} custom-call(bf16[256,1280]{1,0:T(8,128)(2,1)S(1)} %pad_maximum_fusion.rows_ref, bf16[1280,640]{1,0:T(8,128)(2,1)S(1)} %bitcast.16, bf16[1280,640]{1,0:T(8,128)(2,1)S(1)} %collective-permute-done.3.in_other, bf16[640,1280]{1,0:T(8,128)(2,1)S(1)} %bitcast.20, bf16[640,1280]{1,0:T(8,128)(2,1)} %collective-permute-done.4.out_other), custom_call_target="tpu_custom_call" | custom-call | flops 1677721600 | bytes 8519680 | tf_op jit(solution)/shard_map/expert/pallas_call | solution.py:234
  59.4 2.7 %expert.5 = f32[128,1280]{1,0:T(8,128)S(1)} custom-call(bf16[128,1280]{1,0:T(8,128)(2,1)S(1)} %pad_maximum_fusion.1.rows_ref, bf16[1280,640]{1,0:T(8,128)(2,1)S(1)} %bitcast.17, bf16[1280,640]{1,0:T(8,128)(2,1)S(1)} %collective-permute-done.3.in_other, bf16[640,1280]{1,0:T(8,128)(2,1)S(1)} %bitcast.21, bf16[640,1280]{1,0:T(8,128)(2,1)} %collective-permute-done.4.out_other), custom_call_target="tpu_custom_call" | custom-call | flops 838860800 | bytes 7536640 | tf_op jit(solution)/shard_map/expert/pallas_call | solution.py:234
  64.6 2.8 %collective-permute-start.10 = (bf16[64,1280]{1,0:T(8,128)(2,1)S(1)}, bf16[64,1280]{1,0:T(8,128)(2,1)S(1)}, u32[]{:S(2)}, u32[]{:S(2)}) collective-permute-start(bf16[64,1280]{1,0:T(8,128)(2,1)S(1)} %get-tuple-element.88), channel_id=1, source_target_pairs={{0,192},{32,224},{64,0},{96,32},{128,64},{160,96},{192,128},{224,1... | collective-permute-start | bytes 491528 | tf_op jit(solution)/shard_map/ppermute | solution.py:349
  67.4 3.5 %collective-permute-done.11 = f32[8,1,1280]{2,0,1:T(8,128)S(1)} collective-permute-done((f32[8,1,1280]{2,0,1:T(8,128)S(1)}, f32[8,1,1280]{2,0,1:T(8,128)S(1)}, u32[]{:S(2)}, u32[]{:S(2)}) %collective-permute-start.11) | collective-permute-done | bytes 40992 | tf_op jit(solution)/shard_map/ppermute | solution.py:352
  74.6 4.0 %collective-permute-start.16 = (f32[16,1,1280]{2,0,1:T(8,128)S(1)}, f32[16,1,1280]{2,0,1:T(8,128)S(1)}, u32[]{:S(2)}, u32[]{:S(2)}) collective-permute-start(f32[16,1,1280]{2,0,1:T(8,128)S(1)} %pad_maximum_fusion.4), channel_id=1, source_target_pairs={{32,56},{33,57},{34,58},{35,59},{36,60},{37,61},{38,62},{39,63},{4... | collective-permute-start | bytes 245768 | tf_op jit(solution)/shard_map/ppermute | solution.py:364
  78.6 2.4 %collective-permute-start.15 = (f32[16,1,1280]{2,0,1:T(8,128)S(1)}, f32[16,1,1280]{2,0,1:T(8,128)S(1)}, u32[]{:S(2)}, u32[]{:S(2)}) collective-permute-start(f32[16,1,1280]{2,0,1:T(8,128)S(1)} %pad_maximum_fusion.4), channel_id=1, source_target_pairs={{32,48},{33,49},{34,50},{35,51},{36,52},{37,53},{38,54},{39,55},{4... | collective-permute-start | bytes 245768 | tf_op jit(solution)/shard_map/ppermute | solution.py:364
  88.5 6.5 %all-to-all-start.1 = ((bf16[32,4,1280]{2,1,0:T(4,128)(2,1)}), bf16[32,4,1280]{2,1,0:T(4,128)(2,1)S(1)}, u32[]{:S(2)}, u32[]{:S(2)}) async-start(bf16[32,4,1280]{2,1,0:T(4,128)(2,1)} %reshape.49), calls=%async_computation.1 | async-start | bytes 655360 | tf_op jit(solution)/shard_map/all_to_all | solution.py:298
  95.1 9.8 %all-to-all-done.1 = bf16[32,4,1280]{2,1,0:T(4,128)(2,1)S(1)} async-done(((bf16[32,4,1280]{2,1,0:T(4,128)(2,1)}), bf16[32,4,1280]{2,1,0:T(4,128)(2,1)S(1)}, u32[]{:S(2)}, u32[]{:S(2)}) %all-to-all-start.1) | async-done | bytes 327712 | tf_op jit(solution)/shard_map/all_to_all | solution.py:298
  105.8 2.6 %combine.1 = (bf16[256,1280]{1,0:T(8,128)(2,1)}, f32[320,128]{1,0:T(8,128)}) custom-call(bf16[128,1280]{1,0:T(8,128)(2,1)} %reshape.50.returned_ref, s32[1,256]{1,0:T(1,128)} %get-tuple-element.64.target_ref, f32[1,256]{1,0:T(1,128)} %bitcast.31, bf16[256,1280]{1,0:T(8,128)(2,1)} %tokens_ref.1), custom_call_target="tpu_custom_call" | custom-call | tf_op jit(solution)/shard_map/combine/pallas_call | solution.py:108
  108.3 3.5 %collective-permute-start.19 = (f32[640,128]{1,0:T(8,128)S(1)}, f32[640,128]{1,0:T(8,128)S(1)}, u32[]{:S(2)}, u32[]{:S(2)}) collective-permute-start(f32[640,128]{1,0:T(8,128)S(1)} %reshape.52.refs_10_), channel_id=1, source_target_pairs={{32,224},{33,225},{34,226},{35,227},{36,228},{37,229},{38,230},{39... | collective-permute-start | bytes 983048 | tf_op jit(solution)/shard_map/ppermute | solution.py:373
  113.9 2.3 %collective-permute-start.17 = (f32[640,128]{1,0:T(8,128)S(1)}, f32[640,128]{1,0:T(8,128)S(1)}, u32[]{:S(2)}, u32[]{:S(2)}) collective-permute-start(f32[640,128]{1,0:T(8,128)S(1)} %reshape.52.refs_10_), channel_id=1, source_target_pairs={{32,96},{33,97},{34,98},{35,99},{36,100},{37,101},{38,102},{39,103... | collective-permute-start | bytes 983048 | tf_op jit(solution)/shard_map/ppermute | solution.py:373
  116.3 14.1 %all_to_all.16 = f32[32,1,1280]{2,1,0:T(1,128)S(1)} all-to-all(f32[32,1,1280]{2,1,0:T(1,128)} %bitcast.28), channel_id=1, replica_groups=mesh['dp'=8,'expert'=32] {'expert'}, dimensions={0} | all-to-all | bytes 327680 | tf_op jit(solution)/shard_map/all_to_all | solution.py:298
  132.7 2.5 %collective-permute-done.21.refs_2_ = f32[320,128]{1,0:T(8,128)S(1)} collective-permute-done((f32[320,128]{1,0:T(8,128)S(1)}, f32[320,128]{1,0:T(8,128)S(1)}, u32[]{:S(2)}, u32[]{:S(2)}) %collective-permute-start.21) | collective-permute-done | bytes 163872 | tf_op jit(solution)/shard_map/ppermute | solution.py:378
  135.2 2.9 %collective-permute-start.23 = (f32[160,128]{1,0:T(8,128)S(1)}, f32[160,128]{1,0:T(8,128)S(1)}, u32[]{:S(2)}, u32[]{:S(2)}) collective-permute-start(f32[160,128]{1,0:T(8,128)S(1)} %slice.47), channel_id=1, source_target_pairs={{0,192},{32,224},{64,0},{96,32},{128,64},{160,96},{192,128},{224,1... | collective-permute-start | bytes 245768 | tf_op jit(solution)/shard_map/ppermute | solution.py:379
  139.6 3.1 %collective-permute-done.22.refs_3_ = f32[160,128]{1,0:T(8,128)S(1)} collective-permute-done((f32[160,128]{1,0:T(8,128)S(1)}, f32[160,128]{1,0:T(8,128)S(1)}, u32[]{:S(2)}, u32[]{:S(2)}) %collective-permute-start.22) | collective-permute-done | bytes 81952 | tf_op jit(solution)/shard_map/ppermute | solution.py:379
  143.3 2.4 %collective-permute-start.29 = (f32[640,128]{1,0:T(8,128)S(1)}, f32[640,128]{1,0:T(8,128)S(1)}, u32[]{:S(2)}, u32[]{:S(2)}) collective-permute-start(f32[640,128]{1,0:T(8,128)S(1)} %reshape.52.refs_10_), channel_id=1, source_target_pairs={{32,0},{96,64},{160,128},{224,192},{33,1},{97,65},{161,129},{225,1... | collective-permute-start | bytes 983048 | tf_op jit(solution)/shard_map/ppermute | solution.py:388
  147.8 2.4 %collective-permute-start.31 = (f32[640,128]{1,0:T(8,128)S(1)}, f32[640,128]{1,0:T(8,128)S(1)}, u32[]{:S(2)}, u32[]{:S(2)}) collective-permute-start(f32[640,128]{1,0:T(8,128)S(1)} %collective-permute-done.18.refs_12_), channel_id=1, source_target_pairs={{32,0},{96,64},{160,128},{224,192},{33,1},{97,65},{161,129},{225,1... | collective-permute-start | bytes 983048 | tf_op jit(solution)/shard_map/ppermute | solution.py:388
  156.5 4.0 %contrast.1 = (f32[1,1]{1,0:T(1,128)}, f32[1,1280]{1,0:T(1,128)}, f32[1,1280]{1,0:T(1,128)}) custom-call(s32[3]{0:T(128)S(1)} %pad_add_fusion.place_ref, f32[1]{0:T(128)S(6)} %copy.23.scale_ref, f32[1,1280]{1,0:T(1,128)S(1)} %copy-done.11, f32[320,128]{1,0:T(8,128)S(1)} %bitcast.25, f32[320,128]{1,0:T(8,128)S(1)} %collective-permute-done.20.refs_1_, ...), custom_call_target="tpu_custom_call" | custom-call | tf_op jit(solution)/shard_map/contrast/pallas_call | solution.py:196
  (112 shorter events, 47.0 us)
Async XLA Ops:
  6.9 34.3 %collective-permute-start.3 = (bf16[1280,640]{1,0:T(8,128)(2,1)}, bf16[1280,640]{1,0:T(8,128)(2,1)S(1)}, u32[]{:S(2)}, u32[]{:S(2)}) collective-permute-start(bf16[1280,640]{1,0:T(8,128)(2,1)} %bitcast.14), channel_id=1, source_target_pairs={{0,32},{32,0},{64,96},{96,64},{128,160},{160,128},{192,224},{224,1... | collective-permute-start | bytes 4915208 | tf_op jit(solution)/shard_map/ppermute | solution.py:322
  9.2 32.0 %collective-permute-start.4 = (bf16[640,1280]{1,0:T(8,128)(2,1)}, bf16[640,1280]{1,0:T(8,128)(2,1)}, u32[]{:S(2)}, u32[]{:S(2)}) collective-permute-start(bf16[640,1280]{1,0:T(8,128)(2,1)} %bitcast.18), channel_id=1, source_target_pairs={{0,32},{32,0},{64,96},{96,64},{128,160},{160,128},{192,224},{224,1... | collective-permute-start | bytes 4915208 | tf_op jit(solution)/shard_map/ppermute | solution.py:324
  33.3 13.1 %collective-permute-start.2 = (bf16[128,1280]{1,0:T(8,128)(2,1)}, bf16[128,1280]{1,0:T(8,128)(2,1)}, u32[]{:S(2)}, u32[]{:S(2)}) collective-permute-start(bf16[128,1280]{1,0:T(8,128)(2,1)} %reshape.48.rows_ref), channel_id=1, source_target_pairs={{0,192},{32,224},{64,0},{96,32},{128,64},{160,96},{192,128},{224,1... | collective-permute-start | bytes 983048 | tf_op jit(solution)/shard_map/ppermute | solution.py:331
  35.8 10.6 %collective-permute-start.1 = (bf16[128,1280]{1,0:T(8,128)(2,1)}, bf16[128,1280]{1,0:T(8,128)(2,1)}, u32[]{:S(2)}, u32[]{:S(2)}) collective-permute-start(bf16[128,1280]{1,0:T(8,128)(2,1)} %reshape.48.rows_ref), channel_id=1, source_target_pairs={{0,64},{32,96},{64,128},{96,160},{128,192},{160,224},{192,0},{224,... | collective-permute-start | bytes 983048 | tf_op jit(solution)/shard_map/ppermute | solution.py:330
  35.8 10.6 %collective-permute-start.5 = (f32[2,1,1280]{2,0,1:T(2,128)S(1)}, f32[2,1,1280]{2,0,1:T(2,128)S(1)}, u32[]{:S(2)}, u32[]{:S(2)}) collective-permute-start(f32[2,1,1280]{2,0,1:T(2,128)S(1)} %pad_maximum_fusion.7), channel_id=1, source_target_pairs={{32,33},{33,32},{34,35},{35,34},{36,37},{37,36},{38,39},{39,38},{4... | collective-permute-start | bytes 30728 | tf_op jit(solution)/shard_map/ppermute | solution.py:333
  49.6 8.8 %collective-permute-start.7 = (bf16[64,1280]{1,0:T(8,128)(2,1)S(1)}, bf16[64,1280]{1,0:T(8,128)(2,1)S(1)}, u32[]{:S(2)}, u32[]{:S(2)}) collective-permute-start(bf16[64,1280]{1,0:T(8,128)(2,1)S(1)} %slice.33), channel_id=1, source_target_pairs={{0,192},{32,224},{64,0},{96,32},{128,64},{160,96},{192,128},{224,1... | collective-permute-start | bytes 491528 | tf_op jit(solution)/shard_map/ppermute | solution.py:340
  52.3 7.0 %collective-permute-start.6 = (bf16[64,1280]{1,0:T(8,128)(2,1)S(1)}, bf16[64,1280]{1,0:T(8,128)(2,1)S(1)}, u32[]{:S(2)}, u32[]{:S(2)}) collective-permute-start(bf16[64,1280]{1,0:T(8,128)(2,1)S(1)} %slice.32), channel_id=1, source_target_pairs={{0,64},{32,96},{64,128},{96,160},{128,192},{160,224},{192,0},{224,... | collective-permute-start | bytes 491528 | tf_op jit(solution)/shard_map/ppermute | solution.py:339
  52.4 7.0 %collective-permute-start.8 = (f32[4,1,1280]{2,0,1:T(4,128)S(1)}, f32[4,1,1280]{2,0,1:T(4,128)S(1)}, u32[]{:S(2)}, u32[]{:S(2)}) collective-permute-start(f32[4,1,1280]{2,0,1:T(4,128)S(1)} %pad_maximum_fusion.6), channel_id=1, source_target_pairs={{32,34},{33,35},{34,32},{35,33},{36,38},{37,39},{38,36},{39,37},{4... | collective-permute-start | bytes 61448 | tf_op jit(solution)/shard_map/ppermute | solution.py:344
  62.3 8.7 %collective-permute-start.11 = (f32[8,1,1280]{2,0,1:T(8,128)S(1)}, f32[8,1,1280]{2,0,1:T(8,128)S(1)}, u32[]{:S(2)}, u32[]{:S(2)}) collective-permute-start(f32[8,1,1280]{2,0,1:T(8,128)S(1)} %pad_maximum_fusion.5), channel_id=1, source_target_pairs={{32,36},{33,37},{34,38},{35,39},{36,32},{37,33},{38,34},{39,35},{4... | collective-permute-start | bytes 122888 | tf_op jit(solution)/shard_map/ppermute | solution.py:352
  64.6 6.4 %collective-permute-start.10 = (bf16[64,1280]{1,0:T(8,128)(2,1)S(1)}, bf16[64,1280]{1,0:T(8,128)(2,1)S(1)}, u32[]{:S(2)}, u32[]{:S(2)}) collective-permute-start(bf16[64,1280]{1,0:T(8,128)(2,1)S(1)} %get-tuple-element.88), channel_id=1, source_target_pairs={{0,192},{32,224},{64,0},{96,32},{128,64},{160,96},{192,128},{224,1... | collective-permute-start | bytes 491528 | tf_op jit(solution)/shard_map/ppermute | solution.py:349
  72.8 14.7 %collective-permute-start.12 = (bf16[128,1280]{1,0:T(8,128)(2,1)S(1)}, bf16[128,1280]{1,0:T(8,128)(2,1)S(1)}, u32[]{:S(2)}, u32[]{:S(2)}) collective-permute-start(bf16[128,1280]{1,0:T(8,128)(2,1)S(1)} %get-tuple-element.59), channel_id=1, source_target_pairs={{0,192},{32,224},{64,0},{96,32},{128,64},{160,96},{192,128},{224,1... | collective-permute-start | bytes 983048 | tf_op jit(solution)/shard_map/ppermute | solution.py:361
  73.1 14.4 %collective-permute-start.13 = (bf16[128,1280]{1,0:T(8,128)(2,1)S(1)}, bf16[128,1280]{1,0:T(8,128)(2,1)S(1)}, u32[]{:S(2)}, u32[]{:S(2)}) collective-permute-start(bf16[128,1280]{1,0:T(8,128)(2,1)S(1)} %get-tuple-element.60), channel_id=1, source_target_pairs={{0,64},{32,96},{64,128},{96,160},{128,192},{160,224},{192,0},{224,... | collective-permute-start | bytes 983048 | tf_op jit(solution)/shard_map/ppermute | solution.py:362
  74.6 8.7 %collective-permute-start.16 = (f32[16,1,1280]{2,0,1:T(8,128)S(1)}, f32[16,1,1280]{2,0,1:T(8,128)S(1)}, u32[]{:S(2)}, u32[]{:S(2)}) collective-permute-start(f32[16,1,1280]{2,0,1:T(8,128)S(1)} %pad_maximum_fusion.4), channel_id=1, source_target_pairs={{32,56},{33,57},{34,58},{35,59},{36,60},{37,61},{38,62},{39,63},{4... | collective-permute-start | bytes 245768 | tf_op jit(solution)/shard_map/ppermute | solution.py:364
  78.6 6.7 %collective-permute-start.15 = (f32[16,1,1280]{2,0,1:T(8,128)S(1)}, f32[16,1,1280]{2,0,1:T(8,128)S(1)}, u32[]{:S(2)}, u32[]{:S(2)}) collective-permute-start(f32[16,1,1280]{2,0,1:T(8,128)S(1)} %pad_maximum_fusion.4), channel_id=1, source_target_pairs={{32,48},{33,49},{34,50},{35,51},{36,52},{37,53},{38,54},{39,55},{4... | collective-permute-start | bytes 245768 | tf_op jit(solution)/shard_map/ppermute | solution.py:364
  81.1 6.4 %collective-permute-start.14 = (f32[16,1,1280]{2,0,1:T(8,128)S(1)}, f32[16,1,1280]{2,0,1:T(8,128)S(1)}, u32[]{:S(2)}, u32[]{:S(2)}) collective-permute-start(f32[16,1,1280]{2,0,1:T(8,128)S(1)} %pad_maximum_fusion.4), channel_id=1, source_target_pairs={{32,40},{33,41},{34,42},{35,43},{36,44},{37,45},{38,46},{39,47},{4... | collective-permute-start | bytes 245768 | tf_op jit(solution)/shard_map/ppermute | solution.py:364
  88.5 16.4 %all-to-all-start.1 = ((bf16[32,4,1280]{2,1,0:T(4,128)(2,1)}), bf16[32,4,1280]{2,1,0:T(4,128)(2,1)S(1)}, u32[]{:S(2)}, u32[]{:S(2)}) async-start(bf16[32,4,1280]{2,1,0:T(4,128)(2,1)} %reshape.49), calls=%async_computation.1 | async-start | bytes 655360 | tf_op jit(solution)/shard_map/all_to_all | solution.py:298
  108.3 22.0 %collective-permute-start.19 = (f32[640,128]{1,0:T(8,128)S(1)}, f32[640,128]{1,0:T(8,128)S(1)}, u32[]{:S(2)}, u32[]{:S(2)}) collective-permute-start(f32[640,128]{1,0:T(8,128)S(1)} %reshape.52.refs_10_), channel_id=1, source_target_pairs={{32,224},{33,225},{34,226},{35,227},{36,228},{37,229},{38,230},{39... | collective-permute-start | bytes 983048 | tf_op jit(solution)/shard_map/ppermute | solution.py:373
  111.8 18.5 %collective-permute-start.18 = (f32[640,128]{1,0:T(8,128)S(1)}, f32[640,128]{1,0:T(8,128)S(1)}, u32[]{:S(2)}, u32[]{:S(2)}) collective-permute-start(f32[640,128]{1,0:T(8,128)S(1)} %reshape.52.refs_10_), channel_id=1, source_target_pairs={{32,160},{33,161},{34,162},{35,163},{36,164},{37,165},{38,166},{39... | collective-permute-start | bytes 983048 | tf_op jit(solution)/shard_map/ppermute | solution.py:373
  113.9 16.4 %collective-permute-start.17 = (f32[640,128]{1,0:T(8,128)S(1)}, f32[640,128]{1,0:T(8,128)S(1)}, u32[]{:S(2)}, u32[]{:S(2)}) collective-permute-start(f32[640,128]{1,0:T(8,128)S(1)} %reshape.52.refs_10_), channel_id=1, source_target_pairs={{32,96},{33,97},{34,98},{35,99},{36,100},{37,101},{38,102},{39,103... | collective-permute-start | bytes 983048 | tf_op jit(solution)/shard_map/ppermute | solution.py:373
  132.7 14.4 %collective-permute-start.24 = (f32[320,128]{1,0:T(8,128)S(1)}, f32[320,128]{1,0:T(8,128)S(1)}, u32[]{:S(2)}, u32[]{:S(2)}) collective-permute-start(f32[320,128]{1,0:T(8,128)S(1)} %bitcast.24), channel_id=1, source_target_pairs={{0,32},{32,0},{64,96},{96,64},{128,160},{160,128},{192,224},{224,1... | collective-permute-start | bytes 491528 | tf_op jit(solution)/shard_map/ppermute | solution.py:386
  139.6 7.6 %collective-permute-start.28 = (f32[160,128]{1,0:T(8,128)S(1)}, f32[160,128]{1,0:T(8,128)S(1)}, u32[]{:S(2)}, u32[]{:S(2)}) collective-permute-start(f32[160,128]{1,0:T(8,128)S(1)} %collective-permute-done.23.refs_4_), channel_id=1, source_target_pairs={{0,32},{32,0},{64,96},{96,64},{128,160},{160,128},{192,224},{224,1... | collective-permute-start | bytes 245768 | tf_op jit(solution)/shard_map/ppermute | solution.py:386
  142.7 7.5 %collective-permute-start.27 = (f32[160,128]{1,0:T(8,128)S(1)}, f32[160,128]{1,0:T(8,128)S(1)}, u32[]{:S(2)}, u32[]{:S(2)}) collective-permute-start(f32[160,128]{1,0:T(8,128)S(1)} %collective-permute-done.22.refs_3_), channel_id=1, source_target_pairs={{0,32},{32,0},{64,96},{96,64},{128,160},{160,128},{192,224},{224,1... | collective-permute-start | bytes 245768 | tf_op jit(solution)/shard_map/ppermute | solution.py:386
  143.3 10.5 %collective-permute-start.29 = (f32[640,128]{1,0:T(8,128)S(1)}, f32[640,128]{1,0:T(8,128)S(1)}, u32[]{:S(2)}, u32[]{:S(2)}) collective-permute-start(f32[640,128]{1,0:T(8,128)S(1)} %reshape.52.refs_10_), channel_id=1, source_target_pairs={{32,0},{96,64},{160,128},{224,192},{33,1},{97,65},{161,129},{225,1... | collective-permute-start | bytes 983048 | tf_op jit(solution)/shard_map/ppermute | solution.py:388
  145.7 8.1 %collective-permute-start.30 = (f32[640,128]{1,0:T(8,128)S(1)}, f32[640,128]{1,0:T(8,128)S(1)}, u32[]{:S(2)}, u32[]{:S(2)}) collective-permute-start(f32[640,128]{1,0:T(8,128)S(1)} %collective-permute-done.17.refs_11_), channel_id=1, source_target_pairs={{32,0},{96,64},{160,128},{224,192},{33,1},{97,65},{161,129},{225,1... | collective-permute-start | bytes 983048 | tf_op jit(solution)/shard_map/ppermute | solution.py:388
  (22 other events, 175.0 us)

commit v5 on v3

--- a/solution.py
+++ b/solution.py
@@ -87,7 +87,9 @@
     )(*inputs)
 
 
-def combine_kernel(returned_ref, target_ref, gate_ref, tokens_ref, out_ref, pooled_ref):
+def combine_kernel(
+    returned_ref, target_ref, gate_ref, tokens_ref, text_ref, out_ref, pair_ref
+):
     expert_part = lax.dot_general(
         table_of(target_ref[...]),
         returned_ref[...],
@@ -97,53 +99,53 @@
     moe_out = narrow(wide(tokens_ref[...]) + as_column(gate_ref[...]) * expert_part)
     out_ref[...] = moe_out
     pooled = jnp.mean(wide(moe_out), axis=0, keepdims=True)
-    pieces = pooled.shape[1] // LANES
+    pair = jnp.concatenate([pooled, text_ref[...]], axis=1)
+    pieces = pair.shape[1] // LANES
     for index in range(pieces):
-        piece = pooled[:, index * LANES : (index + 1) * LANES]
-        pooled_ref[pl.ds(index, Y * Z, stride=pieces), :] = jnp.broadcast_to(piece, (Y * Z, LANES))
-
-
-def combine(returned, target, gate, tokens):
+        piece = pair[:, index * LANES : (index + 1) * LANES]
+        pair_ref[pl.ds(index, Y * Z, stride=pieces), :] = jnp.broadcast_to(piece, (Y * Z, LANES))
+
+
+def combine(returned, target, gate, tokens, text):
     rows, width = tokens.shape
     return pl.pallas_call(
         combine_kernel,
         out_shape=(
             jax.ShapeDtypeStruct((rows, width), jnp.bfloat16),
-            jax.ShapeDtypeStruct((Y * Z * width // LANES, LANES), jnp.float32),
+            jax.ShapeDtypeStruct((Y * Z * 2 * width // LANES, LANES), jnp.float32),
         ),
-        in_specs=[VMEM] * 4,
+        in_specs=[VMEM] * 5,
         out_specs=(VMEM, VMEM),
         name="combine",
-    )(returned, target, gate, tokens)
-
-
-def full_rows(ref):
+    )(returned, target, gate, tokens, text)
+
+
+def full_rows(ref, which):
     pieces = WIDTH // LANES
-    count = ref.shape[0] // pieces
+    count = ref.shape[0] // (2 * pieces)
     return jnp.concatenate(
-        [ref[pl.ds(i, count, stride=pieces), :] for i in range(pieces)], axis=1
+        [ref[pl.ds(which * pieces + i, count, stride=2 * pieces), :] for i in range(pieces)],
+        axis=1,
     )
 
 
 def contrast_kernel(place_ref, scale_ref, *refs):
-    images, texts = (refs[:5], refs[5:10]), (refs[10:14], refs[14:18])
-    loss_ref, image_ref, dtext_ref, image_scr, text_scr = refs[18:]
+    blocks = (refs[:5], refs[5:10])
+    loss_ref, image_ref, dtext_ref, image_scr, text_scr = refs[10:]
     place_x, core, expert = place_ref[0], place_ref[1], place_ref[2]
     me = (place_x * CORES + core) * (Y * Z) + expert
     scale = scale_ref[0]
 
-    def put(scratch, x, c, first, rows):
-        square = jnp.sum(rows * rows, axis=-1, keepdims=True)
-        start = pl.multiple_of((x & (X - 1)) * (CORES * Y * Z) + c * (Y * Z) + first, 8)
-        scratch[pl.ds(start, rows.shape[0]), :] = rows / jnp.sqrt(square + 1e-06)
-
     half = Y * Z // 2
     for side in range(CORES):
         c = core + side - 2 * core * side
-        for ref, step, first in zip(images[side], (0, 3, 1, 2, 2), (0, 0, 0, 0, half)):
-            put(image_scr, place_x + step, c, first, full_rows(ref))
-        for ref, step in zip(texts[side], (0, 3, 2, 1)):
-            put(text_scr, place_x + step, c, 0, full_rows(ref))
+        for ref, step, first in zip(blocks[side], (0, 3, 1, 2, 2), (0, 0, 0, 0, half)):
+            x = (place_x + step) & (X - 1)
+            start = pl.multiple_of((x * CORES + c) * (Y * Z) + first, 8)
+            for which, scratch in enumerate((image_scr, text_scr)):
+                rows = full_rows(ref, which)
+                square = jnp.sum(rows * rows, axis=-1, keepdims=True)
+                scratch[pl.ds(start, rows.shape[0]), :] = rows / jnp.sqrt(square + 1e-06)
     image_unit = image_scr[...]
     text_unit = text_scr[...]
     logits = scale * lax.dot_general(
@@ -177,27 +179,28 @@
         radius = jnp.sqrt(jnp.sum(rows * rows, axis=-1, keepdims=True) + 1e-06)
         return rows / radius, radius
 
-    def own_row(ref):
+    def own_row(which):
         pieces = WIDTH // LANES
+        first = (2 * expert + which) * pieces
         return jnp.concatenate(
-            [ref[pl.ds(expert * pieces + i, 1), :] for i in range(pieces)], axis=1
+            [blocks[0][0][pl.ds(first + i, 1), :] for i in range(pieces)], axis=1
         )
 
-    image_ref[...] = back(*own(own_row(images[0][0])), d_image)
-    dtext_ref[...] = back(*own(own_row(texts[0][0])), d_text)
-
-
-def contrast(places, scale, images, other_images, texts, other_texts):
+    image_ref[...] = back(*own(own_row(0)), d_image)
+    dtext_ref[...] = back(*own(own_row(1)), d_text)
+
+
+def contrast(places, scale, blocks, other_blocks):
     row = jax.ShapeDtypeStruct((1, WIDTH), jnp.float32)
     return pl.pallas_call(
         contrast_kernel,
         out_shape=(jax.ShapeDtypeStruct((1, 1), jnp.float32), row, row),
-        in_specs=[SMEM, SMEM] + [VMEM] * 18,
+        in_specs=[SMEM, SMEM] + [VMEM] * 10,
         out_specs=(VMEM, VMEM, VMEM),
         scratch_shapes=[pltpu.VMEM((PAIRS, WIDTH), jnp.float32)] * 2,
         compiler_params=pltpu.CompilerParams(vmem_limit_bytes=32 * 2**20),
         name="contrast",
-    )(places, scale, *images, *other_images, *texts, *other_texts)
+    )(places, scale, *blocks, *other_blocks)
 
 
 def expert_kernel(rows_ref, in_own, in_other, out_own, out_other, out_ref, hidden_scr):
@@ -251,26 +254,6 @@
     return "dp", [(i, i ^ 1) for i in range(X * CORES)]
 
 
-def along_y(step):
-    return "expert", [(y * Z + z, (y + step) % Y * Z + z) for y in range(Y) for z in range(Z)]
-
-
-def flip_z(bit):
-    return "expert", [(e, e ^ bit) for e in range(Y * Z)]
-
-
-def in_order(block, other, place, bit):
-    first = (place & bit) == 0
-    return jnp.concatenate([jnp.where(first, block, other), jnp.where(first, other, block)])
-
-
-def in_order_y(got, place):
-    order = [got[-k % Y] for k in range(Y)]
-    rows = got[0].shape[0]
-    start = (Y - place) % Y * rows
-    return lax.dynamic_slice_in_dim(jnp.concatenate(order + order), start, Y * rows)
-
-
 def to_experts(blocks):
     return lax.all_to_all(blocks, "expert", split_axis=0, concat_axis=0, tiled=True)
 
@@ -283,12 +266,6 @@
     dp_place = lax.axis_index("dp")
     places = jnp.stack([dp_place // CORES, dp_place % CORES, lax.axis_index("expert")])
 
-    expert_place = lax.axis_index("expert")
-    place_y, place_z = expert_place // Z, expert_place % Z
-
-    text = text_emb.reshape(1, 1, width)
-    other = lax.ppermute(text, *flip_z(1))
-
     outgoing, target = dispatch(
         tokens, norm_gain.reshape(width // LANES, LANES), expert_ids.reshape(1, rows), priority
     )
@@ -302,26 +279,19 @@
     )
 
     own_rows = to_experts(outgoing.reshape(Y * Z, CAP, width)).reshape(SLOTS, width)
-    other, own_rows = lax.optimization_barrier((other, own_rows))
-    text = in_order(text, other, place_z, 1)
 
     left_rows = lax.ppermute(own_rows, *along_x(1))
     right_rows = lax.ppermute(own_rows, *along_x(-1))
     own_part = expert_rows(own_rows, *weights)
-    other = lax.ppermute(text, *flip_z(2))
-    left_rows, right_rows, own_part, other = lax.optimization_barrier(
-        (left_rows, right_rows, own_part, other)
-    )
+    left_rows, right_rows, own_part = lax.optimization_barrier((left_rows, right_rows, own_part))
     far_rows = jnp.concatenate(
         [
             lax.ppermute(left_rows[:half], *along_x(1)),
             lax.ppermute(right_rows[half:], *along_x(-1)),
         ]
     )
-    text = in_order(text, other, place_z, 2)
-    other = lax.ppermute(text, *flip_z(4))
     side_part = expert_rows(jnp.concatenate([left_rows, right_rows]), *weights)
-    far_rows, side_part, other = lax.optimization_barrier((far_rows, side_part, other))
+    far_rows, side_part = lax.optimization_barrier((far_rows, side_part))
     far_part = narrow(expert_rows(far_rows, *weights))
 
     from_right = lax.ppermute(far_part[:half], *along_x(-1))
@@ -330,36 +300,24 @@
     right_sum = jnp.concatenate(
         [side_part[SLOTS : SLOTS + half], side_part[SLOTS + half :] + wide(from_left)]
     )
-    left_sum, right_sum, other = lax.optimization_barrier(
-        (narrow(left_sum), narrow(right_sum), other)
-    )
-    left_sum = lax.ppermute(left_sum, *along_x(-1))
-    right_sum = lax.ppermute(right_sum, *along_x(1))
-    text = in_order(text, other, place_z, 4)
-    others = [lax.ppermute(text, *along_y(d)) for d in range(1, Y)]
-    left_sum, right_sum, *others = lax.optimization_barrier([left_sum, right_sum] + others)
+    left_sum = lax.ppermute(narrow(left_sum), *along_x(-1))
+    right_sum = lax.ppermute(narrow(right_sum), *along_x(1))
     result = narrow(own_part + wide(left_sum) + wide(right_sum))
-    text = in_order_y([text] + others, place_y)
 
     returned = to_experts(result.reshape(Y * Z, CAP, width)).reshape(SLOTS, width)
-    moe_out, pooled = combine(returned, target, gate_prob.reshape(1, rows), tokens)
-
-    text, pooled = lax.optimization_barrier((text.reshape(pooled.shape), pooled))
-    texts = [text] + [lax.ppermute(text, *along_x(d)) for d in range(1, X)]
-    near = to_experts(pooled.reshape(Y * Z, 1, width)).reshape(pooled.shape)
-    texts, near = lax.optimization_barrier((texts, near))
+    moe_out, pair = combine(returned, target, gate_prob.reshape(1, rows), tokens, text_emb)
+
+    near = to_experts(pair.reshape(Y * Z, 1, 2 * width)).reshape(pair.shape)
     half = near.shape[0] // 2
     left = lax.ppermute(near, *along_x(1))
     right = lax.ppermute(near, *along_x(-1))
     far = [lax.ppermute(left[:half], *along_x(1)), lax.ppermute(right[half:], *along_x(-1))]
-    images = [near, left, right] + far
+    blocks = [near, left, right] + far
     loss, grad_image, grad_text = contrast(
         places,
         logit_scale,
-        images,
-        [lax.ppermute(block, *along_core()) for block in images],
-        texts,
-        [lax.ppermute(block, *along_core()) for block in texts],
+        blocks,
+        [lax.ppermute(block, *along_core()) for block in blocks],
     )
     return (moe_out, loss.reshape(1), grad_image, grad_text)
 

time: 135 us -> 131 us (0.970)
  blocking collectives: 0 us -> 52.5 us
  starting transfers between devices: 71.8 us -> 37.8 us
  waiting for transfers between devices: 34.9 us -> 12.7 us
    all_to_all x0 -> x3, blocking collectives: none -> 52.5 us  [to_experts(): lax.all_to_all(blocks, 'expert', split_axis=0, concat_axis=0, tiled=True)]
    all_to_all x3 -> x0, starting transfers between devices: 20.9 us -> none  [to_experts(): lax.all_to_all(blocks, 'expert', split_axis=0, concat_axis=0, tiled=True)]
    all_to_all x3 -> x0, waiting for transfers between devices: 19.8 us -> none  [to_experts(): lax.all_to_all(blocks, 'expert', split_axis=0, concat_axis=0, tiled=True)]
    ppermute x11 -> x2, starting transfers between devices: 15.5 us -> 3 us  [the longest x1 2.91 us: on_device(): left_sum = lax.ppermute(narrow(left_sum), *along_x(-1))]
    ppermute x11 -> x2, waiting for transfers between devices: 11.2 us -> 5.94 us  [the longest x1 5.94 us: on_device(): right_sum = lax.ppermute(narrow(right_sum), *along_x(1))]
    ppermute x1, waiting for transfers between devices: 0.01 us -> 2.79 us  [on_device(): from_right = lax.ppermute(far_part[:half], *along_x(-1))]
    ppermute x1, starting transfers between devices: 0.99 us -> 2.96 us  [on_device(): right = lax.ppermute(near, *along_x(-1))]
    ppermute x1, starting transfers between devices: 2.93 us -> 1.14 us  [on_device(): from_right = lax.ppermute(far_part[:half], *along_x(-1))]
  transfers between devices with their start and end apart: 35 -> 19, of which waited for: 13 -> 5; matrix products, arithmetic and copies ran while one was open for 3% -> 3% of each run, Pallas kernels for 5% -> 5%
where the time goes in v5:
time: 131 us; the launch traced here: 130 us
  blocking collectives  52.5 us (40%)
  starting transfers between devices  37.8 us (29%)
  Pallas kernels  17.8 us (14%)
  waiting for transfers between devices  12.7 us (10%)
  local copies, waits for them, and re-layouts  6.97 us (5%)
  between operations  1.51 us (1%)
    all_to_all x3, blocking collectives, to_experts(): lax.all_to_all(blocks, 'expert', split_axis=0, concat_axis=0, tiled=True)  52.5 us
    ppermute x5, starting transfers between devices, on_device(): lax.ppermute(block, *along_core())  18.8 us
    pallas_call x3, Pallas kernels, expert_rows(): pl.pallas_call(expert_kernel, out_shape=jax.ShapeDtypeStruct((count, widt...  9.11 us
    ppermute x1, waiting for transfers between devices, on_device(): right_sum = lax.ppermute(narrow(right_sum), *along_x(1))  5.94 us
    pallas_call x1, Pallas kernels, contrast(): pl.pallas_call(contrast_kernel, out_shape=(jax.ShapeDtypeStruct((1, 1), j...  3.59 us
    ppermute x1, starting transfers between devices, on_device(): lax.ppermute(w_in[0], *along_core())  3.33 us
    ppermute x1, starting transfers between devices, on_device(): right = lax.ppermute(near, *along_x(-1))  2.96 us
    ppermute x1, starting transfers between devices, on_device(): lax.ppermute(right[half:], *along_x(-1))  2.93 us
  transfers between devices with their start and end apart: 19, of which 5 were waited for; matrix products, arithmetic and copies ran while one was open for 3% of the time, Pallas kernels for 5%

profile of v5, /device:TPU:1, one launch (start us, length us, event | category | flops | bytes accessed | tf_op | source)
XLA Modules:
  0.0 129.6 jit_solution(4446632096171433101)
XLA Ops:
  0.6 2.5 %dispatch.1 = (bf16[128,1280]{1,0:T(8,128)(2,1)}, s32[1,256]{1,0:T(1,128)}) custom-call(bf16[256,1280]{1,0:T(8,128)(2,1)} %tokens_ref.1, f32[10,128]{1,0:T(8,128)} %bitcast.24, s32[1,256]{1,0:T(1,128)} %bitcast.25, s32[1,256]{1,0:T(1,128)} %ranks_hbm.1), custom_call_target="tpu_custom_call" | custom-call | tf_op jit(solution)/shard_map/dispatch/pallas_call | solution.py:75
  3.1 3.3 %collective-permute-start.2 = (bf16[1280,640]{1,0:T(8,128)(2,1)}, bf16[1280,640]{1,0:T(8,128)(2,1)S(1)}, u32[]{:S(2)}, u32[]{:S(2)}) collective-permute-start(bf16[1280,640]{1,0:T(8,128)(2,1)} %bitcast.11), channel_id=1, source_target_pairs={{0,32},{32,0},{64,96},{96,64},{128,160},{160,128},{192,224},{224,1... | collective-permute-start | bytes 4915208 | tf_op jit(solution)/shard_map/ppermute | solution.py:276
  6.6 1.8 %reshape.40 = bf16[32,4,1280]{2,1,0:T(4,128)(2,1)} reshape(bf16[128,1280]{1,0:T(8,128)(2,1)} %get-tuple-element.20) | data formatting | bytes 655360 | tf_op jit(solution)/shard_map/reshape | solution.py:281
  8.4 20.0 %all_to_all.15 = bf16[32,4,1280]{2,1,0:T(4,128)(2,1)} all-to-all(bf16[32,4,1280]{2,1,0:T(4,128)(2,1)} %reshape.40), channel_id=1, replica_groups=mesh['dp'=8,'expert'=32] {'expert'}, dimensions={0} | all-to-all | bytes 655360 | tf_op jit(solution)/shard_map/all_to_all | solution.py:258
  28.4 1.8 %reshape.41.rows_ref = bf16[128,1280]{1,0:T(8,128)(2,1)} reshape(bf16[32,4,1280]{2,1,0:T(4,128)(2,1)} %all_to_all.15) | data formatting | bytes 655360 | tf_op jit(solution)/shard_map/reshape | solution.py:281
  31.4 1.5 %collective-permute-start.1 = (bf16[128,1280]{1,0:T(8,128)(2,1)}, bf16[128,1280]{1,0:T(8,128)(2,1)S(1)}, u32[]{:S(2)}, u32[]{:S(2)}) collective-permute-start(bf16[128,1280]{1,0:T(8,128)(2,1)} %reshape.41.rows_ref), channel_id=1, source_target_pairs={{0,192},{32,224},{64,0},{96,32},{128,64},{160,96},{192,128},{224,1... | collective-permute-start | bytes 983048 | tf_op jit(solution)/shard_map/ppermute | solution.py:284
  35.3 2.7 %expert.3 = f32[128,1280]{1,0:T(8,128)S(1)} custom-call(bf16[128,1280]{1,0:T(8,128)(2,1)S(1)} %copy-done.2, bf16[1280,640]{1,0:T(8,128)(2,1)S(1)} %bitcast.12, bf16[1280,640]{1,0:T(8,128)(2,1)S(1)} %collective-permute-done.2.in_other, bf16[640,1280]{1,0:T(8,128)(2,1)S(1)} %bitcast.16, bf16[640,1280]{1,0:T(8,128)(2,1)} %collective-permute-done.3.out_other), custom_call_target="tpu_custom_call" | custom-call | flops 838860800 | bytes 7536640 | tf_op jit(solution)/shard_map/expert/pallas_call | solution.py:233
  38.0 2.3 %collective-permute-start.5 = (bf16[64,1280]{1,0:T(8,128)(2,1)S(1)}, bf16[64,1280]{1,0:T(8,128)(2,1)S(1)}, u32[]{:S(2)}, u32[]{:S(2)}) collective-permute-start(bf16[64,1280]{1,0:T(8,128)(2,1)S(1)} %slice.33), channel_id=1, source_target_pairs={{0,192},{32,224},{64,0},{96,32},{128,64},{160,96},{192,128},{224,1... | collective-permute-start | bytes 491528 | tf_op jit(solution)/shard_map/ppermute | solution.py:290
  40.4 3.7 %expert.4 = f32[256,1280]{1,0:T(8,128)S(1)} custom-call(bf16[256,1280]{1,0:T(8,128)(2,1)S(1)} %pad_maximum_fusion.rows_ref, bf16[1280,640]{1,0:T(8,128)(2,1)S(1)} %bitcast.13, bf16[1280,640]{1,0:T(8,128)(2,1)S(1)} %collective-permute-done.2.in_other, bf16[640,1280]{1,0:T(8,128)(2,1)S(1)} %bitcast.17, bf16[640,1280]{1,0:T(8,128)(2,1)} %collective-permute-done.3.out_other), custom_call_target="tpu_custom_call" | custom-call | flops 1677721600 | bytes 8519680 | tf_op jit(solution)/shard_map/expert/pallas_call | solution.py:233
  44.1 1.6 %collective-permute-done.4 = bf16[64,1280]{1,0:T(8,128)(2,1)S(1)} collective-permute-done((bf16[64,1280]{1,0:T(8,128)(2,1)S(1)}, bf16[64,1280]{1,0:T(8,128)(2,1)S(1)}, u32[]{:S(2)}, u32[]{:S(2)}) %collective-permute-start.4) | collective-permute-done | bytes 163872 | tf_op jit(solution)/shard_map/ppermute | solution.py:289
  45.8 2.7 %expert.5 = f32[128,1280]{1,0:T(8,128)S(1)} custom-call(bf16[128,1280]{1,0:T(8,128)(2,1)S(1)} %pad_maximum_fusion.1.rows_ref, bf16[1280,640]{1,0:T(8,128)(2,1)S(1)} %bitcast.14, bf16[1280,640]{1,0:T(8,128)(2,1)S(1)} %collective-permute-done.2.in_other, bf16[640,1280]{1,0:T(8,128)(2,1)S(1)} %bitcast.18, bf16[640,1280]{1,0:T(8,128)(2,1)} %collective-permute-done.3.out_other), custom_call_target="tpu_custom_call" | custom-call | flops 838860800 | bytes 7536640 | tf_op jit(solution)/shard_map/expert/pallas_call | solution.py:233
  50.2 2.8 %collective-permute-done.6 = bf16[64,1280]{1,0:T(8,128)(2,1)S(1)} collective-permute-done((bf16[64,1280]{1,0:T(8,128)(2,1)S(1)}, bf16[64,1280]{1,0:T(8,128)(2,1)S(1)}, u32[]{:S(2)}, u32[]{:S(2)}) %collective-permute-start.6) | collective-permute-done | bytes 163872 | tf_op jit(solution)/shard_map/ppermute | solution.py:297
  53.0 2.1 %collective-permute-done.8 = bf16[64,1280]{1,0:T(8,128)(2,1)S(1)} collective-permute-done((bf16[64,1280]{1,0:T(8,128)(2,1)S(1)}, bf16[64,1280]{1,0:T(8,128)(2,1)S(1)}, u32[]{:S(2)}, u32[]{:S(2)}) %collective-permute-start.8) | collective-permute-done | bytes 163872 | tf_op jit(solution)/shard_map/ppermute | solution.py:298
  55.3 2.9 %collective-permute-start.7 = (bf16[128,1280]{1,0:T(8,128)(2,1)S(1)}, bf16[128,1280]{1,0:T(8,128)(2,1)S(1)}, u32[]{:S(2)}, u32[]{:S(2)}) collective-permute-start(bf16[128,1280]{1,0:T(8,128)(2,1)S(1)} %pad_maximum_fusion.2), channel_id=1, source_target_pairs={{0,192},{32,224},{64,0},{96,32},{128,64},{160,96},{192,128},{224,1... | collective-permute-start | bytes 983048 | tf_op jit(solution)/shard_map/ppermute | solution.py:303
  58.2 5.9 %collective-permute-done.9 = bf16[128,1280]{1,0:T(8,128)(2,1)S(1)} collective-permute-done((bf16[128,1280]{1,0:T(8,128)(2,1)S(1)}, bf16[128,1280]{1,0:T(8,128)(2,1)S(1)}, u32[]{:S(2)}, u32[]{:S(2)}) %collective-permute-start.9) | collective-permute-done | bytes 327712 | tf_op jit(solution)/shard_map/ppermute | solution.py:304
  64.4 17.7 %all_to_all.16 = bf16[32,4,1280]{2,1,0:T(4,128)(2,1)S(1)} all-to-all(bf16[32,4,1280]{2,1,0:T(4,128)(2,1)S(1)} %reshape.42), channel_id=1, replica_groups=mesh['dp'=8,'expert'=32] {'expert'}, dimensions={0} | all-to-all | bytes 655360 | tf_op jit(solution)/shard_map/all_to_all | solution.py:258
  82.8 2.6 %combine.1 = (bf16[256,1280]{1,0:T(8,128)(2,1)}, f32[640,128]{1,0:T(8,128)}) custom-call(bf16[128,1280]{1,0:T(8,128)(2,1)} %reshape.43.returned_ref, s32[1,256]{1,0:T(1,128)} %get-tuple-element.28.target_ref, f32[1,256]{1,0:T(1,128)} %bitcast.26, bf16[256,1280]{1,0:T(8,128)(2,1)} %tokens_ref.1, f32[1,1280]{1,0:T(1,128)} %text_ref.1), custom_call_target="tpu_custom_call" | custom-call | tf_op jit(solution)/shard_map/combine/pallas_call | solution.py:111
  85.4 14.8 %all_to_all.17 = f32[32,1,2560]{2,1,0:T(1,128)S(1)} all-to-all(f32[32,1,2560]{2,1,0:T(1,128)} %bitcast.23), channel_id=1, replica_groups=mesh['dp'=8,'expert'=32] {'expert'}, dimensions={0} | all-to-all | bytes 655360 | tf_op jit(solution)/shard_map/all_to_all | solution.py:258
  100.2 3.0 %collective-permute-start.11 = (f32[640,128]{1,0:T(8,128)S(1)}, f32[640,128]{1,0:T(8,128)S(1)}, u32[]{:S(2)}, u32[]{:S(2)}) collective-permute-start(f32[640,128]{1,0:T(8,128)S(1)} %bitcast.20), channel_id=1, source_target_pairs={{0,192},{32,224},{64,0},{96,32},{128,64},{160,96},{192,128},{224,1... | collective-permute-start | bytes 983048 | tf_op jit(solution)/shard_map/ppermute | solution.py:313
  103.1 8.6 %collective-permute-start.14 = (f32[640,128]{1,0:T(8,128)S(1)}, f32[640,128]{1,0:T(8,128)S(1)}, u32[]{:S(2)}, u32[]{:S(2)}) collective-permute-start(f32[640,128]{1,0:T(8,128)S(1)} %bitcast.21), channel_id=1, source_target_pairs={{0,32},{32,0},{64,96},{96,64},{128,160},{160,128},{192,224},{224,1... | collective-permute-start | bytes 983048 | tf_op jit(solution)/shard_map/ppermute | solution.py:320
  111.8 5.7 %collective-permute-start.15 = (f32[640,128]{1,0:T(8,128)S(1)}, f32[640,128]{1,0:T(8,128)S(1)}, u32[]{:S(2)}, u32[]{:S(2)}) collective-permute-start(f32[640,128]{1,0:T(8,128)S(1)} %collective-permute-done.10.refs_1_), channel_id=1, source_target_pairs={{0,32},{32,0},{64,96},{96,64},{128,160},{160,128},{192,224},{224,1... | collective-permute-start | bytes 983048 | tf_op jit(solution)/shard_map/ppermute | solution.py:320
  117.7 2.9 %collective-permute-start.13 = (f32[320,128]{1,0:T(8,128)S(1)}, f32[320,128]{1,0:T(8,128)S(1)}, u32[]{:S(2)}, u32[]{:S(2)}) collective-permute-start(f32[320,128]{1,0:T(8,128)S(1)} %slice.47), channel_id=1, source_target_pairs={{0,192},{32,224},{64,0},{96,32},{128,64},{160,96},{192,128},{224,1... | collective-permute-start | bytes 491528 | tf_op jit(solution)/shard_map/ppermute | solution.py:314
  120.6 3.4 %collective-permute-start.17 = (f32[320,128]{1,0:T(8,128)S(1)}, f32[320,128]{1,0:T(8,128)S(1)}, u32[]{:S(2)}, u32[]{:S(2)}) collective-permute-start(f32[320,128]{1,0:T(8,128)S(1)} %collective-permute-done.12.refs_3_), channel_id=1, source_target_pairs={{0,32},{32,0},{64,96},{96,64},{128,160},{160,128},{192,224},{224,1... | collective-permute-start | bytes 491528 | tf_op jit(solution)/shard_map/ppermute | solution.py:320
  126.0 3.6 %contrast.1 = (f32[1,1]{1,0:T(1,128)}, f32[1,1280]{1,0:T(1,128)}, f32[1,1280]{1,0:T(1,128)}) custom-call(s32[3]{0:T(128)S(1)} %pad_add_fusion.place_ref, f32[1]{0:T(128)S(6)} %copy.14.scale_ref, f32[640,128]{1,0:T(8,128)S(1)} %bitcast.22, f32[640,128]{1,0:T(8,128)S(1)} %collective-permute-done.10.refs_1_, f32[640,128]{1,0:T(8,128)S(1)} %collective-permute-done.11.refs_2_, ...), custom_call_target="tpu_custom_call" | custom-call | tf_op jit(solution)/shard_map/contrast/pallas_call | solution.py:195
  (48 shorter events, 8.4 us)
Async XLA Ops:
  3.1 29.7 %copy-start = (bf16[1,1280,640]{2,1,0:T(8,128)(2,1)S(1)}, bf16[1,1280,640]{2,1,0:T(8,128)(2,1)}, u32[]{:S(2)}) copy-start(bf16[1,1280,640]{2,1,0:T(8,128)(2,1)} %param.14) | copy-start | bytes 4915204
  3.1 29.7 %collective-permute-start.2 = (bf16[1280,640]{1,0:T(8,128)(2,1)}, bf16[1280,640]{1,0:T(8,128)(2,1)S(1)}, u32[]{:S(2)}, u32[]{:S(2)}) collective-permute-start(bf16[1280,640]{1,0:T(8,128)(2,1)} %bitcast.11), channel_id=1, source_target_pairs={{0,32},{32,0},{64,96},{96,64},{128,160},{160,128},{192,224},{224,1... | collective-permute-start | bytes 4915208 | tf_op jit(solution)/shard_map/ppermute | solution.py:276
  6.5 26.4 %collective-permute-start.3 = (bf16[640,1280]{1,0:T(8,128)(2,1)}, bf16[640,1280]{1,0:T(8,128)(2,1)}, u32[]{:S(2)}, u32[]{:S(2)}) collective-permute-start(bf16[640,1280]{1,0:T(8,128)(2,1)} %bitcast.15), channel_id=1, source_target_pairs={{0,32},{32,0},{64,96},{96,64},{128,160},{160,128},{192,224},{224,1... | collective-permute-start | bytes 4915208 | tf_op jit(solution)/shard_map/ppermute | solution.py:278
  30.2 7.8 %collective-permute-start = (bf16[128,1280]{1,0:T(8,128)(2,1)}, bf16[128,1280]{1,0:T(8,128)(2,1)S(1)}, u32[]{:S(2)}, u32[]{:S(2)}) collective-permute-start(bf16[128,1280]{1,0:T(8,128)(2,1)} %reshape.41.rows_ref), channel_id=1, source_target_pairs={{0,64},{32,96},{64,128},{96,160},{128,192},{160,224},{192,0},{224,... | collective-permute-start | bytes 983048 | tf_op jit(solution)/shard_map/ppermute | solution.py:283
  31.4 6.6 %collective-permute-start.1 = (bf16[128,1280]{1,0:T(8,128)(2,1)}, bf16[128,1280]{1,0:T(8,128)(2,1)S(1)}, u32[]{:S(2)}, u32[]{:S(2)}) collective-permute-start(bf16[128,1280]{1,0:T(8,128)(2,1)} %reshape.41.rows_ref), channel_id=1, source_target_pairs={{0,192},{32,224},{64,0},{96,32},{128,64},{160,96},{192,128},{224,1... | collective-permute-start | bytes 983048 | tf_op jit(solution)/shard_map/ppermute | solution.py:284
  32.8 1.4 %copy-start.1 = (bf16[1,640,1280]{2,1,0:T(8,128)(2,1)S(1)}, bf16[1,640,1280]{2,1,0:T(8,128)(2,1)}, u32[]{:S(2)}) copy-start(bf16[1,640,1280]{2,1,0:T(8,128)(2,1)} %param.15) | copy-start | bytes 4915204
  34.3 1.0 copy-start.2
  38.0 6.1 %collective-permute-start.5 = (bf16[64,1280]{1,0:T(8,128)(2,1)S(1)}, bf16[64,1280]{1,0:T(8,128)(2,1)S(1)}, u32[]{:S(2)}, u32[]{:S(2)}) collective-permute-start(bf16[64,1280]{1,0:T(8,128)(2,1)S(1)} %slice.33), channel_id=1, source_target_pairs={{0,192},{32,224},{64,0},{96,32},{128,64},{160,96},{192,128},{224,1... | collective-permute-start | bytes 491528 | tf_op jit(solution)/shard_map/ppermute | solution.py:290
  40.3 5.5 %collective-permute-start.4 = (bf16[64,1280]{1,0:T(8,128)(2,1)S(1)}, bf16[64,1280]{1,0:T(8,128)(2,1)S(1)}, u32[]{:S(2)}, u32[]{:S(2)}) collective-permute-start(bf16[64,1280]{1,0:T(8,128)(2,1)S(1)} %slice.32), channel_id=1, source_target_pairs={{0,64},{32,96},{64,128},{96,160},{128,192},{160,224},{192,0},{224,... | collective-permute-start | bytes 491528 | tf_op jit(solution)/shard_map/ppermute | solution.py:289
  48.6 4.4 %collective-permute-start.6 = (bf16[64,1280]{1,0:T(8,128)(2,1)S(1)}, bf16[64,1280]{1,0:T(8,128)(2,1)S(1)}, u32[]{:S(2)}, u32[]{:S(2)}) collective-permute-start(bf16[64,1280]{1,0:T(8,128)(2,1)S(1)} %get-tuple-element.38), channel_id=1, source_target_pairs={{0,192},{32,224},{64,0},{96,32},{128,64},{160,96},{192,128},{224,1... | collective-permute-start | bytes 491528 | tf_op jit(solution)/shard_map/ppermute | solution.py:297
  49.7 5.4 %collective-permute-start.8 = (bf16[64,1280]{1,0:T(8,128)(2,1)S(1)}, bf16[64,1280]{1,0:T(8,128)(2,1)S(1)}, u32[]{:S(2)}, u32[]{:S(2)}) collective-permute-start(bf16[64,1280]{1,0:T(8,128)(2,1)S(1)} %get-tuple-element.39), channel_id=1, source_target_pairs={{0,64},{32,96},{64,128},{96,160},{128,192},{160,224},{192,0},{224,... | collective-permute-start | bytes 491528 | tf_op jit(solution)/shard_map/ppermute | solution.py:298
  55.2 9.0 %collective-permute-start.9 = (bf16[128,1280]{1,0:T(8,128)(2,1)S(1)}, bf16[128,1280]{1,0:T(8,128)(2,1)S(1)}, u32[]{:S(2)}, u32[]{:S(2)}) collective-permute-start(bf16[128,1280]{1,0:T(8,128)(2,1)S(1)} %pad_maximum_fusion.3), channel_id=1, source_target_pairs={{0,64},{32,96},{64,128},{96,160},{128,192},{160,224},{192,0},{224,... | collective-permute-start | bytes 983048 | tf_op jit(solution)/shard_map/ppermute | solution.py:304
  55.3 8.9 %collective-permute-start.7 = (bf16[128,1280]{1,0:T(8,128)(2,1)S(1)}, bf16[128,1280]{1,0:T(8,128)(2,1)S(1)}, u32[]{:S(2)}, u32[]{:S(2)}) collective-permute-start(bf16[128,1280]{1,0:T(8,128)(2,1)S(1)} %pad_maximum_fusion.2), channel_id=1, source_target_pairs={{0,192},{32,224},{64,0},{96,32},{128,64},{160,96},{192,128},{224,1... | collective-permute-start | bytes 983048 | tf_op jit(solution)/shard_map/ppermute | solution.py:303
  100.2 11.6 %collective-permute-start.10 = (f32[640,128]{1,0:T(8,128)S(1)}, f32[640,128]{1,0:T(8,128)S(1)}, u32[]{:S(2)}, u32[]{:S(2)}) collective-permute-start(f32[640,128]{1,0:T(8,128)S(1)} %bitcast.19), channel_id=1, source_target_pairs={{0,64},{32,96},{64,128},{96,160},{128,192},{160,224},{192,0},{224,... | collective-permute-start | bytes 983048 | tf_op jit(solution)/shard_map/ppermute | solution.py:312
  100.2 17.4 %collective-permute-start.11 = (f32[640,128]{1,0:T(8,128)S(1)}, f32[640,128]{1,0:T(8,128)S(1)}, u32[]{:S(2)}, u32[]{:S(2)}) collective-permute-start(f32[640,128]{1,0:T(8,128)S(1)} %bitcast.20), channel_id=1, source_target_pairs={{0,192},{32,224},{64,0},{96,32},{128,64},{160,96},{192,128},{224,1... | collective-permute-start | bytes 983048 | tf_op jit(solution)/shard_map/ppermute | solution.py:313
  103.1 22.6 %collective-permute-start.14 = (f32[640,128]{1,0:T(8,128)S(1)}, f32[640,128]{1,0:T(8,128)S(1)}, u32[]{:S(2)}, u32[]{:S(2)}) collective-permute-start(f32[640,128]{1,0:T(8,128)S(1)} %bitcast.21), channel_id=1, source_target_pairs={{0,32},{32,0},{64,96},{96,64},{128,160},{160,128},{192,224},{224,1... | collective-permute-start | bytes 983048 | tf_op jit(solution)/shard_map/ppermute | solution.py:320
  111.8 8.9 %collective-permute-start.12 = (f32[320,128]{1,0:T(8,128)S(1)}, f32[320,128]{1,0:T(8,128)S(1)}, u32[]{:S(2)}, u32[]{:S(2)}) collective-permute-start(f32[320,128]{1,0:T(8,128)S(1)} %slice.46), channel_id=1, source_target_pairs={{0,64},{32,96},{64,128},{96,160},{128,192},{160,224},{192,0},{224,... | collective-permute-start | bytes 491528 | tf_op jit(solution)/shard_map/ppermute | solution.py:314
  111.8 13.9 %collective-permute-start.15 = (f32[640,128]{1,0:T(8,128)S(1)}, f32[640,128]{1,0:T(8,128)S(1)}, u32[]{:S(2)}, u32[]{:S(2)}) collective-permute-start(f32[640,128]{1,0:T(8,128)S(1)} %collective-permute-done.10.refs_1_), channel_id=1, source_target_pairs={{0,32},{32,0},{64,96},{96,64},{128,160},{160,128},{192,224},{224,1... | collective-permute-start | bytes 983048 | tf_op jit(solution)/shard_map/ppermute | solution.py:320
  117.6 8.2 %collective-permute-start.16 = (f32[640,128]{1,0:T(8,128)S(1)}, f32[640,128]{1,0:T(8,128)S(1)}, u32[]{:S(2)}, u32[]{:S(2)}) collective-permute-start(f32[640,128]{1,0:T(8,128)S(1)} %collective-permute-done.11.refs_2_), channel_id=1, source_target_pairs={{0,32},{32,0},{64,96},{96,64},{128,160},{160,128},{192,224},{224,1... | collective-permute-start | bytes 983048 | tf_op jit(solution)/shard_map/ppermute | solution.py:320
  117.7 6.3 %collective-permute-start.13 = (f32[320,128]{1,0:T(8,128)S(1)}, f32[320,128]{1,0:T(8,128)S(1)}, u32[]{:S(2)}, u32[]{:S(2)}) collective-permute-start(f32[320,128]{1,0:T(8,128)S(1)} %slice.47), channel_id=1, source_target_pairs={{0,192},{32,224},{64,0},{96,32},{128,64},{160,96},{192,128},{224,1... | collective-permute-start | bytes 491528 | tf_op jit(solution)/shard_map/ppermute | solution.py:314
  120.6 5.2 %collective-permute-start.17 = (f32[320,128]{1,0:T(8,128)S(1)}, f32[320,128]{1,0:T(8,128)S(1)}, u32[]{:S(2)}, u32[]{:S(2)}) collective-permute-start(f32[320,128]{1,0:T(8,128)S(1)} %collective-permute-done.12.refs_3_), channel_id=1, source_target_pairs={{0,32},{32,0},{64,96},{96,64},{128,160},{160,128},{192,224},{224,1... | collective-permute-start | bytes 491528 | tf_op jit(solution)/shard_map/ppermute | solution.py:320
  124.0 2.1 %collective-permute-start.18 = (f32[320,128]{1,0:T(8,128)S(1)}, f32[320,128]{1,0:T(8,128)S(1)}, u32[]{:S(2)}, u32[]{:S(2)}) collective-permute-start(f32[320,128]{1,0:T(8,128)S(1)} %collective-permute-done.13.refs_4_), channel_id=1, source_target_pairs={{0,32},{32,0},{64,96},{96,64},{128,160},{160,128},{192,224},{224,1... | collective-permute-start | bytes 491528 | tf_op jit(solution)/shard_map/ppermute | solution.py:320

commit v6 on v5

--- a/solution.py
+++ b/solution.py
@@ -11,7 +11,6 @@
 SLOTS = Y * Z * CAP
 PAIRS = X * CORES * Y * Z
 VMEM = pl.BlockSpec(memory_space=pltpu.VMEM)
-HBM = pl.BlockSpec(memory_space=pltpu.HBM)
 SMEM = pl.BlockSpec(memory_space=pltpu.SMEM)
 
 
@@ -37,23 +36,10 @@
     return narrow(wide(iota((SLOTS, target.shape[1]), 0) == target))
 
 
-def fetch(pairs, sems):
-    copies = [
-        pltpu.make_async_copy(source, target, sems.at[i]) for i, (source, target) in enumerate(pairs)
-    ]
-    for copy in copies:
-        copy.start()
-    for copy in copies:
-        copy.wait()
-
-
-def dispatch_kernel(tokens_hbm, gain_hbm, ids_hbm, ranks_hbm, out_ref, target_ref, *scratch):
-    tokens_ref, gain_ref, ids_ref, ranks_ref, sems = scratch
-    sources = (tokens_hbm, gain_hbm, ids_hbm, ranks_hbm)
-    fetch(list(zip(sources, (tokens_ref, gain_ref, ids_ref, ranks_ref))), sems)
-    ids = ids_ref[...]
-    base = wide(ids * 256)
-    key = base + wide(ranks_ref[...])
+def dispatch_kernel(tokens_ref, gain_ref, key_ref, out_ref, target_ref):
+    whole_key = key_ref[...]
+    ids = whole_key >> 8
+    base, key = wide(ids * 256), wide(whole_key)
     others = as_column(key)
     earlier = (others >= base) & (others < key)
     slots = jnp.sum(wide(earlier), axis=0, keepdims=True).astype(jnp.int32)
@@ -69,22 +55,19 @@
     )
 
 
-def dispatch(tokens, gain, ids, ranks):
+def dispatch(tokens, gain, key):
     rows, width = tokens.shape
-    inputs = (tokens, gain, ids, ranks)
     return pl.pallas_call(
         dispatch_kernel,
         out_shape=(
             jax.ShapeDtypeStruct((SLOTS, width), jnp.bfloat16),
             jax.ShapeDtypeStruct((1, rows), jnp.int32),
         ),
-        in_specs=[HBM] * 4,
+        in_specs=[VMEM] * 3,
         out_specs=(VMEM, VMEM),
-        scratch_shapes=[pltpu.VMEM(x.shape, x.dtype) for x in inputs]
-        + [pltpu.SemaphoreType.DMA((len(inputs),))],
-        compiler_params=pltpu.CompilerParams(vmem_limit_bytes=64 * 2**20),
+        compiler_params=pltpu.CompilerParams(vmem_limit_bytes=24 * 2**20),
         name="dispatch",
-    )(*inputs)
+    )(tokens, gain, key)
 
 
 def combine_kernel(
@@ -116,6 +99,7 @@
         ),
         in_specs=[VMEM] * 5,
         out_specs=(VMEM, VMEM),
+        compiler_params=pltpu.CompilerParams(vmem_limit_bytes=24 * 2**20),
         name="combine",
     )(returned, target, gate, tokens, text)
 
@@ -266,10 +250,8 @@
     dp_place = lax.axis_index("dp")
     places = jnp.stack([dp_place // CORES, dp_place % CORES, lax.axis_index("expert")])
 
-    outgoing, target = dispatch(
-        tokens, norm_gain.reshape(width // LANES, LANES), expert_ids.reshape(1, rows), priority
-    )
-    outgoing, w_in, w_out = lax.optimization_barrier((outgoing, w_in, w_out))
+    key = expert_ids.reshape(1, rows) * 256 + priority
+    outgoing, target = dispatch(tokens, norm_gain.reshape(width // LANES, LANES), key)
 
     weights = (
         w_in[0],

time: 131 us -> 130 us (level)
  Pallas kernels: 17.8 us -> 14.8 us
  local copies, waits for them, and re-layouts: 6.97 us -> 8.74 us
    unnamed x6 -> x20, local copies, waits for them, and re-layouts: 2.4 us -> 4.93 us
    pallas_call x1, Pallas kernels: 2.48 us -> 0.66 us  [dispatch(): pl.pallas_call(dispatch_kernel, out_shape=(jax.ShapeDtypeStruct((SLOTS, w...]
  transfers between devices with their start and end apart: 19 -> 19, of which waited for: 5 -> 5; matrix products, arithmetic and copies ran while one was open for 3% -> 4% of each run, Pallas kernels for 5% -> 6%
where the time goes in v6:
time: 130 us; the launch traced here: 129 us
  blocking collectives  52.4 us (40%)
  starting transfers between devices  37.8 us (29%)
  Pallas kernels  14.8 us (11%)
  waiting for transfers between devices  12.7 us (10%)
  local copies, waits for them, and re-layouts  8.74 us (7%)
  between operations  1.58 us (1%)
    all_to_all x3, blocking collectives, to_experts(): lax.all_to_all(blocks, 'expert', split_axis=0, concat_axis=0, tiled=True)  52.4 us
    ppermute x5, starting transfers between devices, on_device(): lax.ppermute(block, *along_core())  18.8 us
    pallas_call x3, Pallas kernels, expert_rows(): pl.pallas_call(expert_kernel, out_shape=jax.ShapeDtypeStruct((count, widt...  9.29 us
    ppermute x1, waiting for transfers between devices, on_device(): right_sum = lax.ppermute(narrow(right_sum), *along_x(1))  5.94 us
    unnamed x20, local copies, waits for them, and re-layouts  4.93 us
    pallas_call x1, Pallas kernels, contrast(): pl.pallas_call(contrast_kernel, out_shape=(jax.ShapeDtypeStruct((1, 1), j...  3.59 us
    ppermute x1, starting transfers between devices, on_device(): lax.ppermute(w_in[0], *along_core())  3.33 us
    ppermute x1, starting transfers between devices, on_device(): lax.ppermute(right[half:], *along_x(-1))  2.99 us
  transfers between devices with their start and end apart: 19, of which 5 were waited for; matrix products, arithmetic and copies ran while one was open for 4% of the time, Pallas kernels for 6%

profile of v6, /device:TPU:1, one launch (start us, length us, event | category | flops | bytes accessed | tf_op | source)
XLA Modules:
  0.0 129.2 jit_solution(15428589472840744797)
XLA Ops:
  0.6 3.3 %collective-permute-start.2 = (bf16[1280,640]{1,0:T(8,128)(2,1)}, bf16[1280,640]{1,0:T(8,128)(2,1)S(1)}, u32[]{:S(2)}, u32[]{:S(2)}) collective-permute-start(bf16[1280,640]{1,0:T(8,128)(2,1)} %bitcast.12), channel_id=1, source_target_pairs={{0,32},{32,0},{64,96},{96,64},{128,160},{160,128},{192,224},{224,1... | collective-permute-start | bytes 4915208 | tf_op jit(solution)/shard_map/ppermute | solution.py:258
  7.9 1.8 %reshape.51 = bf16[32,4,1280]{2,1,0:T(4,128)(2,1)} reshape(bf16[128,1280]{1,0:T(8,128)(2,1)} %copy-done.6) | data formatting | bytes 655360 | tf_op jit(solution)/shard_map/reshape | solution.py:263
  9.7 20.0 %all_to_all.15 = bf16[32,4,1280]{2,1,0:T(4,128)(2,1)} all-to-all(bf16[32,4,1280]{2,1,0:T(4,128)(2,1)} %reshape.51), channel_id=1, replica_groups=mesh['dp'=8,'expert'=32] {'expert'}, dimensions={0} | all-to-all | bytes 655360 | tf_op jit(solution)/shard_map/all_to_all | solution.py:242
  29.7 1.8 %reshape.52.rows_ref = bf16[128,1280]{1,0:T(8,128)(2,1)} reshape(bf16[32,4,1280]{2,1,0:T(4,128)(2,1)} %all_to_all.15) | data formatting | bytes 655360 | tf_op jit(solution)/shard_map/reshape | solution.py:263
  32.7 1.5 %collective-permute-start.1 = (bf16[128,1280]{1,0:T(8,128)(2,1)}, bf16[128,1280]{1,0:T(8,128)(2,1)S(1)}, u32[]{:S(2)}, u32[]{:S(2)}) collective-permute-start(bf16[128,1280]{1,0:T(8,128)(2,1)} %reshape.52.rows_ref), channel_id=1, source_target_pairs={{0,192},{32,224},{64,0},{96,32},{128,64},{160,96},{192,128},{224,1... | collective-permute-start | bytes 983048 | tf_op jit(solution)/shard_map/ppermute | solution.py:266
  34.2 1.4 %copy-done.1 = bf16[1,640,1280]{2,1,0:T(8,128)(2,1)S(1)} copy-done((bf16[1,640,1280]{2,1,0:T(8,128)(2,1)S(1)}, bf16[1,640,1280]{2,1,0:T(8,128)(2,1)}, u32[]{:S(2)}) %copy-start.1) | copy-done | bytes 1638424
  36.6 2.7 %expert.3 = f32[128,1280]{1,0:T(8,128)S(1)} custom-call(bf16[128,1280]{1,0:T(8,128)(2,1)S(1)} %copy-done.5, bf16[1280,640]{1,0:T(8,128)(2,1)S(1)} %bitcast.13, bf16[1280,640]{1,0:T(8,128)(2,1)S(1)} %collective-permute-done.2.in_other, bf16[640,1280]{1,0:T(8,128)(2,1)S(1)} %bitcast.17, bf16[640,1280]{1,0:T(8,128)(2,1)} %collective-permute-done.3.out_other), custom_call_target="tpu_custom_call" | custom-call | flops 838860800 | bytes 7536640 | tf_op jit(solution)/shard_map/expert/pallas_call | solution.py:217
  39.4 2.2 %collective-permute-start.5 = (bf16[64,1280]{1,0:T(8,128)(2,1)S(1)}, bf16[64,1280]{1,0:T(8,128)(2,1)S(1)}, u32[]{:S(2)}, u32[]{:S(2)}) collective-permute-start(bf16[64,1280]{1,0:T(8,128)(2,1)S(1)} %slice.33), channel_id=1, source_target_pairs={{0,192},{32,224},{64,0},{96,32},{128,64},{160,96},{192,128},{224,1... | collective-permute-start | bytes 491528 | tf_op jit(solution)/shard_map/ppermute | solution.py:272
  41.8 3.8 %expert.4 = f32[256,1280]{1,0:T(8,128)S(1)} custom-call(bf16[256,1280]{1,0:T(8,128)(2,1)S(1)} %pad_maximum_fusion.rows_ref, bf16[1280,640]{1,0:T(8,128)(2,1)S(1)} %bitcast.14, bf16[1280,640]{1,0:T(8,128)(2,1)S(1)} %collective-permute-done.2.in_other, bf16[640,1280]{1,0:T(8,128)(2,1)S(1)} %bitcast.18, bf16[640,1280]{1,0:T(8,128)(2,1)} %collective-permute-done.3.out_other), custom_call_target="tpu_custom_call" | custom-call | flops 1677721600 | bytes 8519680 | tf_op jit(solution)/shard_map/expert/pallas_call | solution.py:217
  45.6 1.5 %collective-permute-done.4 = bf16[64,1280]{1,0:T(8,128)(2,1)S(1)} collective-permute-done((bf16[64,1280]{1,0:T(8,128)(2,1)S(1)}, bf16[64,1280]{1,0:T(8,128)(2,1)S(1)}, u32[]{:S(2)}, u32[]{:S(2)}) %collective-permute-start.4) | collective-permute-done | bytes 163872 | tf_op jit(solution)/shard_map/ppermute | solution.py:271
  47.1 2.7 %expert.5 = f32[128,1280]{1,0:T(8,128)S(1)} custom-call(bf16[128,1280]{1,0:T(8,128)(2,1)S(1)} %pad_maximum_fusion.1.rows_ref, bf16[1280,640]{1,0:T(8,128)(2,1)S(1)} %bitcast.15, bf16[1280,640]{1,0:T(8,128)(2,1)S(1)} %collective-permute-done.2.in_other, bf16[640,1280]{1,0:T(8,128)(2,1)S(1)} %bitcast.19, bf16[640,1280]{1,0:T(8,128)(2,1)} %collective-permute-done.3.out_other), custom_call_target="tpu_custom_call" | custom-call | flops 838860800 | bytes 7536640 | tf_op jit(solution)/shard_map/expert/pallas_call | solution.py:217
  51.6 2.8 %collective-permute-done.6 = bf16[64,1280]{1,0:T(8,128)(2,1)S(1)} collective-permute-done((bf16[64,1280]{1,0:T(8,128)(2,1)S(1)}, bf16[64,1280]{1,0:T(8,128)(2,1)S(1)}, u32[]{:S(2)}, u32[]{:S(2)}) %collective-permute-start.6) | collective-permute-done | bytes 163872 | tf_op jit(solution)/shard_map/ppermute | solution.py:279
  54.4 2.3 %collective-permute-done.8 = bf16[64,1280]{1,0:T(8,128)(2,1)S(1)} collective-permute-done((bf16[64,1280]{1,0:T(8,128)(2,1)S(1)}, bf16[64,1280]{1,0:T(8,128)(2,1)S(1)}, u32[]{:S(2)}, u32[]{:S(2)}) %collective-permute-start.8) | collective-permute-done | bytes 163872 | tf_op jit(solution)/shard_map/ppermute | solution.py:280
  56.8 2.9 %collective-permute-start.7 = (bf16[128,1280]{1,0:T(8,128)(2,1)S(1)}, bf16[128,1280]{1,0:T(8,128)(2,1)S(1)}, u32[]{:S(2)}, u32[]{:S(2)}) collective-permute-start(bf16[128,1280]{1,0:T(8,128)(2,1)S(1)} %pad_maximum_fusion.2), channel_id=1, source_target_pairs={{0,192},{32,224},{64,0},{96,32},{128,64},{160,96},{192,128},{224,1... | collective-permute-start | bytes 983048 | tf_op jit(solution)/shard_map/ppermute | solution.py:285
  59.7 5.9 %collective-permute-done.9 = bf16[128,1280]{1,0:T(8,128)(2,1)S(1)} collective-permute-done((bf16[128,1280]{1,0:T(8,128)(2,1)S(1)}, bf16[128,1280]{1,0:T(8,128)(2,1)S(1)}, u32[]{:S(2)}, u32[]{:S(2)}) %collective-permute-start.9) | collective-permute-done | bytes 327712 | tf_op jit(solution)/shard_map/ppermute | solution.py:286
  65.9 17.8 %all_to_all.16 = bf16[32,4,1280]{2,1,0:T(4,128)(2,1)S(1)} all-to-all(bf16[32,4,1280]{2,1,0:T(4,128)(2,1)S(1)} %reshape.53), channel_id=1, replica_groups=mesh['dp'=8,'expert'=32] {'expert'}, dimensions={0} | all-to-all | bytes 655360 | tf_op jit(solution)/shard_map/all_to_all | solution.py:242
  83.9 1.3 %combine.1 = (bf16[256,1280]{1,0:T(8,128)(2,1)}, f32[640,128]{1,0:T(8,128)S(1)}) custom-call(bf16[128,1280]{1,0:T(8,128)(2,1)S(1)} %reshape.54.returned_ref, s32[1,256]{1,0:T(1,128)S(1)} %get-tuple-element.22.target_ref, f32[1,256]{1,0:T(1,128)S(1)} %bitcast.26, bf16[256,1280]{1,0:T(8,128)(2,1)S(1)} %copy-done.4, f32[1,1280]{1,0:T(1,128)S(1)} %copy-done.8), custom_call_target="tpu_custom_call" | custom-call | tf_op jit(solution)/shard_map/combine/pallas_call | solution.py:94
  85.2 14.6 %all_to_all.17 = f32[32,1,2560]{2,1,0:T(1,128)S(1)} all-to-all(f32[32,1,2560]{2,1,0:T(1,128)S(1)} %bitcast.24), channel_id=1, replica_groups=mesh['dp'=8,'expert'=32] {'expert'}, dimensions={0} | all-to-all | bytes 655360 | tf_op jit(solution)/shard_map/all_to_all | solution.py:242
  99.7 3.0 %collective-permute-start.11 = (f32[640,128]{1,0:T(8,128)S(1)}, f32[640,128]{1,0:T(8,128)S(1)}, u32[]{:S(2)}, u32[]{:S(2)}) collective-permute-start(f32[640,128]{1,0:T(8,128)S(1)} %bitcast.21), channel_id=1, source_target_pairs={{0,192},{32,224},{64,0},{96,32},{128,64},{160,96},{192,128},{224,1... | collective-permute-start | bytes 983048 | tf_op jit(solution)/shard_map/ppermute | solution.py:295
  102.7 8.5 %collective-permute-start.14 = (f32[640,128]{1,0:T(8,128)S(1)}, f32[640,128]{1,0:T(8,128)S(1)}, u32[]{:S(2)}, u32[]{:S(2)}) collective-permute-start(f32[640,128]{1,0:T(8,128)S(1)} %bitcast.22), channel_id=1, source_target_pairs={{0,32},{32,0},{64,96},{96,64},{128,160},{160,128},{192,224},{224,1... | collective-permute-start | bytes 983048 | tf_op jit(solution)/shard_map/ppermute | solution.py:302
  111.3 5.7 %collective-permute-start.15 = (f32[640,128]{1,0:T(8,128)S(1)}, f32[640,128]{1,0:T(8,128)S(1)}, u32[]{:S(2)}, u32[]{:S(2)}) collective-permute-start(f32[640,128]{1,0:T(8,128)S(1)} %collective-permute-done.10.refs_1_), channel_id=1, source_target_pairs={{0,32},{32,0},{64,96},{96,64},{128,160},{160,128},{192,224},{224,1... | collective-permute-start | bytes 983048 | tf_op jit(solution)/shard_map/ppermute | solution.py:302
  117.2 3.0 %collective-permute-start.13 = (f32[320,128]{1,0:T(8,128)S(1)}, f32[320,128]{1,0:T(8,128)S(1)}, u32[]{:S(2)}, u32[]{:S(2)}) collective-permute-start(f32[320,128]{1,0:T(8,128)S(1)} %slice.47), channel_id=1, source_target_pairs={{0,192},{32,224},{64,0},{96,32},{128,64},{160,96},{192,128},{224,1... | collective-permute-start | bytes 491528 | tf_op jit(solution)/shard_map/ppermute | solution.py:296
  120.1 3.3 %collective-permute-start.17 = (f32[320,128]{1,0:T(8,128)S(1)}, f32[320,128]{1,0:T(8,128)S(1)}, u32[]{:S(2)}, u32[]{:S(2)}) collective-permute-start(f32[320,128]{1,0:T(8,128)S(1)} %collective-permute-done.12.refs_3_), channel_id=1, source_target_pairs={{0,32},{32,0},{64,96},{96,64},{128,160},{160,128},{192,224},{224,1... | collective-permute-start | bytes 491528 | tf_op jit(solution)/shard_map/ppermute | solution.py:302
  125.6 3.6 %contrast.1 = (f32[1,1]{1,0:T(1,128)}, f32[1,1280]{1,0:T(1,128)}, f32[1,1280]{1,0:T(1,128)}) custom-call(s32[3]{0:T(128)S(1)} %pad_add_fusion.place_ref, f32[1]{0:T(128)S(6)} %copy.14.scale_ref, f32[640,128]{1,0:T(8,128)S(1)} %bitcast.23, f32[640,128]{1,0:T(8,128)S(1)} %collective-permute-done.10.refs_1_, f32[640,128]{1,0:T(8,128)S(1)} %collective-permute-done.11.refs_2_, ...), custom_call_target="tpu_custom_call" | custom-call | tf_op jit(solution)/shard_map/contrast/pallas_call | solution.py:179
  (63 shorter events, 10.2 us)
Async XLA Ops:
  0.6 33.6 %collective-permute-start.2 = (bf16[1280,640]{1,0:T(8,128)(2,1)}, bf16[1280,640]{1,0:T(8,128)(2,1)S(1)}, u32[]{:S(2)}, u32[]{:S(2)}) collective-permute-start(bf16[1280,640]{1,0:T(8,128)(2,1)} %bitcast.12), channel_id=1, source_target_pairs={{0,32},{32,0},{64,96},{96,64},{128,160},{160,128},{192,224},{224,1... | collective-permute-start | bytes 4915208 | tf_op jit(solution)/shard_map/ppermute | solution.py:258
  4.0 30.2 %collective-permute-start.3 = (bf16[640,1280]{1,0:T(8,128)(2,1)}, bf16[640,1280]{1,0:T(8,128)(2,1)}, u32[]{:S(2)}, u32[]{:S(2)}) collective-permute-start(bf16[640,1280]{1,0:T(8,128)(2,1)} %bitcast.16), channel_id=1, source_target_pairs={{0,32},{32,0},{64,96},{96,64},{128,160},{160,128},{192,224},{224,1... | collective-permute-start | bytes 4915208 | tf_op jit(solution)/shard_map/ppermute | solution.py:260
  6.5 27.6 %copy-start = (bf16[1,1280,640]{2,1,0:T(8,128)(2,1)S(1)}, bf16[1,1280,640]{2,1,0:T(8,128)(2,1)}, u32[]{:S(2)}) copy-start(bf16[1,1280,640]{2,1,0:T(8,128)(2,1)} %param.14) | copy-start | bytes 4915204
  31.5 7.8 %collective-permute-start = (bf16[128,1280]{1,0:T(8,128)(2,1)}, bf16[128,1280]{1,0:T(8,128)(2,1)S(1)}, u32[]{:S(2)}, u32[]{:S(2)}) collective-permute-start(bf16[128,1280]{1,0:T(8,128)(2,1)} %reshape.52.rows_ref), channel_id=1, source_target_pairs={{0,64},{32,96},{64,128},{96,160},{128,192},{160,224},{192,0},{224,... | collective-permute-start | bytes 983048 | tf_op jit(solution)/shard_map/ppermute | solution.py:265
  32.7 6.6 %collective-permute-start.1 = (bf16[128,1280]{1,0:T(8,128)(2,1)}, bf16[128,1280]{1,0:T(8,128)(2,1)S(1)}, u32[]{:S(2)}, u32[]{:S(2)}) collective-permute-start(bf16[128,1280]{1,0:T(8,128)(2,1)} %reshape.52.rows_ref), channel_id=1, source_target_pairs={{0,192},{32,224},{64,0},{96,32},{128,64},{160,96},{192,128},{224,1... | collective-permute-start | bytes 983048 | tf_op jit(solution)/shard_map/ppermute | solution.py:266
  39.4 6.2 %collective-permute-start.5 = (bf16[64,1280]{1,0:T(8,128)(2,1)S(1)}, bf16[64,1280]{1,0:T(8,128)(2,1)S(1)}, u32[]{:S(2)}, u32[]{:S(2)}) collective-permute-start(bf16[64,1280]{1,0:T(8,128)(2,1)S(1)} %slice.33), channel_id=1, source_target_pairs={{0,192},{32,224},{64,0},{96,32},{128,64},{160,96},{192,128},{224,1... | collective-permute-start | bytes 491528 | tf_op jit(solution)/shard_map/ppermute | solution.py:272
  41.6 5.5 %collective-permute-start.4 = (bf16[64,1280]{1,0:T(8,128)(2,1)S(1)}, bf16[64,1280]{1,0:T(8,128)(2,1)S(1)}, u32[]{:S(2)}, u32[]{:S(2)}) collective-permute-start(bf16[64,1280]{1,0:T(8,128)(2,1)S(1)} %slice.32), channel_id=1, source_target_pairs={{0,64},{32,96},{64,128},{96,160},{128,192},{160,224},{192,0},{224,... | collective-permute-start | bytes 491528 | tf_op jit(solution)/shard_map/ppermute | solution.py:271
  41.8 5.3 %copy-start.2 = (bf16[1,640,1280]{2,1,0:T(8,128)(2,1)S(1)}, bf16[1,640,1280]{2,1,0:T(8,128)(2,1)}, u32[]{:S(2)}) copy-start(bf16[1,640,1280]{2,1,0:T(8,128)(2,1)} %param.15) | copy-start | bytes 4915204
  50.0 4.4 %collective-permute-start.6 = (bf16[64,1280]{1,0:T(8,128)(2,1)S(1)}, bf16[64,1280]{1,0:T(8,128)(2,1)S(1)}, u32[]{:S(2)}, u32[]{:S(2)}) collective-permute-start(bf16[64,1280]{1,0:T(8,128)(2,1)S(1)} %get-tuple-element.32), channel_id=1, source_target_pairs={{0,192},{32,224},{64,0},{96,32},{128,64},{160,96},{192,128},{224,1... | collective-permute-start | bytes 491528 | tf_op jit(solution)/shard_map/ppermute | solution.py:279
  51.2 5.4 %collective-permute-start.8 = (bf16[64,1280]{1,0:T(8,128)(2,1)S(1)}, bf16[64,1280]{1,0:T(8,128)(2,1)S(1)}, u32[]{:S(2)}, u32[]{:S(2)}) collective-permute-start(bf16[64,1280]{1,0:T(8,128)(2,1)S(1)} %get-tuple-element.33), channel_id=1, source_target_pairs={{0,64},{32,96},{64,128},{96,160},{128,192},{160,224},{192,0},{224,... | collective-permute-start | bytes 491528 | tf_op jit(solution)/shard_map/ppermute | solution.py:280
  56.7 9.0 %collective-permute-start.9 = (bf16[128,1280]{1,0:T(8,128)(2,1)S(1)}, bf16[128,1280]{1,0:T(8,128)(2,1)S(1)}, u32[]{:S(2)}, u32[]{:S(2)}) collective-permute-start(bf16[128,1280]{1,0:T(8,128)(2,1)S(1)} %pad_maximum_fusion.3), channel_id=1, source_target_pairs={{0,64},{32,96},{64,128},{96,160},{128,192},{160,224},{192,0},{224,... | collective-permute-start | bytes 983048 | tf_op jit(solution)/shard_map/ppermute | solution.py:286
  56.8 8.9 %collective-permute-start.7 = (bf16[128,1280]{1,0:T(8,128)(2,1)S(1)}, bf16[128,1280]{1,0:T(8,128)(2,1)S(1)}, u32[]{:S(2)}, u32[]{:S(2)}) collective-permute-start(bf16[128,1280]{1,0:T(8,128)(2,1)S(1)} %pad_maximum_fusion.2), channel_id=1, source_target_pairs={{0,192},{32,224},{64,0},{96,32},{128,64},{160,96},{192,128},{224,1... | collective-permute-start | bytes 983048 | tf_op jit(solution)/shard_map/ppermute | solution.py:285
  65.8 18.0 %copy-start.4 = (bf16[256,1280]{1,0:T(8,128)(2,1)S(1)}, bf16[256,1280]{1,0:T(8,128)(2,1)}, u32[]{:S(2)}) copy-start(bf16[256,1280]{1,0:T(8,128)(2,1)} %tokens_ref.3) | copy-start | bytes 1966084
  65.8 18.0 %copy-start.8 = (f32[1,1280]{1,0:T(1,128)S(1)}, f32[1,1280]{1,0:T(1,128)}, u32[]{:S(2)}) copy-start(f32[1,1280]{1,0:T(1,128)} %text_ref.1) | copy-start | bytes 15364
  65.8 18.0 %copy-start.9 = (f32[256]{0:T(256)S(1)}, f32[256]{0:T(256)}, u32[]{:S(2)}) copy-start(f32[256]{0:T(256)} %param.13) | copy-start | bytes 3076
  99.7 11.5 %collective-permute-start.10 = (f32[640,128]{1,0:T(8,128)S(1)}, f32[640,128]{1,0:T(8,128)S(1)}, u32[]{:S(2)}, u32[]{:S(2)}) collective-permute-start(f32[640,128]{1,0:T(8,128)S(1)} %bitcast.20), channel_id=1, source_target_pairs={{0,64},{32,96},{64,128},{96,160},{128,192},{160,224},{192,0},{224,... | collective-permute-start | bytes 983048 | tf_op jit(solution)/shard_map/ppermute | solution.py:294
  99.7 17.3 %collective-permute-start.11 = (f32[640,128]{1,0:T(8,128)S(1)}, f32[640,128]{1,0:T(8,128)S(1)}, u32[]{:S(2)}, u32[]{:S(2)}) collective-permute-start(f32[640,128]{1,0:T(8,128)S(1)} %bitcast.21), channel_id=1, source_target_pairs={{0,192},{32,224},{64,0},{96,32},{128,64},{160,96},{192,128},{224,1... | collective-permute-start | bytes 983048 | tf_op jit(solution)/shard_map/ppermute | solution.py:295
  102.7 22.6 %collective-permute-start.14 = (f32[640,128]{1,0:T(8,128)S(1)}, f32[640,128]{1,0:T(8,128)S(1)}, u32[]{:S(2)}, u32[]{:S(2)}) collective-permute-start(f32[640,128]{1,0:T(8,128)S(1)} %bitcast.22), channel_id=1, source_target_pairs={{0,32},{32,0},{64,96},{96,64},{128,160},{160,128},{192,224},{224,1... | collective-permute-start | bytes 983048 | tf_op jit(solution)/shard_map/ppermute | solution.py:302
  111.2 8.9 %collective-permute-start.12 = (f32[320,128]{1,0:T(8,128)S(1)}, f32[320,128]{1,0:T(8,128)S(1)}, u32[]{:S(2)}, u32[]{:S(2)}) collective-permute-start(f32[320,128]{1,0:T(8,128)S(1)} %slice.46), channel_id=1, source_target_pairs={{0,64},{32,96},{64,128},{96,160},{128,192},{160,224},{192,0},{224,... | collective-permute-start | bytes 491528 | tf_op jit(solution)/shard_map/ppermute | solution.py:296
  111.3 14.0 %collective-permute-start.15 = (f32[640,128]{1,0:T(8,128)S(1)}, f32[640,128]{1,0:T(8,128)S(1)}, u32[]{:S(2)}, u32[]{:S(2)}) collective-permute-start(f32[640,128]{1,0:T(8,128)S(1)} %collective-permute-done.10.refs_1_), channel_id=1, source_target_pairs={{0,32},{32,0},{64,96},{96,64},{128,160},{160,128},{192,224},{224,1... | collective-permute-start | bytes 983048 | tf_op jit(solution)/shard_map/ppermute | solution.py:302
  117.0 8.3 %collective-permute-start.16 = (f32[640,128]{1,0:T(8,128)S(1)}, f32[640,128]{1,0:T(8,128)S(1)}, u32[]{:S(2)}, u32[]{:S(2)}) collective-permute-start(f32[640,128]{1,0:T(8,128)S(1)} %collective-permute-done.11.refs_2_), channel_id=1, source_target_pairs={{0,32},{32,0},{64,96},{96,64},{128,160},{160,128},{192,224},{224,1... | collective-permute-start | bytes 983048 | tf_op jit(solution)/shard_map/ppermute | solution.py:302
  117.2 6.3 %collective-permute-start.13 = (f32[320,128]{1,0:T(8,128)S(1)}, f32[320,128]{1,0:T(8,128)S(1)}, u32[]{:S(2)}, u32[]{:S(2)}) collective-permute-start(f32[320,128]{1,0:T(8,128)S(1)} %slice.47), channel_id=1, source_target_pairs={{0,192},{32,224},{64,0},{96,32},{128,64},{160,96},{192,128},{224,1... | collective-permute-start | bytes 491528 | tf_op jit(solution)/shard_map/ppermute | solution.py:296
  120.1 5.2 %collective-permute-start.17 = (f32[320,128]{1,0:T(8,128)S(1)}, f32[320,128]{1,0:T(8,128)S(1)}, u32[]{:S(2)}, u32[]{:S(2)}) collective-permute-start(f32[320,128]{1,0:T(8,128)S(1)} %collective-permute-done.12.refs_3_), channel_id=1, source_target_pairs={{0,32},{32,0},{64,96},{96,64},{128,160},{160,128},{192,224},{224,1... | collective-permute-start | bytes 491528 | tf_op jit(solution)/shard_map/ppermute | solution.py:302
  123.5 2.1 %collective-permute-start.18 = (f32[320,128]{1,0:T(8,128)S(1)}, f32[320,128]{1,0:T(8,128)S(1)}, u32[]{:S(2)}, u32[]{:S(2)}) collective-permute-start(f32[320,128]{1,0:T(8,128)S(1)} %collective-permute-done.13.refs_4_), channel_id=1, source_target_pairs={{0,32},{32,0},{64,96},{96,64},{128,160},{160,128},{192,224},{224,1... | collective-permute-start | bytes 491528 | tf_op jit(solution)/shard_map/ppermute | solution.py:302
  (5 other events, 4.9 us)

commit v7 on v6

--- a/solution.py
+++ b/solution.py
@@ -253,14 +253,15 @@
     key = expert_ids.reshape(1, rows) * 256 + priority
     outgoing, target = dispatch(tokens, norm_gain.reshape(width // LANES, LANES), key)
 
+    own_rows = to_experts(outgoing.reshape(Y * Z, CAP, width)).reshape(SLOTS, width)
+
+    own_rows, w_in, w_out = lax.optimization_barrier((own_rows, w_in, w_out))
     weights = (
         w_in[0],
         lax.ppermute(w_in[0], *along_core()),
         w_out[0],
         lax.ppermute(w_out[0], *along_core()),
     )
-
-    own_rows = to_experts(outgoing.reshape(Y * Z, CAP, width)).reshape(SLOTS, width)
 
     left_rows = lax.ppermute(own_rows, *along_x(1))
     right_rows = lax.ppermute(own_rows, *along_x(-1))

time: 130 us -> 124 us (0.954)
  local copies, waits for them, and re-layouts: 8.74 us -> 3.65 us
  Pallas kernels: 14.8 us -> 10.4 us
  waiting for transfers between devices: 12.7 us -> 16.1 us
  starting transfers between devices: 37.8 us -> 39.5 us
  blocking collectives: 52.4 us -> 50.8 us
    pallas_call x3, Pallas kernels: 9.29 us -> 4.82 us  [expert_rows(): pl.pallas_call(expert_kernel, out_shape=jax.ShapeDtypeStruct((count, widt...]
    ppermute x1, waiting for transfers between devices: 0.01 us -> 1.79 us  [on_device(): left_rows = lax.ppermute(own_rows, *along_x(1))]
    ppermute x1, waiting for transfers between devices: 5.94 us -> 4.18 us  [on_device(): right_sum = lax.ppermute(narrow(right_sum), *along_x(1))]
    reshape x1, local copies, waits for them, and re-layouts: 1.78 us -> 0.08 us  [on_device(): outgoing.reshape(Y * Z, CAP, width)]
    reshape x1, local copies, waits for them, and re-layouts: 1.77 us -> 0.08 us  [on_device(): to_experts(outgoing.reshape(Y * Z, CAP, width)).reshape(SLOTS, width)]
    unnamed x20 -> x16, local copies, waits for them, and re-layouts: 4.93 us -> 3.24 us
    ppermute x1, waiting for transfers between devices: 0.01 us -> 1.69 us  [on_device(): lax.ppermute(w_in[0], *along_core())]
    ppermute x1, waiting for transfers between devices: 1.46 us -> 3.03 us  [on_device(): lax.ppermute(left_rows[:half], *along_x(1))]
  transfers between devices with their start and end apart: 19 -> 19, of which waited for: 5 -> 8; matrix products, arithmetic and copies ran while one was open for 4% -> 0% of each run, Pallas kernels for 6% -> 3%
where the time goes in v7:
time: 124 us; the launch traced here: 123 us
  blocking collectives  50.8 us (41%)
  starting transfers between devices  39.5 us (32%)
  waiting for transfers between devices  16.1 us (13%)
  Pallas kernels  10.4 us (8%)
  local copies, waits for them, and re-layouts  3.65 us (3%)
  between operations  1.55 us (1%)
    all_to_all x3, blocking collectives, to_experts(): lax.all_to_all(blocks, 'expert', split_axis=0, concat_axis=0, tiled=True)  50.8 us
    ppermute x5, starting transfers between devices, on_device(): lax.ppermute(block, *along_core())  19.2 us
    pallas_call x3, Pallas kernels, expert_rows(): pl.pallas_call(expert_kernel, out_shape=jax.ShapeDtypeStruct((count, widt...  4.82 us
    ppermute x1, starting transfers between devices, on_device(): lax.ppermute(w_in[0], *along_core())  4.43 us
    ppermute x1, waiting for transfers between devices, on_device(): right_sum = lax.ppermute(narrow(right_sum), *along_x(1))  4.18 us
    pallas_call x1, Pallas kernels, contrast(): pl.pallas_call(contrast_kernel, out_shape=(jax.ShapeDtypeStruct((1, 1), j...  3.59 us
    unnamed x16, local copies, waits for them, and re-layouts  3.24 us
    ppermute x1, waiting for transfers between devices, on_device(): lax.ppermute(left_rows[:half], *along_x(1))  3.03 us
  transfers between devices with their start and end apart: 19, of which 8 were waited for; matrix products, arithmetic and copies ran while one was open for 0% of the time, Pallas kernels for 3%

profile of v7, /device:TPU:1, one launch (start us, length us, event | category | flops | bytes accessed | tf_op | source)
XLA Modules:
  0.0 123.2 jit_solution(15934378407645733235)
XLA Ops:
  3.9 22.0 %all_to_all.15 = bf16[32,4,1280]{2,1,0:T(4,128)(2,1)S(1)} all-to-all(bf16[32,4,1280]{2,1,0:T(4,128)(2,1)S(1)} %reshape.51), channel_id=1, replica_groups=mesh['dp'=8,'expert'=32] {'expert'}, dimensions={0} | all-to-all | bytes 655360 | tf_op jit(solution)/shard_map/all_to_all | solution.py:242
  26.0 4.4 %collective-permute-start.2 = (bf16[1280,640]{1,0:T(8,128)(2,1)S(1)}, bf16[1280,640]{1,0:T(8,128)(2,1)S(1)}, u32[]{:S(2)}, u32[]{:S(2)}) collective-permute-start(bf16[1280,640]{1,0:T(8,128)(2,1)S(1)} %bitcast.12), channel_id=1, source_target_pairs={{0,32},{32,0},{64,96},{96,64},{128,160},{160,128},{192,224},{224,1... | collective-permute-start | bytes 4915208 | tf_op jit(solution)/shard_map/ppermute | solution.py:261
  31.7 1.5 %collective-permute-start.1 = (bf16[128,1280]{1,0:T(8,128)(2,1)S(1)}, bf16[128,1280]{1,0:T(8,128)(2,1)S(1)}, u32[]{:S(2)}, u32[]{:S(2)}) collective-permute-start(bf16[128,1280]{1,0:T(8,128)(2,1)S(1)} %reshape.52.rows_ref), channel_id=1, source_target_pairs={{0,192},{32,224},{64,0},{96,32},{128,64},{160,96},{192,128},{224,1... | collective-permute-start | bytes 983048 | tf_op jit(solution)/shard_map/ppermute | solution.py:267
  33.2 1.7 %collective-permute-done.2.in_other = bf16[1280,640]{1,0:T(8,128)(2,1)S(1)} collective-permute-done((bf16[1280,640]{1,0:T(8,128)(2,1)S(1)}, bf16[1280,640]{1,0:T(8,128)(2,1)S(1)}, u32[]{:S(2)}, u32[]{:S(2)}) %collective-permute-start.2) | collective-permute-done | bytes 1638432 | tf_op jit(solution)/shard_map/ppermute | solution.py:261
  36.1 1.4 %copy-done.1 = bf16[1,640,1280]{2,1,0:T(8,128)(2,1)S(1)} copy-done((bf16[1,640,1280]{2,1,0:T(8,128)(2,1)S(1)}, bf16[1,640,1280]{2,1,0:T(8,128)(2,1)}, u32[]{:S(2)}) %copy-start.1) | copy-done | bytes 1638424
  38.8 1.8 %collective-permute-done = bf16[128,1280]{1,0:T(8,128)(2,1)S(1)} collective-permute-done((bf16[128,1280]{1,0:T(8,128)(2,1)S(1)}, bf16[128,1280]{1,0:T(8,128)(2,1)S(1)}, u32[]{:S(2)}, u32[]{:S(2)}) %collective-permute-start) | collective-permute-done | bytes 327712 | tf_op jit(solution)/shard_map/ppermute | solution.py:266
  40.6 2.4 %collective-permute-start.5 = (bf16[64,1280]{1,0:T(8,128)(2,1)S(1)}, bf16[64,1280]{1,0:T(8,128)(2,1)S(1)}, u32[]{:S(2)}, u32[]{:S(2)}) collective-permute-start(bf16[64,1280]{1,0:T(8,128)(2,1)S(1)} %slice.33), channel_id=1, source_target_pairs={{0,192},{32,224},{64,0},{96,32},{128,64},{160,96},{192,128},{224,1... | collective-permute-start | bytes 491528 | tf_op jit(solution)/shard_map/ppermute | solution.py:273
  43.2 2.3 %expert.4 = f32[256,1280]{1,0:T(8,128)S(1)} custom-call(bf16[256,1280]{1,0:T(8,128)(2,1)S(1)} %pad_maximum_fusion.rows_ref, bf16[1280,640]{1,0:T(8,128)(2,1)S(1)} %bitcast.14, bf16[1280,640]{1,0:T(8,128)(2,1)S(1)} %collective-permute-done.2.in_other, bf16[640,1280]{1,0:T(8,128)(2,1)S(1)} %bitcast.18, bf16[640,1280]{1,0:T(8,128)(2,1)S(1)} %collective-permute-done.3.out_other), custom_call_target="tpu_custom_call" | custom-call | flops 1677721600 | bytes 8519680 | tf_op jit(solution)/shard_map/expert/pallas_call | solution.py:217
  45.5 3.0 %collective-permute-done.4 = bf16[64,1280]{1,0:T(8,128)(2,1)S(1)} collective-permute-done((bf16[64,1280]{1,0:T(8,128)(2,1)S(1)}, bf16[64,1280]{1,0:T(8,128)(2,1)S(1)}, u32[]{:S(2)}, u32[]{:S(2)}) %collective-permute-start.4) | collective-permute-done | bytes 163872 | tf_op jit(solution)/shard_map/ppermute | solution.py:272
  48.6 1.3 %expert.5 = f32[128,1280]{1,0:T(8,128)S(1)} custom-call(bf16[128,1280]{1,0:T(8,128)(2,1)S(1)} %pad_maximum_fusion.1.rows_ref, bf16[1280,640]{1,0:T(8,128)(2,1)S(1)} %bitcast.15, bf16[1280,640]{1,0:T(8,128)(2,1)S(1)} %collective-permute-done.2.in_other, bf16[640,1280]{1,0:T(8,128)(2,1)S(1)} %bitcast.19, bf16[640,1280]{1,0:T(8,128)(2,1)S(1)} %collective-permute-done.3.out_other), custom_call_target="tpu_custom_call" | custom-call | flops 838860800 | bytes 7536640 | tf_op jit(solution)/shard_map/expert/pallas_call | solution.py:217
  50.0 1.5 %collective-permute-start.8 = (bf16[64,1280]{1,0:T(8,128)(2,1)S(1)}, bf16[64,1280]{1,0:T(8,128)(2,1)S(1)}, u32[]{:S(2)}, u32[]{:S(2)}) collective-permute-start(bf16[64,1280]{1,0:T(8,128)(2,1)S(1)} %get-tuple-element.39), channel_id=1, source_target_pairs={{0,64},{32,96},{64,128},{96,160},{128,192},{160,224},{192,0},{224,... | collective-permute-start | bytes 491528 | tf_op jit(solution)/shard_map/ppermute | solution.py:281
  51.6 2.6 %collective-permute-done.6 = bf16[64,1280]{1,0:T(8,128)(2,1)S(1)} collective-permute-done((bf16[64,1280]{1,0:T(8,128)(2,1)S(1)}, bf16[64,1280]{1,0:T(8,128)(2,1)S(1)}, u32[]{:S(2)}, u32[]{:S(2)}) %collective-permute-start.6) | collective-permute-done | bytes 163872 | tf_op jit(solution)/shard_map/ppermute | solution.py:280
  54.2 1.3 %collective-permute-done.8 = bf16[64,1280]{1,0:T(8,128)(2,1)S(1)} collective-permute-done((bf16[64,1280]{1,0:T(8,128)(2,1)S(1)}, bf16[64,1280]{1,0:T(8,128)(2,1)S(1)}, u32[]{:S(2)}, u32[]{:S(2)}) %collective-permute-start.8) | collective-permute-done | bytes 163872 | tf_op jit(solution)/shard_map/ppermute | solution.py:281
  56.1 2.5 %collective-permute-start.7 = (bf16[128,1280]{1,0:T(8,128)(2,1)S(1)}, bf16[128,1280]{1,0:T(8,128)(2,1)S(1)}, u32[]{:S(2)}, u32[]{:S(2)}) collective-permute-start(bf16[128,1280]{1,0:T(8,128)(2,1)S(1)} %pad_maximum_fusion.2), channel_id=1, source_target_pairs={{0,192},{32,224},{64,0},{96,32},{128,64},{160,96},{192,128},{224,1... | collective-permute-start | bytes 983048 | tf_op jit(solution)/shard_map/ppermute | solution.py:286
  58.6 4.2 %collective-permute-done.9 = bf16[128,1280]{1,0:T(8,128)(2,1)S(1)} collective-permute-done((bf16[128,1280]{1,0:T(8,128)(2,1)S(1)}, bf16[128,1280]{1,0:T(8,128)(2,1)S(1)}, u32[]{:S(2)}, u32[]{:S(2)}) %collective-permute-start.9) | collective-permute-done | bytes 327712 | tf_op jit(solution)/shard_map/ppermute | solution.py:287
  63.0 14.3 %all_to_all.16 = bf16[32,4,1280]{2,1,0:T(4,128)(2,1)S(1)} all-to-all(bf16[32,4,1280]{2,1,0:T(4,128)(2,1)S(1)} %reshape.53), channel_id=1, replica_groups=mesh['dp'=8,'expert'=32] {'expert'}, dimensions={0} | all-to-all | bytes 655360 | tf_op jit(solution)/shard_map/all_to_all | solution.py:242
  77.4 1.3 %combine.1 = (bf16[256,1280]{1,0:T(8,128)(2,1)}, f32[640,128]{1,0:T(8,128)S(1)}) custom-call(bf16[128,1280]{1,0:T(8,128)(2,1)S(1)} %reshape.54.returned_ref, s32[1,256]{1,0:T(1,128)S(1)} %get-tuple-element.28.target_ref, f32[1,256]{1,0:T(1,128)S(1)} %bitcast.26, bf16[256,1280]{1,0:T(8,128)(2,1)S(1)} %copy-done.4, f32[1,1280]{1,0:T(1,128)S(1)} %copy-done.6), custom_call_target="tpu_custom_call" | custom-call | tf_op jit(solution)/shard_map/combine/pallas_call | solution.py:94
  78.7 14.6 %all_to_all.17 = f32[32,1,2560]{2,1,0:T(1,128)S(1)} all-to-all(f32[32,1,2560]{2,1,0:T(1,128)S(1)} %bitcast.24), channel_id=1, replica_groups=mesh['dp'=8,'expert'=32] {'expert'}, dimensions={0} | all-to-all | bytes 655360 | tf_op jit(solution)/shard_map/all_to_all | solution.py:242
  93.4 2.9 %collective-permute-start.11 = (f32[640,128]{1,0:T(8,128)S(1)}, f32[640,128]{1,0:T(8,128)S(1)}, u32[]{:S(2)}, u32[]{:S(2)}) collective-permute-start(f32[640,128]{1,0:T(8,128)S(1)} %bitcast.21), channel_id=1, source_target_pairs={{0,192},{32,224},{64,0},{96,32},{128,64},{160,96},{192,128},{224,1... | collective-permute-start | bytes 983048 | tf_op jit(solution)/shard_map/ppermute | solution.py:296
  96.3 9.0 %collective-permute-start.14 = (f32[640,128]{1,0:T(8,128)S(1)}, f32[640,128]{1,0:T(8,128)S(1)}, u32[]{:S(2)}, u32[]{:S(2)}) collective-permute-start(f32[640,128]{1,0:T(8,128)S(1)} %bitcast.22), channel_id=1, source_target_pairs={{0,32},{32,0},{64,96},{96,64},{128,160},{160,128},{192,224},{224,1... | collective-permute-start | bytes 983048 | tf_op jit(solution)/shard_map/ppermute | solution.py:303
  105.4 5.7 %collective-permute-start.15 = (f32[640,128]{1,0:T(8,128)S(1)}, f32[640,128]{1,0:T(8,128)S(1)}, u32[]{:S(2)}, u32[]{:S(2)}) collective-permute-start(f32[640,128]{1,0:T(8,128)S(1)} %collective-permute-done.10.refs_1_), channel_id=1, source_target_pairs={{0,32},{32,0},{64,96},{96,64},{128,160},{160,128},{192,224},{224,1... | collective-permute-start | bytes 983048 | tf_op jit(solution)/shard_map/ppermute | solution.py:303
  111.2 2.9 %collective-permute-start.13 = (f32[320,128]{1,0:T(8,128)S(1)}, f32[320,128]{1,0:T(8,128)S(1)}, u32[]{:S(2)}, u32[]{:S(2)}) collective-permute-start(f32[320,128]{1,0:T(8,128)S(1)} %slice.47), channel_id=1, source_target_pairs={{0,192},{32,224},{64,0},{96,32},{128,64},{160,96},{192,128},{224,1... | collective-permute-start | bytes 491528 | tf_op jit(solution)/shard_map/ppermute | solution.py:297
  114.1 3.4 %collective-permute-start.17 = (f32[320,128]{1,0:T(8,128)S(1)}, f32[320,128]{1,0:T(8,128)S(1)}, u32[]{:S(2)}, u32[]{:S(2)}) collective-permute-start(f32[320,128]{1,0:T(8,128)S(1)} %collective-permute-done.12.refs_3_), channel_id=1, source_target_pairs={{0,32},{32,0},{64,96},{96,64},{128,160},{160,128},{192,224},{224,1... | collective-permute-start | bytes 491528 | tf_op jit(solution)/shard_map/ppermute | solution.py:303
  119.6 3.6 %contrast.1 = (f32[1,1]{1,0:T(1,128)}, f32[1,1280]{1,0:T(1,128)}, f32[1,1280]{1,0:T(1,128)}) custom-call(s32[3]{0:T(128)S(1)} %pad_add_fusion.place_ref, f32[1]{0:T(128)S(6)} %copy.14.scale_ref, f32[640,128]{1,0:T(8,128)S(1)} %bitcast.23, f32[640,128]{1,0:T(8,128)S(1)} %collective-permute-done.10.refs_1_, f32[640,128]{1,0:T(8,128)S(1)} %collective-permute-done.11.refs_2_, ...), custom_call_target="tpu_custom_call" | custom-call | tf_op jit(solution)/shard_map/contrast/pallas_call | solution.py:179
  (59 shorter events, 10.2 us)
Async XLA Ops:
  3.1 22.9 %copy-start = (bf16[1,1280,640]{2,1,0:T(8,128)(2,1)S(1)}, bf16[1,1280,640]{2,1,0:T(8,128)(2,1)}, u32[]{:S(2)}) copy-start(bf16[1,1280,640]{2,1,0:T(8,128)(2,1)} %param.14) | copy-start | bytes 4915204
  26.0 8.9 %collective-permute-start.2 = (bf16[1280,640]{1,0:T(8,128)(2,1)S(1)}, bf16[1280,640]{1,0:T(8,128)(2,1)S(1)}, u32[]{:S(2)}, u32[]{:S(2)}) collective-permute-start(bf16[1280,640]{1,0:T(8,128)(2,1)S(1)} %bitcast.12), channel_id=1, source_target_pairs={{0,32},{32,0},{64,96},{96,64},{128,160},{160,128},{192,224},{224,1... | collective-permute-start | bytes 4915208 | tf_op jit(solution)/shard_map/ppermute | solution.py:261
  30.4 5.7 %collective-permute-start.3 = (bf16[640,1280]{1,0:T(8,128)(2,1)}, bf16[640,1280]{1,0:T(8,128)(2,1)S(1)}, u32[]{:S(2)}, u32[]{:S(2)}) collective-permute-start(bf16[640,1280]{1,0:T(8,128)(2,1)} %bitcast.16), channel_id=1, source_target_pairs={{0,32},{32,0},{64,96},{96,64},{128,160},{160,128},{192,224},{224,1... | collective-permute-start | bytes 4915208 | tf_op jit(solution)/shard_map/ppermute | solution.py:263
  30.5 10.1 %collective-permute-start = (bf16[128,1280]{1,0:T(8,128)(2,1)S(1)}, bf16[128,1280]{1,0:T(8,128)(2,1)S(1)}, u32[]{:S(2)}, u32[]{:S(2)}) collective-permute-start(bf16[128,1280]{1,0:T(8,128)(2,1)S(1)} %reshape.52.rows_ref), channel_id=1, source_target_pairs={{0,64},{32,96},{64,128},{96,160},{128,192},{160,224},{192,0},{224,... | collective-permute-start | bytes 983048 | tf_op jit(solution)/shard_map/ppermute | solution.py:266
  31.7 8.9 %collective-permute-start.1 = (bf16[128,1280]{1,0:T(8,128)(2,1)S(1)}, bf16[128,1280]{1,0:T(8,128)(2,1)S(1)}, u32[]{:S(2)}, u32[]{:S(2)}) collective-permute-start(bf16[128,1280]{1,0:T(8,128)(2,1)S(1)} %reshape.52.rows_ref), channel_id=1, source_target_pairs={{0,192},{32,224},{64,0},{96,32},{128,64},{160,96},{192,128},{224,1... | collective-permute-start | bytes 983048 | tf_op jit(solution)/shard_map/ppermute | solution.py:267
  40.6 4.9 %collective-permute-start.5 = (bf16[64,1280]{1,0:T(8,128)(2,1)S(1)}, bf16[64,1280]{1,0:T(8,128)(2,1)S(1)}, u32[]{:S(2)}, u32[]{:S(2)}) collective-permute-start(bf16[64,1280]{1,0:T(8,128)(2,1)S(1)} %slice.33), channel_id=1, source_target_pairs={{0,192},{32,224},{64,0},{96,32},{128,64},{160,96},{192,128},{224,1... | collective-permute-start | bytes 491528 | tf_op jit(solution)/shard_map/ppermute | solution.py:273
  43.1 5.5 %collective-permute-start.4 = (bf16[64,1280]{1,0:T(8,128)(2,1)S(1)}, bf16[64,1280]{1,0:T(8,128)(2,1)S(1)}, u32[]{:S(2)}, u32[]{:S(2)}) collective-permute-start(bf16[64,1280]{1,0:T(8,128)(2,1)S(1)} %slice.32), channel_id=1, source_target_pairs={{0,64},{32,96},{64,128},{96,160},{128,192},{160,224},{192,0},{224,... | collective-permute-start | bytes 491528 | tf_op jit(solution)/shard_map/ppermute | solution.py:272
  43.2 5.3 %copy-start.2 = (bf16[1,640,1280]{2,1,0:T(8,128)(2,1)S(1)}, bf16[1,640,1280]{2,1,0:T(8,128)(2,1)}, u32[]{:S(2)}) copy-start(bf16[1,640,1280]{2,1,0:T(8,128)(2,1)} %param.15) | copy-start | bytes 4915204
  49.9 4.2 %collective-permute-start.6 = (bf16[64,1280]{1,0:T(8,128)(2,1)S(1)}, bf16[64,1280]{1,0:T(8,128)(2,1)S(1)}, u32[]{:S(2)}, u32[]{:S(2)}) collective-permute-start(bf16[64,1280]{1,0:T(8,128)(2,1)S(1)} %get-tuple-element.38), channel_id=1, source_target_pairs={{0,192},{32,224},{64,0},{96,32},{128,64},{160,96},{192,128},{224,1... | collective-permute-start | bytes 491528 | tf_op jit(solution)/shard_map/ppermute | solution.py:280
  50.0 5.5 %collective-permute-start.8 = (bf16[64,1280]{1,0:T(8,128)(2,1)S(1)}, bf16[64,1280]{1,0:T(8,128)(2,1)S(1)}, u32[]{:S(2)}, u32[]{:S(2)}) collective-permute-start(bf16[64,1280]{1,0:T(8,128)(2,1)S(1)} %get-tuple-element.39), channel_id=1, source_target_pairs={{0,64},{32,96},{64,128},{96,160},{128,192},{160,224},{192,0},{224,... | collective-permute-start | bytes 491528 | tf_op jit(solution)/shard_map/ppermute | solution.py:281
  55.6 7.2 %collective-permute-start.9 = (bf16[128,1280]{1,0:T(8,128)(2,1)S(1)}, bf16[128,1280]{1,0:T(8,128)(2,1)S(1)}, u32[]{:S(2)}, u32[]{:S(2)}) collective-permute-start(bf16[128,1280]{1,0:T(8,128)(2,1)S(1)} %pad_maximum_fusion.3), channel_id=1, source_target_pairs={{0,64},{32,96},{64,128},{96,160},{128,192},{160,224},{192,0},{224,... | collective-permute-start | bytes 983048 | tf_op jit(solution)/shard_map/ppermute | solution.py:287
  56.1 6.7 %collective-permute-start.7 = (bf16[128,1280]{1,0:T(8,128)(2,1)S(1)}, bf16[128,1280]{1,0:T(8,128)(2,1)S(1)}, u32[]{:S(2)}, u32[]{:S(2)}) collective-permute-start(bf16[128,1280]{1,0:T(8,128)(2,1)S(1)} %pad_maximum_fusion.2), channel_id=1, source_target_pairs={{0,192},{32,224},{64,0},{96,32},{128,64},{160,96},{192,128},{224,1... | collective-permute-start | bytes 983048 | tf_op jit(solution)/shard_map/ppermute | solution.py:286
  62.9 14.5 %copy-start.4 = (bf16[256,1280]{1,0:T(8,128)(2,1)S(1)}, bf16[256,1280]{1,0:T(8,128)(2,1)}, u32[]{:S(2)}) copy-start(bf16[256,1280]{1,0:T(8,128)(2,1)} %tokens_ref.3) | copy-start | bytes 1966084
  62.9 14.5 %copy-start.6 = (f32[1,1280]{1,0:T(1,128)S(1)}, f32[1,1280]{1,0:T(1,128)}, u32[]{:S(2)}) copy-start(f32[1,1280]{1,0:T(1,128)} %text_ref.1) | copy-start | bytes 15364
  62.9 14.5 %copy-start.7 = (f32[256]{0:T(256)S(1)}, f32[256]{0:T(256)}, u32[]{:S(2)}) copy-start(f32[256]{0:T(256)} %param.13) | copy-start | bytes 3076
  93.3 12.0 %collective-permute-start.10 = (f32[640,128]{1,0:T(8,128)S(1)}, f32[640,128]{1,0:T(8,128)S(1)}, u32[]{:S(2)}, u32[]{:S(2)}) collective-permute-start(f32[640,128]{1,0:T(8,128)S(1)} %bitcast.20), channel_id=1, source_target_pairs={{0,64},{32,96},{64,128},{96,160},{128,192},{160,224},{192,0},{224,... | collective-permute-start | bytes 983048 | tf_op jit(solution)/shard_map/ppermute | solution.py:295
  93.4 17.7 %collective-permute-start.11 = (f32[640,128]{1,0:T(8,128)S(1)}, f32[640,128]{1,0:T(8,128)S(1)}, u32[]{:S(2)}, u32[]{:S(2)}) collective-permute-start(f32[640,128]{1,0:T(8,128)S(1)} %bitcast.21), channel_id=1, source_target_pairs={{0,192},{32,224},{64,0},{96,32},{128,64},{160,96},{192,128},{224,1... | collective-permute-start | bytes 983048 | tf_op jit(solution)/shard_map/ppermute | solution.py:296
  96.3 23.0 %collective-permute-start.14 = (f32[640,128]{1,0:T(8,128)S(1)}, f32[640,128]{1,0:T(8,128)S(1)}, u32[]{:S(2)}, u32[]{:S(2)}) collective-permute-start(f32[640,128]{1,0:T(8,128)S(1)} %bitcast.22), channel_id=1, source_target_pairs={{0,32},{32,0},{64,96},{96,64},{128,160},{160,128},{192,224},{224,1... | collective-permute-start | bytes 983048 | tf_op jit(solution)/shard_map/ppermute | solution.py:303
  105.3 8.8 %collective-permute-start.12 = (f32[320,128]{1,0:T(8,128)S(1)}, f32[320,128]{1,0:T(8,128)S(1)}, u32[]{:S(2)}, u32[]{:S(2)}) collective-permute-start(f32[320,128]{1,0:T(8,128)S(1)} %slice.46), channel_id=1, source_target_pairs={{0,64},{32,96},{64,128},{96,160},{128,192},{160,224},{192,0},{224,... | collective-permute-start | bytes 491528 | tf_op jit(solution)/shard_map/ppermute | solution.py:297
  105.4 13.9 %collective-permute-start.15 = (f32[640,128]{1,0:T(8,128)S(1)}, f32[640,128]{1,0:T(8,128)S(1)}, u32[]{:S(2)}, u32[]{:S(2)}) collective-permute-start(f32[640,128]{1,0:T(8,128)S(1)} %collective-permute-done.10.refs_1_), channel_id=1, source_target_pairs={{0,32},{32,0},{64,96},{96,64},{128,160},{160,128},{192,224},{224,1... | collective-permute-start | bytes 983048 | tf_op jit(solution)/shard_map/ppermute | solution.py:303
  111.1 8.2 %collective-permute-start.16 = (f32[640,128]{1,0:T(8,128)S(1)}, f32[640,128]{1,0:T(8,128)S(1)}, u32[]{:S(2)}, u32[]{:S(2)}) collective-permute-start(f32[640,128]{1,0:T(8,128)S(1)} %collective-permute-done.11.refs_2_), channel_id=1, source_target_pairs={{0,32},{32,0},{64,96},{96,64},{128,160},{160,128},{192,224},{224,1... | collective-permute-start | bytes 983048 | tf_op jit(solution)/shard_map/ppermute | solution.py:303
  111.2 6.3 %collective-permute-start.13 = (f32[320,128]{1,0:T(8,128)S(1)}, f32[320,128]{1,0:T(8,128)S(1)}, u32[]{:S(2)}, u32[]{:S(2)}) collective-permute-start(f32[320,128]{1,0:T(8,128)S(1)} %slice.47), channel_id=1, source_target_pairs={{0,192},{32,224},{64,0},{96,32},{128,64},{160,96},{192,128},{224,1... | collective-permute-start | bytes 491528 | tf_op jit(solution)/shard_map/ppermute | solution.py:297
  114.1 5.2 %collective-permute-start.17 = (f32[320,128]{1,0:T(8,128)S(1)}, f32[320,128]{1,0:T(8,128)S(1)}, u32[]{:S(2)}, u32[]{:S(2)}) collective-permute-start(f32[320,128]{1,0:T(8,128)S(1)} %collective-permute-done.12.refs_3_), channel_id=1, source_target_pairs={{0,32},{32,0},{64,96},{96,64},{128,160},{160,128},{192,224},{224,1... | collective-permute-start | bytes 491528 | tf_op jit(solution)/shard_map/ppermute | solution.py:303
  117.5 2.1 %collective-permute-start.18 = (f32[320,128]{1,0:T(8,128)S(1)}, f32[320,128]{1,0:T(8,128)S(1)}, u32[]{:S(2)}, u32[]{:S(2)}) collective-permute-start(f32[320,128]{1,0:T(8,128)S(1)} %collective-permute-done.13.refs_4_), channel_id=1, source_target_pairs={{0,32},{32,0},{64,96},{96,64},{128,160},{160,128},{192,224},{224,1... | collective-permute-start | bytes 491528 | tf_op jit(solution)/shard_map/ppermute | solution.py:303
  (3 other events, 3.2 us)
